TPU v7x, 32 devices: a whole 2x2x4 slice. The times are simulated.
32 devices in a mesh: cuts: 2 (over x), wide: 8 (over z, y), narrow: 2 (over core).
Axes of the slice: x: 2, y: 2, z: 4, core: 2. Of those that a mesh axis runs over, the one named last changes fastest.
Arguments:
- stem_tensor: float32 [2, 16384, 512], P(None, ('cuts', 'wide', 'narrow')), parts along dimension 1, may hold values from -6 to 6
- leaves: bfloat16 [16, 4, 2, 512, 512], P(('cuts', 'wide')), parts along dimension 0, may hold values from -1 to 1
- root_devices: int32 [4], replicated, may hold values from 0 to 7, as said below
- mode_orders: int32 [4, 9], replicated, may hold values from 0 to 8, each once within a row
Outputs:
- contracted: float32 [2, 16384, 512], P(None, ('cuts', 'wide', 'narrow')), parts along dimension 1
There are 2 independent parts, one for each index of `cuts`. A program takes and returns all parts, laid end to end along the dimension named above; an argument that names none is the same for every part. Nothing has to cross between parts.
Inputs may be any that keep to these rules, and one draw needn't show every extreme that they name: `root_devices`: the roots include 0, 4 and 7. `mode_orders`: each row holds every number of 0 to 8 once.
All inputs are finite; a program needn't handle non-finite values.
Results may differ from a plain program's by a relative error of at most 0.0081.
Values may be sent and summed in bfloat16 or wider, within the bound.
No kernel may reach another device: no remote copies, remote signals or barrier semaphores. Data moves between devices by JAX's collectives and lax.ppermute only.
A program may use at most 64 MiB of HBM per device.

v0:
```python
import jax
import jax.numpy as jnp
from jax import lax
from jax.sharding import PartitionSpec as P

STEPS = 4


def from_partner(value, axis, apart):
    return lax.ppermute(value, axis, [(i, i ^ 1 << apart) for i in range(lax.axis_size(axis))])


def broadcast(block, axis, holder):
    block = jnp.where(lax.axis_index(axis) == holder, block, jnp.zeros_like(block))
    return lax.psum(block, axis)


def complex_product(left_matrix, right_matrix, precision=None):
    real_part = jnp.dot(
        left_matrix[0], right_matrix[0], preferred_element_type=jnp.float32, precision=precision
    ) - jnp.dot(
        left_matrix[1], right_matrix[1], preferred_element_type=jnp.float32, precision=precision
    )
    imag_part = jnp.dot(
        left_matrix[0], right_matrix[1], preferred_element_type=jnp.float32, precision=precision
    ) + jnp.dot(
        left_matrix[1], right_matrix[0], preferred_element_type=jnp.float32, precision=precision
    )
    return jnp.stack([real_part, imag_part])


def column_source(order_row, branch_width):
    column = jnp.arange(branch_width, dtype=jnp.int32)
    mode_count = order_row.shape[0]
    powers = jnp.left_shift(jnp.int32(1), jnp.arange(mode_count, dtype=jnp.int32))
    bit_table = column[:, None] // powers[None, :] % 2
    weights = jnp.left_shift(jnp.int32(1), order_row)
    return jnp.sum(bit_table * weights[None, :], axis=1)


def stem_product(network, ordered):
    highest = lax.Precision.HIGHEST
    return complex_product(network, ordered, highest)


def local(stem_tensor, leaves, root_devices, mode_orders):
    network = stem_tensor
    branch_width = stem_tensor.shape[2]
    rows_local = stem_tensor.shape[1]
    core_count = lax.axis_size("narrow")
    row_share = branch_width // core_count
    core_index = lax.axis_index("narrow")
    wide_index = lax.axis_index("wide")
    lower_leaf = wide_index % 2 == 0
    lower_pair = wide_index // 2 % 2 == 0
    for step_index in range(STEPS):
        own_leaf = leaves[0, step_index]
        partner = from_partner(own_leaf, "wide", 0)
        left_leaf = jnp.where(lower_leaf, own_leaf, partner)
        right_leaf = jnp.where(lower_leaf, partner, own_leaf)
        source = column_source(mode_orders[step_index], branch_width)
        row_block = lax.dynamic_slice_in_dim(left_leaf, core_index * row_share, row_share, 1)
        pair_part = complex_product(row_block, right_leaf).astype(jnp.bfloat16)
        pair_other = from_partner(pair_part, "wide", 1)
        pair_lower = jnp.where(lower_pair, pair_part, pair_other)
        pair_upper = jnp.where(lower_pair, pair_other, pair_part)
        branch_part = complex_product(
            pair_lower, lax.all_gather(pair_upper, "narrow", axis=1, tiled=True)
        )
        ordered_part = jnp.take(branch_part, source, axis=2)
        ordered_part = broadcast(ordered_part, "wide", root_devices[step_index])
        current = network
        network = stem_product(current, lax.all_gather(ordered_part, "narrow", axis=1, tiled=True))
        if step_index % 2 == 0:
            stem_view = network.reshape(2, rows_local, core_count, row_share)
            network = lax.all_to_all(
                stem_view, "narrow", split_axis=2, concat_axis=2, tiled=True
            ).reshape(2, rows_local, branch_width)
    return network


def solution(mesh):
    placed = (
        P(None, ("cuts", "wide", "narrow"), None),
        P(("cuts", "wide"), None, None, None, None),
        P(),
        P(),
    )
    return jax.shard_map(
        local,
        mesh=mesh,
        in_specs=placed,
        out_specs=P(None, ("cuts", "wide", "narrow"), None),
        check_vma=False,
    )
```

profile of v0, /device:TPU:0, one launch (start us, length us, event | category | flops | bytes accessed | tf_op | source)
XLA Modules:
  0.0 471.4 jit_solution(2376073138795786767)
XLA Ops:
  6.5 4.3 slice_bitcast_fusion
  19.7 85.0 %collective-permute-done.4 = bf16[2,512,512]{2,1,0:T(8,128)(2,1)S(1)} collective-permute-done((bf16[2,512,512]{2,1,0:T(8,128)(2,1)}, bf16[2,512,512]{2,1,0:T(8,128)(2,1)S(1)}, u32[]{:S(2)}, u32[]{:S(2)}) %collective-permute-start.4) | collective-permute-done | bytes 1048608 | tf_op jit(solution)/shard_map/ppermute | solution.py:10
  108.2 3.8 broadcast_select_fusion.3
  120.7 10.0 %collective-permute-done.3 = bf16[2,256,512]{2,1,0:T(8,128)(2,1)S(1)} collective-permute-done((bf16[2,256,512]{2,1,0:T(8,128)(2,1)S(1)}, bf16[2,256,512]{2,1,0:T(8,128)(2,1)S(1)}, u32[]{:S(2)}, u32[]{:S(2)}) %collective-permute-start.3) | collective-permute-done | bytes 524320 | tf_op jit(solution)/shard_map/ppermute | solution.py:10
  135.6 6.4 %collective-permute-done.5 = bf16[2,256,512]{2,1,0:T(8,128)(2,1)} collective-permute-done((bf16[2,256,512]{2,1,0:T(8,128)(2,1)}, bf16[2,256,512]{2,1,0:T(8,128)(2,1)}, u32[]{:S(2)}, u32[]{:S(2)}) %collective-permute-start.5) | collective-permute-done | bytes 524320 | tf_op jit(solution)/shard_map/ppermute | solution.py:10
  147.0 4.4 collective-permute-done.1
  156.5 10.7 %collective-permute-done.7 = bf16[2,256,512]{2,1,0:T(8,128)(2,1)S(1)} collective-permute-done((bf16[2,256,512]{2,1,0:T(8,128)(2,1)S(1)}, bf16[2,256,512]{2,1,0:T(8,128)(2,1)S(1)}, u32[]{:S(2)}, u32[]{:S(2)}) %collective-permute-start.7) | collective-permute-done | bytes 524320 | tf_op jit(solution)/shard_map/ppermute | solution.py:10
  204.6 3.6 bitcast_select_fusion.2
  216.2 157.3 %all-reduce.3.cloned.1.call-done = (f32[2,256,512]{1,0,2:T(2,128)}, f32[2,256,512]{1,0,2:T(2,128)}, f32[2,256,512]{1,0,2:T(2,128)}, f32[2,256,512]{1,0,2:T(2,128)}) async-done(((f32[2,256,512]{1,0,2:T(2,128)}, f32[2,256,512]{1,0,2:T(2,128)}, f32[2,256,512]{1,0,2:T(2,128)}, f32[2,256,512]{1,0,2:T(2,128)}), (f32[2,256,512]{1,0,2:T(2,128)}, f32[2,256,512]{1,0,2:T(2,128)}, f32[2,256,512]{1,0,2:T(2,128)}, ...) | async-done | bytes 4194320 | tf_op jit(solution)/shard_map/psum | solution.py:15
  375.8 8.3 %all-gather.11.cloned.1.call-done = f32[2,512,512]{1,0,2:T(2,128)} async-done(((f32[2,256,512]{1,0,2:T(2,128)}), f32[2,512,512]{1,0,2:T(2,128)}) %all-gather.11.cloned.1.call-update) | async-done | bytes 2097168 | tf_op jit(solution)/shard_map/all_gather | solution.py:73
  384.1 4.0 fusion.99
  397.3 5.0 %all-to-all-start = ((f32[2,512,2,256]{1,3,0,2:T(8,128)}), f32[2,512,2,256]{1,3,0,2:T(8,128)}, u32[]{:S(2)}, u32[]{:S(2)}) async-start(f32[2,512,2,256]{1,3,0,2:T(8,128)} %pad_maximum_fusion), calls=%async_computation | async-start | bytes 4194304 | tf_op jit(solution)/shard_map/all_to_all | solution.py:76
  402.3 4.0 fusion.97
  409.4 4.5 fusion.38
  413.9 4.0 fusion.96
  417.9 3.5 fusion.42
  421.4 3.9 convolution_subtract_fusion.2
  429.1 3.5 convolution_add_fusion.2
  438.1 4.8 %all-to-all-start.1 = ((f32[2,512,2,256]{1,3,0,2:T(8,128)}), f32[2,512,2,256]{1,3,0,2:T(8,128)}, u32[]{:S(2)}, u32[]{:S(2)}) async-start(f32[2,512,2,256]{1,3,0,2:T(8,128)} %pad_maximum_fusion.1), calls=%async_computation.1 | async-start | bytes 4194304 | tf_op jit(solution)/shard_map/all_to_all | solution.py:76
  442.9 4.0 fusion.94
  448.7 3.6 fusion.26
  452.3 3.6 fusion.30
  455.8 3.7 fusion
  459.6 3.6 fusion.1
  (176 shorter events, 105.1 us)
Async XLA Ops:
  6.5 9.4 %copy-start.24 = (s32[4,9]{1,0:T(4,128)S(1)}, s32[4,9]{1,0:T(4,128)}, u32[]{:S(2)}) copy-start(s32[4,9]{1,0:T(4,128)} %param.11) | copy-start | bytes 436
  6.5 9.9 %copy-start.23 = (s32[4]{0:T(128)S(1)}, s32[4]{0:T(128)}, u32[]{:S(2)}) copy-start(s32[4]{0:T(128)} %param.10) | copy-start | bytes 52
  6.5 162.1 %all-gather.13.cloned.1.call-start = ((), (), s32[]{:S(2)}) async-start(), calls=%async_computation.4 | async-start | bytes 1572864 | tf_op jit(solution)/shard_map/all_gather | solution.py:68
  10.9 95.3 %collective-permute-start.6 = (bf16[2,512,512]{2,1,0:T(8,128)(2,1)}, bf16[2,512,512]{2,1,0:T(8,128)(2,1)S(1)}, u32[]{:S(2)}, u32[]{:S(2)}) collective-permute-start(bf16[2,512,512]{2,1,0:T(8,128)(2,1)} %get-tuple-element.19), channel_id=1, source_target_pairs={{0,2},{2,0},{4,6},{6,4},{8,10},{10,8},{12,14},{14,12},{1,3},{3,1},... | collective-permute-start | bytes 3145736 | tf_op jit(solution)/shard_map/ppermute | solution.py:10
  13.9 92.3 %collective-permute-start.2 = (bf16[2,512,512]{2,1,0:T(8,128)(2,1)}, bf16[2,512,512]{2,1,0:T(8,128)(2,1)S(1)}, u32[]{:S(2)}, u32[]{:S(2)}) collective-permute-start(bf16[2,512,512]{2,1,0:T(8,128)(2,1)} %get-tuple-element.20), channel_id=1, source_target_pairs={{0,2},{2,0},{4,6},{6,4},{8,10},{10,8},{12,14},{14,12},{1,3},{3,1},... | collective-permute-start | bytes 3145736 | tf_op jit(solution)/shard_map/ppermute | solution.py:10
  13.9 94.3 %collective-permute-start = (bf16[2,512,512]{2,1,0:T(8,128)(2,1)}, bf16[2,512,512]{2,1,0:T(8,128)(2,1)}, u32[]{:S(2)}, u32[]{:S(2)}) collective-permute-start(bf16[2,512,512]{2,1,0:T(8,128)(2,1)} %get-tuple-element.21), channel_id=1, source_target_pairs={{0,2},{2,0},{4,6},{6,4},{8,10},{10,8},{12,14},{14,12},{1,3},{3,1},... | collective-permute-start | bytes 3145736 | tf_op jit(solution)/shard_map/ppermute | solution.py:10
  15.9 88.8 %collective-permute-start.4 = (bf16[2,512,512]{2,1,0:T(8,128)(2,1)}, bf16[2,512,512]{2,1,0:T(8,128)(2,1)S(1)}, u32[]{:S(2)}, u32[]{:S(2)}) collective-permute-start(bf16[2,512,512]{2,1,0:T(8,128)(2,1)} %get-tuple-element.22), channel_id=1, source_target_pairs={{0,2},{2,0},{4,6},{6,4},{8,10},{10,8},{12,14},{14,12},{1,3},{3,1},... | collective-permute-start | bytes 3145736 | tf_op jit(solution)/shard_map/ppermute | solution.py:10
  115.7 14.9 %collective-permute-start.3 = (bf16[2,256,512]{2,1,0:T(8,128)(2,1)S(1)}, bf16[2,256,512]{2,1,0:T(8,128)(2,1)S(1)}, u32[]{:S(2)}, u32[]{:S(2)}) collective-permute-start(bf16[2,256,512]{2,1,0:T(8,128)(2,1)S(1)} %pad_maximum_fusion.8), channel_id=1, source_target_pairs={{0,4},{2,6},{4,0},{6,2},{8,12},{10,14},{12,8},{14,10},{1,5},{3,7},... | collective-permute-start | bytes 1572872 | tf_op jit(solution)/shard_map/ppermute | solution.py:10
  119.1 22.9 %collective-permute-start.5 = (bf16[2,256,512]{2,1,0:T(8,128)(2,1)}, bf16[2,256,512]{2,1,0:T(8,128)(2,1)}, u32[]{:S(2)}, u32[]{:S(2)}) collective-permute-start(bf16[2,256,512]{2,1,0:T(8,128)(2,1)} %pad_maximum_fusion.9), channel_id=1, source_target_pairs={{0,4},{2,6},{4,0},{6,2},{8,12},{10,14},{12,8},{14,10},{1,5},{3,7},... | collective-permute-start | bytes 1572872 | tf_op jit(solution)/shard_map/ppermute | solution.py:10
  131.5 41.6 %all-gather.17.cloned.1.call-start = ((), (), s32[]{:S(2)}) async-start(), calls=%async_computation.6 | async-start | bytes 1572864 | tf_op jit(solution)/shard_map/all_gather | solution.py:68
  132.2 9.8 %copy-start.18 = (bf16[1,256,512]{2,1,0:T(8,128)(2,1)S(1)}, bf16[1,256,512]{2,1,0:T(8,128)(2,1)}, u32[]{:S(2)}) copy-start(bf16[1,256,512]{2,1,0:T(8,128)(2,1)} %copy-done.17) | copy-start | bytes 786436
  133.8 17.7 %collective-permute-start.1 = (bf16[2,256,512]{2,1,0:T(8,128)(2,1)}, bf16[2,256,512]{2,1,0:T(8,128)(2,1)}, u32[]{:S(2)}, u32[]{:S(2)}) collective-permute-start(bf16[2,256,512]{2,1,0:T(8,128)(2,1)} %pad_maximum_fusion.7), channel_id=1, source_target_pairs={{0,4},{2,6},{4,0},{6,2},{8,12},{10,14},{12,8},{14,10},{1,5},{3,7},... | collective-permute-start | bytes 1572872 | tf_op jit(solution)/shard_map/ppermute | solution.py:10
  143.9 37.8 %all-gather.9.cloned.1.call-start = ((), (), s32[]{:S(2)}) async-start(), calls=%async_computation.2 | async-start | bytes 1572864 | tf_op jit(solution)/shard_map/all_gather | solution.py:68
  153.4 32.4 %all-gather.21.cloned.1.call-start = ((), (), s32[]{:S(2)}) async-start(), calls=%async_computation.8 | async-start | bytes 1572864 | tf_op jit(solution)/shard_map/all_gather | solution.py:68
  154.9 12.3 %collective-permute-start.7 = (bf16[2,256,512]{2,1,0:T(8,128)(2,1)S(1)}, bf16[2,256,512]{2,1,0:T(8,128)(2,1)S(1)}, u32[]{:S(2)}, u32[]{:S(2)}) collective-permute-start(bf16[2,256,512]{2,1,0:T(8,128)(2,1)S(1)} %pad_maximum_fusion.10), channel_id=1, source_target_pairs={{0,4},{2,6},{4,0},{6,2},{8,12},{10,14},{12,8},{14,10},{1,5},{3,7},... | collective-permute-start | bytes 1572872 | tf_op jit(solution)/shard_map/ppermute | solution.py:10
  168.1 205.5 %all-reduce.3.cloned.1.call-start = ((), (), s32[]{:S(2)}) async-start(), calls=%async_computation.10 | async-start | bytes 8388608 | tf_op jit(solution)/shard_map/psum | solution.py:15
  195.8 6.2 %copy-start.8 = (f32[2,256,512]{1,0,2:T(2,128)S(1)}, f32[2,256,512]{1,0,2:T(2,128)}, u32[]{:S(2)}) copy-start(f32[2,256,512]{1,0,2:T(2,128)} %copy.24) | copy-start | bytes 3145732
  216.2 168.0 %all-gather.11.cloned.1.call-start = ((), (), s32[]{:S(2)}) async-start(), calls=%async_computation.3 | async-start | bytes 3145728 | tf_op jit(solution)/shard_map/all_gather | solution.py:73
  373.6 28.8 %all-gather.15.cloned.1.call-start = ((), (), s32[]{:S(2)}) async-start(), calls=%async_computation.5 | async-start | bytes 3145728 | tf_op jit(solution)/shard_map/all_gather | solution.py:73
  374.3 39.6 %all-gather.19.cloned.1.call-start = ((), (), s32[]{:S(2)}) async-start(), calls=%async_computation.7 | async-start | bytes 3145728 | tf_op jit(solution)/shard_map/all_gather | solution.py:73
  375.1 67.8 %all-gather.23.cloned.1.call-start = ((), (), s32[]{:S(2)}) async-start(), calls=%async_computation.9 | async-start | bytes 3145728 | tf_op jit(solution)/shard_map/all_gather | solution.py:73
  375.8 12.4 %copy-start.1 = (f32[2,512,512]{2,1,0:T(8,128)S(1)}, f32[2,512,512]{2,1,0:T(8,128)}, u32[]{:S(2)}) copy-start(f32[2,512,512]{2,1,0:T(8,128)} %param.8) | copy-start | bytes 6291460
  397.3 9.1 %all-to-all-start = ((f32[2,512,2,256]{1,3,0,2:T(8,128)}), f32[2,512,2,256]{1,3,0,2:T(8,128)}, u32[]{:S(2)}, u32[]{:S(2)}) async-start(f32[2,512,2,256]{1,3,0,2:T(8,128)} %pad_maximum_fusion), calls=%async_computation | async-start | bytes 4194304 | tf_op jit(solution)/shard_map/all_to_all | solution.py:76
  438.1 8.9 %all-to-all-start.1 = ((f32[2,512,2,256]{1,3,0,2:T(8,128)}), f32[2,512,2,256]{1,3,0,2:T(8,128)}, u32[]{:S(2)}, u32[]{:S(2)}) async-start(f32[2,512,2,256]{1,3,0,2:T(8,128)} %pad_maximum_fusion.1), calls=%async_computation.1 | async-start | bytes 4194304 | tf_op jit(solution)/shard_map/all_to_all | solution.py:76
  (20 other events, 63.6 us)
Sparse Core Ops, SparseCore 0:
  131.7 9.5 all-gather.12
  144.0 9.5 all-gather.16
  155.2 10.2 all-gather.8
  168.2 8.9 all-gather.20
  216.3 157.2 all-reduce.2
  374.9 9.1 all-gather.10
  385.7 11.5 all-gather.14
  398.8 11.5 all-gather.18
  411.9 11.5 all-gather.22
where the time goes:
time: 477 us; the launch traced here: 471 us
  waiting for transfers between devices  284 us (60%)
  matrix products  65.1 us (14%)
  local copies, waits for them, and re-layouts  47.5 us (10%)
  other arithmetic  36.5 us (8%)
  starting transfers between devices  21.4 us (4%)
  between operations  16.7 us (4%)
    psum x1, waiting for transfers between devices, broadcast(): return lax.psum(block, axis)  157 us
    ppermute x8, waiting for transfers between devices, from_partner(): lax.ppermute(value, axis, [(i, i ^ 1 << apart) for i in range(lax.axis_si...  116 us
    dot_general x12, matrix products, complex_product(): jnp.dot(left_matrix[1], right_matrix[0], preferred_element_type=jnp.float...  17.9 us
    dot_general x12, matrix products, complex_product(): jnp.dot(left_matrix[1], right_matrix[1], preferred_element_type=jnp.float...  17.8 us
    dot_general x12, matrix products, complex_product(): jnp.dot(left_matrix[0], right_matrix[1], preferred_element_type=jnp.float...  15.2 us
    dot_general x12, matrix products, complex_product(): jnp.dot(left_matrix[0], right_matrix[0], preferred_element_type=jnp.float...  14.2 us
    slice x3, local copies, waits for them, and re-layouts, complex_product(): right_matrix[0]  12.1 us
    gather x4, local copies, waits for them, and re-layouts, local(): ordered_part = jnp.take(branch_part, source, axis=2)  11.9 us
  transfers between devices with their start and end apart: 19, of which 7 were waited for; matrix products, arithmetic and copies ran while one was open for 18% of the time, Pallas kernels for 0%

commit v1 on v0

v1 whole, which is shorter than its diff:
```python
import functools

import jax
import jax.numpy as jnp
from jax import lax
from jax.experimental import pallas as pl
from jax.experimental.pallas import tpu as pltpu
from jax.sharding import PartitionSpec as P

F32, BF16, I32 = jnp.float32, jnp.bfloat16, jnp.int32
NN = (((1,), (0,)), ((), ()))
NT = (((1,), (1,)), ((), ()))
CHUNKS = 2
LIMIT = 48 * 1024 * 1024


def dot(left, right, dims=NN):
    return lax.dot_general(left, right, dims, preferred_element_type=F32)


def complex_dot(lr, li, rr, ri, dims=NN):
    return dot(lr, rr, dims) - dot(li, ri, dims), dot(lr, ri, dims) + dot(li, rr, dims)


def source_of(column, modes_ref, step, modes, permuted):
    total = jnp.zeros_like(column)
    for b in range(modes):
        weight = jnp.left_shift(jnp.int32(1), modes_ref[step, b])
        total = total + jnp.where((column >> b) & 1 == 1, weight, 0)
    return jnp.where(permuted == 1, total, column)


def send_kernel(modes, meta_ref, modes_ref, leaf_ref, send_ref):
    rows, width = send_ref.shape[1:]
    y, zb, core = meta_ref[2], meta_ref[3], meta_ref[4]

    @pl.when(y == 0)
    def _():
        send_ref[...] = leaf_ref[:, pl.ds(pl.multiple_of(core * rows, rows), rows), :]

    @pl.when(y == 1)
    def _():
        column = lax.broadcasted_iota(I32, (rows, 1), 0) + core * rows
        source = source_of(column, modes_ref, meta_ref[0], modes, zb)
        picked = lax.broadcasted_iota(I32, (rows, width), 1) == source
        picked = jnp.where(picked, 1.0, 0.0).astype(BF16)
        for p in range(2):
            send_ref[p] = dot(picked, leaf_ref[p], NT).astype(BF16)


def keep_kernel(modes, meta_ref, modes_ref, leaf_ref, keep_ref):
    width = keep_ref.shape[2]
    y, zb = meta_ref[2], meta_ref[3]

    @pl.when(y == 0)
    def _():
        same = lax.broadcasted_iota(I32, (width, width), 0) == lax.broadcasted_iota(
            I32, (width, width), 1
        )
        same = jnp.where(same, 1.0, 0.0).astype(BF16)
        for p in range(2):
            keep_ref[p] = dot(same, leaf_ref[p], NT).astype(BF16)

    @pl.when(y == 1)
    def _():
        column = lax.broadcasted_iota(I32, (1, width), 1)
        source = source_of(column, modes_ref, meta_ref[1], modes, zb)
        picked = lax.broadcasted_iota(I32, (width, width), 0) == source
        picked = jnp.where(picked, 1.0, 0.0).astype(BF16)
        for p in range(2):
            keep_ref[p] = dot(leaf_ref[p], picked).astype(BF16)


def leaf_call(kernel, rows, meta, modes, leaves, which):
    width = leaves.shape[-1]
    return pl.pallas_call(
        functools.partial(kernel, modes.shape[1]),
        grid_spec=pltpu.PrefetchScalarGridSpec(
            num_scalar_prefetch=2,
            grid=(1,),
            in_specs=[
                pl.BlockSpec(
                    (None, None, 2, width, width),
                    lambda i, meta_ref, modes_ref: (0, meta_ref[which], 0, 0, 0),
                )
            ],
            out_specs=pl.BlockSpec((2, rows, width), lambda i, *_: (0, 0, 0)),
        ),
        out_shape=jax.ShapeDtypeStruct((2, rows, width), BF16),
        compiler_params=pltpu.CompilerParams(vmem_limit_bytes=LIMIT),
    )(meta, modes, leaves)


def whole(shape):
    return pl.BlockSpec(shape, lambda i, *_: (0,) * len(shape))


def call(kernel, meta, arrays, outs):
    return pl.pallas_call(
        kernel,
        grid_spec=pltpu.PrefetchScalarGridSpec(
            num_scalar_prefetch=1,
            grid=(1,),
            in_specs=[whole(a.shape) for a in arrays],
            out_specs=[whole(o.shape) for o in outs],
        ),
        out_shape=outs,
        compiler_params=pltpu.CompilerParams(vmem_limit_bytes=LIMIT),
    )(meta, *arrays)


def pair_kernel(meta_ref, left_ref, right_ref, out_ref):
    re, im = complex_dot(left_ref[0], left_ref[1], right_ref[0], right_ref[1])
    out_ref[0] = re.astype(BF16)
    out_ref[1] = im.astype(BF16)


def branch_kernel(chunks, meta_ref, left_ref, *refs):
    own, sib, out_ref = refs[:chunks], refs[chunks : 2 * chunks], refs[-1]
    core = meta_ref[4]
    part = own[0].shape[1]
    half = part * chunks
    re = im = None
    for side, group in ((core, own), (1 - core, sib)):
        for i, ref in enumerate(group):
            at = pl.ds(pl.multiple_of(side * half + i * part, part), part)
            r, m = complex_dot(left_ref[0, :, at], left_ref[1, :, at], ref[0], ref[1])
            re, im = (r, m) if re is None else (re + r, im + m)
    out_ref[0] = re.astype(BF16)
    out_ref[1] = im.astype(BF16)


def pick(first, one_ref, other_ref):
    return [jnp.where(first, one_ref[p], other_ref[p]) for p in range(2)]


def early_kernel(chunks, meta_ref, own_ref, sib_ref, *refs):
    mine, cross, mine_sib, cross_sib = (refs[i * chunks : (i + 1) * chunks] for i in range(4))
    own_out, sib_out = refs[4 * chunks :]
    first = meta_ref[2] == 0
    stems = [[ref[p].astype(BF16) for p in range(2)] for ref in (own_ref, sib_ref)]
    second = []
    for near, far in ((mine, cross), (mine_sib, cross_sib)):
        parts = [pick(first, b, a) for a, b in zip(near, far)]
        second.append([jnp.concatenate([q[p] for q in parts], 0) for p in range(2)])
    for near, far, out_ref in ((mine, cross, own_out), (mine_sib, cross_sib, sib_out)):
        parts = [pick(first, a, b) for a, b in zip(near, far)]
        turned = [jnp.concatenate([q[p] for q in parts], 0) for p in range(2)]
        re = im = None
        for stem, right in zip(stems, second):
            r, m = complex_dot(*stem, *turned, NT)
            r, m = complex_dot(r.astype(BF16), m.astype(BF16), *right)
            re, im = (r, m) if re is None else (re + r, im + m)
        out_ref[0] = re.astype(BF16)
        out_ref[1] = im.astype(BF16)


def late_kernel(chunks, meta_ref, own_ref, sib_ref, *refs):
    mine, cross, mine_sib, cross_sib = (refs[i * chunks : (i + 1) * chunks] for i in range(4))
    out_ref = refs[-1]
    first = meta_ref[2] == 0
    parts = [pick(first, a, b) for a, b in zip(mine, cross)]
    turned = [jnp.concatenate([q[p] for q in parts], 0) for p in range(2)]
    re = im = None
    for net, near, far in ((own_ref, mine, cross), (sib_ref, mine_sib, cross_sib)):
        parts = [pick(first, b, a) for a, b in zip(near, far)]
        right = [jnp.concatenate([q[p] for q in parts], 0) for p in range(2)]
        r, m = complex_dot(net[0], net[1], *turned, NT)
        r, m = complex_dot(r.astype(BF16), m.astype(BF16), *right)
        re, im = (r, m) if re is None else (re + r, im + m)
    out_ref[0] = re
    out_ref[1] = im


def swap(value, axis, bit, among=lambda i: True):
    n = lax.axis_size(axis)
    return lax.ppermute(value, axis, [(i, i ^ bit) for i in range(n) if among(i)])


def holds(i):
    return i >> 1 & 1 == i & 1


def after(value, *others):
    return lax.optimization_barrier((value, *others))[0]


def local(stem_tensor, leaves, root_devices, mode_orders):
    steps, width = leaves.shape[1], stem_tensor.shape[2]
    wide = lax.axis_size("wide")
    half = width // lax.axis_size("narrow")
    part = half // CHUNKS
    w = lax.axis_index("wide")
    core = lax.axis_index("narrow")
    y, zb, group = w & 1, w >> 1 & 1, w >> 2
    holder = y == zb
    piece = jax.ShapeDtypeStruct((2, part, width), BF16)

    own_stem = stem_tensor.astype(BF16)
    sib_stem = swap(own_stem, "narrow", 1)

    branches = []
    gate = ()
    for j in range(steps // 2):
        k_keep = 2 * j + y
        k_send = 2 * j + 1 - y
        meta = jnp.stack([k_send, k_keep, y, zb, core]).astype(I32)
        send = leaf_call(send_kernel, half, meta, mode_orders, leaves, 0)
        keep = leaf_call(keep_kernel, width, meta, mode_orders, leaves, 1)
        pairs = []
        got = []
        for i in range(CHUNKS):
            chunk = send[:, i * part : (i + 1) * part]
            if gate:
                chunk = after(chunk, gate[i])
            left = swap(chunk, "wide", 1)
            got.append(left)
            pairs.append(call(pair_kernel, meta, [left, keep], [piece])[0])
        gate = got
        sibs = [swap(p, "narrow", 1) for p in pairs]
        out = []
        for i in range(CHUNKS):
            low = swap(pairs[i], "wide", 2, lambda i: not holds(i))
            [made] = call(
                functools.partial(branch_kernel, CHUNKS), meta, [low, *pairs, *sibs], [piece]
            )
            out.append(made)
        owner = root_devices[k_keep] // 4
        mine = []
        cross = []
        for made in out:
            if wide == 8:
                other = swap(made, "wide", 4, holds)
                made = jnp.where(owner == group, made, other)
                passed = swap(made, "wide", 2, holds)
                made = jnp.where(holder, made, passed)
                mine.append(made)
                cross.append(swap(made, "wide", 1))
            else:
                good = holder & (owner == group)
                both = [
                    lax.psum(jnp.where(good & (y == side), made, jnp.zeros_like(made)), "wide")
                    for side in range(2)
                ]
                mine.append(jnp.where(y == 0, both[0], both[1]))
                cross.append(jnp.where(y == 0, both[1], both[0]))
        branches.append(
            [
                *mine,
                *cross,
                *[swap(m, "narrow", 1) for m in mine],
                *[swap(m, "narrow", 1) for m in cross],
            ]
        )

    middle = jax.ShapeDtypeStruct((2, stem_tensor.shape[1], width), BF16)
    own, sib = call(
        functools.partial(early_kernel, CHUNKS),
        meta,
        [own_stem, sib_stem, *branches[0]],
        [middle, middle],
    )
    result = jax.ShapeDtypeStruct(stem_tensor.shape, F32)
    return call(functools.partial(late_kernel, CHUNKS), meta, [own, sib, *branches[1]], [result])[0]


def solution(mesh):
    placed = (
        P(None, ("cuts", "wide", "narrow"), None),
        P(("cuts", "wide"), None, None, None, None),
        P(),
        P(),
    )
    return jax.shard_map(
        local,
        mesh=mesh,
        in_specs=placed,
        out_specs=P(None, ("cuts", "wide", "narrow"), None),
        check_vma=False,
    )
```

time: 477 us -> 125 us (0.26); the launches traced: 471 us -> 124 us
  waiting for transfers between devices: 284 us -> 34.5 us
  matrix products: 65.1 us -> 0 us
  local copies, waits for them, and re-layouts: 47.5 us -> 6.62 us
  other arithmetic: 36.5 us -> 2.97 us
  starting transfers between devices: 21.4 us -> 48.7 us
  Pallas kernels: 0 us -> 26.6 us
  between operations: 16.7 us -> 5.03 us
    psum x1 -> x0, waiting for transfers between devices: 157 us -> none  [broadcast(): return lax.psum(block, axis)]
    ppermute x8 -> x33, waiting for transfers between devices: 116 us -> 34.5 us  [swap(): lax.ppermute(value, axis, [(i, i ^ bit) for i in range(n) if among(i)])]
    dot_general x48 -> x0, matrix products: 65.1 us -> none  [the longest x12 17.9 us: complex_product(): jnp.dot(left_matrix[1], right_matrix[0], preferred_element_type=jnp.float...]
    ppermute x8 -> x33, starting transfers between devices: 10.5 us -> 48.7 us  [swap(): lax.ppermute(value, axis, [(i, i ^ bit) for i in range(n) if among(i)])]
    pallas_call x0 -> x14, Pallas kernels: none -> 26.6 us  [the longest x10 22.7 us: call(): pl.pallas_call(kernel, grid_spec=pltpu.PrefetchScalarGridSpec(num_scalar_...]
    select_n x17 -> x8, other arithmetic: 26.4 us -> 1.25 us  [the longest x4 1.13 us: local(): made = jnp.where(owner == group, made, other)]
    slice x7 -> x2, local copies, waits for them, and re-layouts: 21.5 us -> 0.77 us  [local(): chunk = send[:, i * part:(i + 1) * part]]
    gather x4 -> x0, local copies, waits for them, and re-layouts: 11.9 us -> none  [local(): ordered_part = jnp.take(branch_part, source, axis=2)]
  transfers between devices with their start and end apart: 19 -> 33, of which waited for: 7 -> 9; matrix products, arithmetic and copies ran while one was open for 18% -> 4% of each run, Pallas kernels for 0% -> 17%
where the time goes in v1:
time: 125 us; the launch traced here: 124 us
  starting transfers between devices  48.7 us (39%)
  waiting for transfers between devices  34.5 us (28%)
  Pallas kernels  26.6 us (21%)
  local copies, waits for them, and re-layouts  6.62 us (5%)
  between operations  5.03 us (4%)
  other arithmetic  2.97 us (2%)
    ppermute x33, starting transfers between devices, swap(): lax.ppermute(value, axis, [(i, i ^ bit) for i in range(n) if among(i)])  48.7 us
    ppermute x33, waiting for transfers between devices, swap(): lax.ppermute(value, axis, [(i, i ^ bit) for i in range(n) if among(i)])  34.5 us
    pallas_call x10, Pallas kernels, call(): pl.pallas_call(kernel, grid_spec=pltpu.PrefetchScalarGridSpec(num_scalar_...  22.7 us
    unnamed x14, local copies, waits for them, and re-layouts  5.08 us
    pallas_call x4, Pallas kernels, leaf_call(): pl.pallas_call(functools.partial(kernel, modes.shape[1]), grid_spec=pltpu...  3.86 us
  transfers between devices with their start and end apart: 33, of which 9 were waited for; matrix products, arithmetic and copies ran while one was open for 4% of the time, Pallas kernels for 17%

profile of v1, /device:TPU:0, one launch (start us, length us, event | category | flops | bytes accessed | tf_op | source)
XLA Modules:
  0.0 124.3 jit_solution(7320315218646734370)
XLA Ops:
  0.1 2.2 %copy-done = bf16[1,4,2,512,512]{4,3,2,1,0:T(8,128)(2,1)S(1)} copy-done((bf16[1,4,2,512,512]{4,3,2,1,0:T(8,128)(2,1)S(1)}, bf16[1,4,2,512,512]{4,3,2,1,0:T(8,128)(2,1)}, u32[]{:S(2)}) %copy-start) | copy-done | bytes 4194328
  3.6 3.6 %collective-permute-start.1 = (bf16[2,128,512]{2,1,0:T(8,128)(2,1)S(1)}, bf16[2,128,512]{2,1,0:T(8,128)(2,1)S(1)}, u32[]{:S(2)}, u32[]{:S(2)}) collective-permute-start(bf16[2,128,512]{2,1,0:T(8,128)(2,1)S(1)} %get-tuple-element.16), channel_id=1, source_target_pairs={{0,2},{2,0},{4,6},{6,4},{8,10},{10,8},{12,14},{14,12},{1,3},{3,1},... | collective-permute-start | bytes 786440 | tf_op jit(solution)/shard_map/ppermute | solution.py:177
  8.7 2.2 %copy-done.1 = bf16[1,4,2,512,512]{4,3,2,1,0:T(8,128)(2,1)S(1)} copy-done((bf16[1,4,2,512,512]{4,3,2,1,0:T(8,128)(2,1)S(1)}, bf16[1,4,2,512,512]{4,3,2,1,0:T(8,128)(2,1)}, u32[]{:S(2)}) %copy-start.1) | copy-done | bytes 4194328
  11.5 2.8 %collective-permute-done.1.left_ref = bf16[2,128,512]{2,1,0:T(8,128)(2,1)S(1)} collective-permute-done((bf16[2,128,512]{2,1,0:T(8,128)(2,1)S(1)}, bf16[2,128,512]{2,1,0:T(8,128)(2,1)S(1)}, u32[]{:S(2)}, u32[]{:S(2)}) %collective-permute-start.1) | collective-permute-done | bytes 262176 | tf_op jit(solution)/shard_map/ppermute | solution.py:177
  17.0 2.1 %collective-permute-done.3.left_ref = bf16[2,128,512]{2,1,0:T(8,128)(2,1)S(1)} collective-permute-done((bf16[2,128,512]{2,1,0:T(8,128)(2,1)S(1)}, bf16[2,128,512]{2,1,0:T(8,128)(2,1)S(1)}, u32[]{:S(2)}, u32[]{:S(2)}) %collective-permute-start.3) | collective-permute-done | bytes 262176 | tf_op jit(solution)/shard_map/ppermute | solution.py:177
  20.9 2.6 %collective-permute-start.17 = (bf16[2,128,512]{2,1,0:T(8,128)(2,1)S(1)}, bf16[2,128,512]{2,1,0:T(8,128)(2,1)S(1)}, u32[]{:S(2)}, u32[]{:S(2)}) collective-permute-start(bf16[2,128,512]{2,1,0:T(8,128)(2,1)S(1)} %get-tuple-element.11), channel_id=1, source_target_pairs={{0,2},{2,0},{4,6},{6,4},{8,10},{10,8},{12,14},{14,12},{1,3},{3,1},... | collective-permute-start | bytes 786440 | tf_op jit(solution)/shard_map/ppermute | solution.py:177
  26.7 4.5 %collective-permute-start.6 = (bf16[2,128,512]{2,1,0:T(8,128)(2,1)S(1)}, bf16[2,128,512]{2,1,0:T(8,128)(2,1)}, u32[]{:S(2)}, u32[]{:S(2)}) collective-permute-start(bf16[2,128,512]{2,1,0:T(8,128)(2,1)S(1)} %shard_map.50), channel_id=1, source_target_pairs={{0,8},{6,14},{8,0},{14,6},{1,9},{7,15},{9,1},{15,7},{16,24},{22,30... | collective-permute-start | bytes 786440 | tf_op jit(solution)/shard_map/ppermute | solution.py:177
  39.3 1.6 %collective-permute-done.8.left_ref = bf16[2,128,512]{2,1,0:T(8,128)(2,1)} collective-permute-done((bf16[2,128,512]{2,1,0:T(8,128)(2,1)S(1)}, bf16[2,128,512]{2,1,0:T(8,128)(2,1)}, u32[]{:S(2)}, u32[]{:S(2)}) %collective-permute-start.8) | collective-permute-done | bytes 262176 | tf_op jit(solution)/shard_map/ppermute | solution.py:177
  41.0 2.9 %shard_map.51 = bf16[2,128,512]{2,1,0:T(8,128)(2,1)} custom-call(s32[5]{0:T(128)S(1)} %stack.35.meta_ref, bf16[2,128,512]{2,1,0:T(8,128)(2,1)} %collective-permute-done.8.left_ref, bf16[2,128,512]{2,1,0:T(8,128)(2,1)S(1)} %shard_map.48.refs_0_, bf16[2,128,512]{2,1,0:T(8,128)(2,1)S(1)} %shard_map.49.refs_1_, ...), custom_call_target="tpu_custom_call" | custom-call | tf_op jit(solution)/shard_map/pallas_call | solution.py:99
  43.9 1.9 %collective-permute-start.9 = (bf16[2,128,512]{2,1,0:T(8,128)(2,1)}, bf16[2,128,512]{2,1,0:T(8,128)(2,1)S(1)}, u32[]{:S(2)}, u32[]{:S(2)}) collective-permute-start(bf16[2,128,512]{2,1,0:T(8,128)(2,1)} %shard_map.51), channel_id=1, source_target_pairs={{0,8},{6,14},{8,0},{14,6},{1,9},{7,15},{9,1},{15,7},{16,24},{22,30... | collective-permute-start | bytes 786440 | tf_op jit(solution)/shard_map/ppermute | solution.py:177
  47.2 4.6 %collective-permute-start.7 = (bf16[2,128,512]{2,1,0:T(8,128)(2,1)S(1)}, bf16[2,128,512]{2,1,0:T(8,128)(2,1)S(1)}, u32[]{:S(2)}, u32[]{:S(2)}) collective-permute-start(bf16[2,128,512]{2,1,0:T(8,128)(2,1)S(1)} %broadcast_select_fusion.3), channel_id=1, source_target_pairs={{0,4},{6,2},{8,12},{14,10},{1,5},{7,3},{9,13},{15,11},{16,20},{22,... | collective-permute-start | bytes 786440 | tf_op jit(solution)/shard_map/ppermute | solution.py:177
  54.0 1.7 %convert_element_type.3.own_ref = bf16[2,512,512]{2,1,0:T(8,128)(2,1)S(1)} convert(f32[2,512,512]{2,1,0:T(8,128)} %param.4) | non-fusion elementwise | flops 524288 | bytes 3145728 | tf_op jit(solution)/shard_map/convert_element_type | solution.py:199
  55.9 2.2 %shard_map.57 = bf16[2,128,512]{2,1,0:T(8,128)(2,1)S(1)} custom-call(s32[5]{0:T(128)S(1)} %stack.33.meta_ref, bf16[2,128,512]{2,1,0:T(8,128)(2,1)} %collective-permute-done.18.left_ref, bf16[2,128,512]{2,1,0:T(8,128)(2,1)S(1)} %shard_map.55.refs_0_, bf16[2,128,512]{2,1,0:T(8,128)(2,1)S(1)} %shard_map.56.refs_1_, ...), custom_call_target="tpu_custom_call" | custom-call | tf_op jit(solution)/shard_map/pallas_call | solution.py:99
  58.1 5.8 %collective-permute-start.22 = (bf16[2,128,512]{2,1,0:T(8,128)(2,1)S(1)}, bf16[2,128,512]{2,1,0:T(8,128)(2,1)S(1)}, u32[]{:S(2)}, u32[]{:S(2)}) collective-permute-start(bf16[2,128,512]{2,1,0:T(8,128)(2,1)S(1)} %shard_map.57), channel_id=1, source_target_pairs={{0,8},{6,14},{8,0},{14,6},{1,9},{7,15},{9,1},{15,7},{16,24},{22,30... | collective-permute-start | bytes 786440 | tf_op jit(solution)/shard_map/ppermute | solution.py:177
  67.4 1.9 %collective-permute-start.25 = (bf16[2,128,512]{2,1,0:T(8,128)(2,1)S(1)}, bf16[2,128,512]{2,1,0:T(8,128)(2,1)S(1)}, u32[]{:S(2)}, u32[]{:S(2)}) collective-permute-start(bf16[2,128,512]{2,1,0:T(8,128)(2,1)S(1)} %shard_map.58), channel_id=1, source_target_pairs={{0,8},{6,14},{8,0},{14,6},{1,9},{7,15},{9,1},{15,7},{16,24},{22,30... | collective-permute-start | bytes 786440 | tf_op jit(solution)/shard_map/ppermute | solution.py:177
  70.8 10.5 %collective-permute-done.25 = bf16[2,128,512]{2,1,0:T(8,128)(2,1)S(1)} collective-permute-done((bf16[2,128,512]{2,1,0:T(8,128)(2,1)S(1)}, bf16[2,128,512]{2,1,0:T(8,128)(2,1)S(1)}, u32[]{:S(2)}, u32[]{:S(2)}) %collective-permute-start.25) | collective-permute-done | bytes 262176 | tf_op jit(solution)/shard_map/ppermute | solution.py:177
  84.2 5.1 %collective-permute-done.23 = bf16[2,128,512]{2,1,0:T(8,128)(2,1)S(1)} collective-permute-done((bf16[2,128,512]{2,1,0:T(8,128)(2,1)S(1)}, bf16[2,128,512]{2,1,0:T(8,128)(2,1)S(1)}, u32[]{:S(2)}, u32[]{:S(2)}) %collective-permute-start.23) | collective-permute-done | bytes 262176 | tf_op jit(solution)/shard_map/ppermute | solution.py:177
  89.2 6.5 %collective-permute-start.12 = (bf16[2,128,512]{2,1,0:T(8,128)(2,1)S(1)}, bf16[2,128,512]{2,1,0:T(8,128)(2,1)S(1)}, u32[]{:S(2)}, u32[]{:S(2)}) collective-permute-start(bf16[2,128,512]{2,1,0:T(8,128)(2,1)S(1)} %broadcast_select_fusion.6.refs_1_), channel_id=1, source_target_pairs={{0,2},{2,0},{4,6},{6,4},{8,10},{10,8},{12,14},{14,12},{1,3},{3,1},... | collective-permute-start | bytes 786440 | tf_op jit(solution)/shard_map/ppermute | solution.py:177
  96.4 4.1 %collective-permute-start.27 = (bf16[2,128,512]{2,1,0:T(8,128)(2,1)S(1)}, bf16[2,128,512]{2,1,0:T(8,128)(2,1)S(1)}, u32[]{:S(2)}, u32[]{:S(2)}) collective-permute-start(bf16[2,128,512]{2,1,0:T(8,128)(2,1)S(1)} %broadcast_select_fusion.5.refs_0_), channel_id=1, source_target_pairs={{0,2},{2,0},{4,6},{6,4},{8,10},{10,8},{12,14},{14,12},{1,3},{3,1},... | collective-permute-start | bytes 786440 | tf_op jit(solution)/shard_map/ppermute | solution.py:177
  100.5 1.6 %collective-permute-start.28 = (bf16[2,128,512]{2,1,0:T(8,128)(2,1)S(1)}, bf16[2,128,512]{2,1,0:T(8,128)(2,1)S(1)}, u32[]{:S(2)}, u32[]{:S(2)}) collective-permute-start(bf16[2,128,512]{2,1,0:T(8,128)(2,1)S(1)} %broadcast_select_fusion.4.refs_1_), channel_id=1, source_target_pairs={{0,2},{2,0},{4,6},{6,4},{8,10},{10,8},{12,14},{14,12},{1,3},{3,1},... | collective-permute-start | bytes 786440 | tf_op jit(solution)/shard_map/ppermute | solution.py:177
  102.7 5.0 %collective-permute-done.27.refs_2_ = bf16[2,128,512]{2,1,0:T(8,128)(2,1)S(1)} collective-permute-done((bf16[2,128,512]{2,1,0:T(8,128)(2,1)S(1)}, bf16[2,128,512]{2,1,0:T(8,128)(2,1)S(1)}, u32[]{:S(2)}, u32[]{:S(2)}) %collective-permute-start.27) | collective-permute-done | bytes 262176 | tf_op jit(solution)/shard_map/ppermute | solution.py:177
  107.6 5.4 %collective-permute-done.28.refs_3_ = bf16[2,128,512]{2,1,0:T(8,128)(2,1)S(1)} collective-permute-done((bf16[2,128,512]{2,1,0:T(8,128)(2,1)S(1)}, bf16[2,128,512]{2,1,0:T(8,128)(2,1)S(1)}, u32[]{:S(2)}, u32[]{:S(2)}) %collective-permute-start.28) | collective-permute-done | bytes 262176 | tf_op jit(solution)/shard_map/ppermute | solution.py:177
  113.1 6.7 %shard_map.52 = (bf16[2,512,512]{2,1,0:T(8,128)(2,1)S(1)}, bf16[2,512,512]{2,1,0:T(8,128)(2,1)S(1)}) custom-call(s32[5]{0:T(128)S(1)} %stack.33.meta_ref, bf16[2,512,512]{2,1,0:T(8,128)(2,1)S(1)} %convert_element_type.3.own_ref, bf16[2,512,512]{2,1,0:T(8,128)(2,1)} %copy-done.5, bf16[2,128,512]{2,1,0:T(8,128)(2,1)S(1)} %broadcast_select_fusion.7.refs_0_, ...), custom_call_target="tpu_custom_call" | custom-call | tf_op jit(solution)/shard_map/pallas_call | solution.py:99
  119.8 4.5 %shard_map.59 = f32[2,512,512]{2,1,0:T(8,128)} custom-call(s32[5]{0:T(128)S(1)} %stack.33.meta_ref, bf16[2,512,512]{2,1,0:T(8,128)(2,1)S(1)} %get-tuple-element.9.own_ref, bf16[2,512,512]{2,1,0:T(8,128)(2,1)S(1)} %get-tuple-element.10.sib_ref, bf16[2,128,512]{2,1,0:T(8,128)(2,1)S(1)} %broadcast_select_fusion.5.refs_0_, ...), custom_call_target="tpu_custom_call" | custom-call | tf_op jit(solution)/shard_map/pallas_call | solution.py:99
  (84 shorter events, 27.4 us)
Async XLA Ops:
  7.2 11.9 %collective-permute-start.3 = (bf16[2,128,512]{2,1,0:T(8,128)(2,1)S(1)}, bf16[2,128,512]{2,1,0:T(8,128)(2,1)S(1)}, u32[]{:S(2)}, u32[]{:S(2)}) collective-permute-start(bf16[2,128,512]{2,1,0:T(8,128)(2,1)S(1)} %get-tuple-element.15), channel_id=1, source_target_pairs={{0,2},{2,0},{4,6},{6,4},{8,10},{10,8},{12,14},{14,12},{1,3},{3,1},... | collective-permute-start | bytes 786440 | tf_op jit(solution)/shard_map/ppermute | solution.py:177
  20.9 11.6 %collective-permute-start.17 = (bf16[2,128,512]{2,1,0:T(8,128)(2,1)S(1)}, bf16[2,128,512]{2,1,0:T(8,128)(2,1)S(1)}, u32[]{:S(2)}, u32[]{:S(2)}) collective-permute-start(bf16[2,128,512]{2,1,0:T(8,128)(2,1)S(1)} %get-tuple-element.11), channel_id=1, source_target_pairs={{0,2},{2,0},{4,6},{6,4},{8,10},{10,8},{12,14},{14,12},{1,3},{3,1},... | collective-permute-start | bytes 786440 | tf_op jit(solution)/shard_map/ppermute | solution.py:177
  23.5 14.3 %collective-permute-start.19 = (bf16[2,128,512]{2,1,0:T(8,128)(2,1)}, bf16[2,128,512]{2,1,0:T(8,128)(2,1)S(1)}, u32[]{:S(2)}, u32[]{:S(2)}) collective-permute-start(bf16[2,128,512]{2,1,0:T(8,128)(2,1)} %get-tuple-element.12), channel_id=1, source_target_pairs={{0,2},{2,0},{4,6},{6,4},{8,10},{10,8},{12,14},{14,12},{1,3},{3,1},... | collective-permute-start | bytes 786440 | tf_op jit(solution)/shard_map/ppermute | solution.py:177
  24.1 16.8 %collective-permute-start.8 = (bf16[2,128,512]{2,1,0:T(8,128)(2,1)S(1)}, bf16[2,128,512]{2,1,0:T(8,128)(2,1)}, u32[]{:S(2)}, u32[]{:S(2)}) collective-permute-start(bf16[2,128,512]{2,1,0:T(8,128)(2,1)S(1)} %shard_map.49.refs_1_), channel_id=1, source_target_pairs={{2,6},{4,0},{10,14},{12,8},{3,7},{5,1},{11,15},{13,9},{18,22},{20,... | collective-permute-start | bytes 786440 | tf_op jit(solution)/shard_map/ppermute | solution.py:177
  26.7 19.1 %collective-permute-start.6 = (bf16[2,128,512]{2,1,0:T(8,128)(2,1)S(1)}, bf16[2,128,512]{2,1,0:T(8,128)(2,1)}, u32[]{:S(2)}, u32[]{:S(2)}) collective-permute-start(bf16[2,128,512]{2,1,0:T(8,128)(2,1)S(1)} %shard_map.50), channel_id=1, source_target_pairs={{0,8},{6,14},{8,0},{14,6},{1,9},{7,15},{9,1},{15,7},{16,24},{22,30... | collective-permute-start | bytes 786440 | tf_op jit(solution)/shard_map/ppermute | solution.py:177
  33.5 13.6 %collective-permute-start.18 = (bf16[2,128,512]{2,1,0:T(8,128)(2,1)S(1)}, bf16[2,128,512]{2,1,0:T(8,128)(2,1)}, u32[]{:S(2)}, u32[]{:S(2)}) collective-permute-start(bf16[2,128,512]{2,1,0:T(8,128)(2,1)S(1)} %shard_map.55.refs_0_), channel_id=1, source_target_pairs={{2,6},{4,0},{10,14},{12,8},{3,7},{5,1},{11,15},{13,9},{18,22},{20,... | collective-permute-start | bytes 786440 | tf_op jit(solution)/shard_map/ppermute | solution.py:177
  37.7 18.1 %collective-permute-start.20 = (bf16[2,128,512]{2,1,0:T(8,128)(2,1)S(1)}, bf16[2,128,512]{2,1,0:T(8,128)(2,1)S(1)}, u32[]{:S(2)}, u32[]{:S(2)}) collective-permute-start(bf16[2,128,512]{2,1,0:T(8,128)(2,1)S(1)} %shard_map.55.refs_0_), channel_id=1, source_target_pairs={{0,1},{1,0},{2,3},{3,2},{4,5},{5,4},{6,7},{7,6},{8,9},{9,8},{10,11... | collective-permute-start | bytes 786440 | tf_op jit(solution)/shard_map/ppermute | solution.py:177
  38.8 17.1 %collective-permute-start.21 = (bf16[2,128,512]{2,1,0:T(8,128)(2,1)S(1)}, bf16[2,128,512]{2,1,0:T(8,128)(2,1)S(1)}, u32[]{:S(2)}, u32[]{:S(2)}) collective-permute-start(bf16[2,128,512]{2,1,0:T(8,128)(2,1)S(1)} %shard_map.56.refs_1_), channel_id=1, source_target_pairs={{0,1},{1,0},{2,3},{3,2},{4,5},{5,4},{6,7},{7,6},{8,9},{9,8},{10,11... | collective-permute-start | bytes 786440 | tf_op jit(solution)/shard_map/ppermute | solution.py:177
  43.9 20.0 %collective-permute-start.9 = (bf16[2,128,512]{2,1,0:T(8,128)(2,1)}, bf16[2,128,512]{2,1,0:T(8,128)(2,1)S(1)}, u32[]{:S(2)}, u32[]{:S(2)}) collective-permute-start(bf16[2,128,512]{2,1,0:T(8,128)(2,1)} %shard_map.51), channel_id=1, source_target_pairs={{0,8},{6,14},{8,0},{14,6},{1,9},{7,15},{9,1},{15,7},{16,24},{22,30... | collective-permute-start | bytes 786440 | tf_op jit(solution)/shard_map/ppermute | solution.py:177
  45.8 20.4 %collective-permute-start.24 = (bf16[2,128,512]{2,1,0:T(8,128)(2,1)S(1)}, bf16[2,128,512]{2,1,0:T(8,128)(2,1)S(1)}, u32[]{:S(2)}, u32[]{:S(2)}) collective-permute-start(bf16[2,128,512]{2,1,0:T(8,128)(2,1)S(1)} %shard_map.56.refs_1_), channel_id=1, source_target_pairs={{2,6},{4,0},{10,14},{12,8},{3,7},{5,1},{11,15},{13,9},{18,22},{20,... | collective-permute-start | bytes 786440 | tf_op jit(solution)/shard_map/ppermute | solution.py:177
  47.2 22.2 %collective-permute-start.7 = (bf16[2,128,512]{2,1,0:T(8,128)(2,1)S(1)}, bf16[2,128,512]{2,1,0:T(8,128)(2,1)S(1)}, u32[]{:S(2)}, u32[]{:S(2)}) collective-permute-start(bf16[2,128,512]{2,1,0:T(8,128)(2,1)S(1)} %broadcast_select_fusion.3), channel_id=1, source_target_pairs={{0,4},{6,2},{8,12},{14,10},{1,5},{7,3},{9,13},{15,11},{16,20},{22,... | collective-permute-start | bytes 786440 | tf_op jit(solution)/shard_map/ppermute | solution.py:177
  55.8 40.6 %collective-permute-start = (bf16[2,512,512]{2,1,0:T(8,128)(2,1)S(1)}, bf16[2,512,512]{2,1,0:T(8,128)(2,1)S(1)}, u32[]{:S(2)}, u32[]{:S(2)}) collective-permute-start(bf16[2,512,512]{2,1,0:T(8,128)(2,1)S(1)} %convert_element_type.3.own_ref), channel_id=1, source_target_pairs={{0,1},{1,0},{2,3},{3,2},{4,5},{5,4},{6,7},{7,6},{8,9},{9,8},{10,11... | collective-permute-start | bytes 3145736 | tf_op jit(solution)/shard_map/ppermute | solution.py:177
  58.1 12.7 %collective-permute-start.22 = (bf16[2,128,512]{2,1,0:T(8,128)(2,1)S(1)}, bf16[2,128,512]{2,1,0:T(8,128)(2,1)S(1)}, u32[]{:S(2)}, u32[]{:S(2)}) collective-permute-start(bf16[2,128,512]{2,1,0:T(8,128)(2,1)S(1)} %shard_map.57), channel_id=1, source_target_pairs={{0,8},{6,14},{8,0},{14,6},{1,9},{7,15},{9,1},{15,7},{16,24},{22,30... | collective-permute-start | bytes 786440 | tf_op jit(solution)/shard_map/ppermute | solution.py:177
  64.9 17.8 %collective-permute-start.10 = (bf16[2,128,512]{2,1,0:T(8,128)(2,1)S(1)}, bf16[2,128,512]{2,1,0:T(8,128)(2,1)S(1)}, u32[]{:S(2)}, u32[]{:S(2)}) collective-permute-start(bf16[2,128,512]{2,1,0:T(8,128)(2,1)S(1)} %broadcast_select_fusion.2), channel_id=1, source_target_pairs={{0,4},{6,2},{8,12},{14,10},{1,5},{7,3},{9,13},{15,11},{16,20},{22,... | collective-permute-start | bytes 786440 | tf_op jit(solution)/shard_map/ppermute | solution.py:177
  67.4 13.8 %collective-permute-start.25 = (bf16[2,128,512]{2,1,0:T(8,128)(2,1)S(1)}, bf16[2,128,512]{2,1,0:T(8,128)(2,1)S(1)}, u32[]{:S(2)}, u32[]{:S(2)}) collective-permute-start(bf16[2,128,512]{2,1,0:T(8,128)(2,1)S(1)} %shard_map.58), channel_id=1, source_target_pairs={{0,8},{6,14},{8,0},{14,6},{1,9},{7,15},{9,1},{15,7},{16,24},{22,30... | collective-permute-start | bytes 786440 | tf_op jit(solution)/shard_map/ppermute | solution.py:177
  69.4 26.3 %collective-permute-start.11 = (bf16[2,128,512]{2,1,0:T(8,128)(2,1)S(1)}, bf16[2,128,512]{2,1,0:T(8,128)(2,1)S(1)}, u32[]{:S(2)}, u32[]{:S(2)}) collective-permute-start(bf16[2,128,512]{2,1,0:T(8,128)(2,1)S(1)} %broadcast_select_fusion.7.refs_0_), channel_id=1, source_target_pairs={{0,2},{2,0},{4,6},{6,4},{8,10},{10,8},{12,14},{14,12},{1,3},{3,1},... | collective-permute-start | bytes 786440 | tf_op jit(solution)/shard_map/ppermute | solution.py:177
  70.8 31.3 %collective-permute-start.13 = (bf16[2,128,512]{2,1,0:T(8,128)(2,1)S(1)}, bf16[2,128,512]{2,1,0:T(8,128)(2,1)S(1)}, u32[]{:S(2)}, u32[]{:S(2)}) collective-permute-start(bf16[2,128,512]{2,1,0:T(8,128)(2,1)S(1)} %broadcast_select_fusion.7.refs_0_), channel_id=1, source_target_pairs={{0,1},{1,0},{2,3},{3,2},{4,5},{5,4},{6,7},{7,6},{8,9},{9,8},{10,11... | collective-permute-start | bytes 786440 | tf_op jit(solution)/shard_map/ppermute | solution.py:177
  82.6 13.2 %collective-permute-start.26 = (bf16[2,128,512]{2,1,0:T(8,128)(2,1)S(1)}, bf16[2,128,512]{2,1,0:T(8,128)(2,1)S(1)}, u32[]{:S(2)}, u32[]{:S(2)}) collective-permute-start(bf16[2,128,512]{2,1,0:T(8,128)(2,1)S(1)} %broadcast_select_fusion), channel_id=1, source_target_pairs={{0,4},{6,2},{8,12},{14,10},{1,5},{7,3},{9,13},{15,11},{16,20},{22,... | collective-permute-start | bytes 786440 | tf_op jit(solution)/shard_map/ppermute | solution.py:177
  89.2 11.3 %collective-permute-start.12 = (bf16[2,128,512]{2,1,0:T(8,128)(2,1)S(1)}, bf16[2,128,512]{2,1,0:T(8,128)(2,1)S(1)}, u32[]{:S(2)}, u32[]{:S(2)}) collective-permute-start(bf16[2,128,512]{2,1,0:T(8,128)(2,1)S(1)} %broadcast_select_fusion.6.refs_1_), channel_id=1, source_target_pairs={{0,2},{2,0},{4,6},{6,4},{8,10},{10,8},{12,14},{14,12},{1,3},{3,1},... | collective-permute-start | bytes 786440 | tf_op jit(solution)/shard_map/ppermute | solution.py:177
  96.4 11.3 %collective-permute-start.27 = (bf16[2,128,512]{2,1,0:T(8,128)(2,1)S(1)}, bf16[2,128,512]{2,1,0:T(8,128)(2,1)S(1)}, u32[]{:S(2)}, u32[]{:S(2)}) collective-permute-start(bf16[2,128,512]{2,1,0:T(8,128)(2,1)S(1)} %broadcast_select_fusion.5.refs_0_), channel_id=1, source_target_pairs={{0,2},{2,0},{4,6},{6,4},{8,10},{10,8},{12,14},{14,12},{1,3},{3,1},... | collective-permute-start | bytes 786440 | tf_op jit(solution)/shard_map/ppermute | solution.py:177
  100.5 12.6 %collective-permute-start.28 = (bf16[2,128,512]{2,1,0:T(8,128)(2,1)S(1)}, bf16[2,128,512]{2,1,0:T(8,128)(2,1)S(1)}, u32[]{:S(2)}, u32[]{:S(2)}) collective-permute-start(bf16[2,128,512]{2,1,0:T(8,128)(2,1)S(1)} %broadcast_select_fusion.4.refs_1_), channel_id=1, source_target_pairs={{0,2},{2,0},{4,6},{6,4},{8,10},{10,8},{12,14},{14,12},{1,3},{3,1},... | collective-permute-start | bytes 786440 | tf_op jit(solution)/shard_map/ppermute | solution.py:177
  102.1 17.7 %collective-permute-start.29 = (bf16[2,128,512]{2,1,0:T(8,128)(2,1)S(1)}, bf16[2,128,512]{2,1,0:T(8,128)(2,1)S(1)}, u32[]{:S(2)}, u32[]{:S(2)}) collective-permute-start(bf16[2,128,512]{2,1,0:T(8,128)(2,1)S(1)} %broadcast_select_fusion.5.refs_0_), channel_id=1, source_target_pairs={{0,1},{1,0},{2,3},{3,2},{4,5},{5,4},{6,7},{7,6},{8,9},{9,8},{10,11... | collective-permute-start | bytes 786440 | tf_op jit(solution)/shard_map/ppermute | solution.py:177
  102.6 17.2 %collective-permute-start.30 = (bf16[2,128,512]{2,1,0:T(8,128)(2,1)S(1)}, bf16[2,128,512]{2,1,0:T(8,128)(2,1)S(1)}, u32[]{:S(2)}, u32[]{:S(2)}) collective-permute-start(bf16[2,128,512]{2,1,0:T(8,128)(2,1)S(1)} %broadcast_select_fusion.4.refs_1_), channel_id=1, source_target_pairs={{0,1},{1,0},{2,3},{3,2},{4,5},{5,4},{6,7},{7,6},{8,9},{9,8},{10,11... | collective-permute-start | bytes 786440 | tf_op jit(solution)/shard_map/ppermute | solution.py:177
  107.6 12.1 %collective-permute-start.31 = (bf16[2,128,512]{2,1,0:T(8,128)(2,1)S(1)}, bf16[2,128,512]{2,1,0:T(8,128)(2,1)S(1)}, u32[]{:S(2)}, u32[]{:S(2)}) collective-permute-start(bf16[2,128,512]{2,1,0:T(8,128)(2,1)S(1)} %collective-permute-done.27.refs_2_), channel_id=1, source_target_pairs={{0,1},{1,0},{2,3},{3,2},{4,5},{5,4},{6,7},{7,6},{8,9},{9,8},{10,11... | collective-permute-start | bytes 786440 | tf_op jit(solution)/shard_map/ppermute | solution.py:177
  (16 other events, 119.5 us)

commit v2 on v1

v2 whole, which is shorter than its diff:
```python
import functools

import jax
import jax.numpy as jnp
from jax import lax
from jax.experimental import pallas as pl
from jax.experimental.pallas import tpu as pltpu
from jax.sharding import PartitionSpec as P

F32, BF16, I32 = jnp.float32, jnp.bfloat16, jnp.int32
NN = (((1,), (0,)), ((), ()))
NT = (((1,), (1,)), ((), ()))
LIMIT = 48 * 1024 * 1024


def dot(left, right, dims=NN):
    return lax.dot_general(left, right, dims, preferred_element_type=F32)


def complex_dot(lr, li, rr, ri, dims=NN):
    return dot(lr, rr, dims) - dot(li, ri, dims), dot(lr, ri, dims) + dot(li, rr, dims)


def source_of(column, modes_ref, step, modes, permuted):
    total = jnp.zeros_like(column)
    for b in range(modes):
        weight = jnp.left_shift(jnp.int32(1), modes_ref[step, b])
        total = total + jnp.where((column >> b) & 1 == 1, weight, 0)
    return jnp.where(permuted == 1, total, column)


def send_kernel(modes, meta_ref, modes_ref, leaf_ref, send_ref):
    rows, width = send_ref.shape[1:]
    y, zb, core = meta_ref[2], meta_ref[3], meta_ref[4]

    @pl.when(y == 0)
    def _():
        send_ref[...] = leaf_ref[:, pl.ds(pl.multiple_of(core * rows, rows), rows), :]

    @pl.when(y == 1)
    def _():
        column = lax.broadcasted_iota(I32, (rows, 1), 0) + core * rows
        source = source_of(column, modes_ref, meta_ref[0], modes, zb)
        picked = lax.broadcasted_iota(I32, (rows, width), 1) == source
        picked = jnp.where(picked, 1.0, 0.0).astype(BF16)
        for p in range(2):
            send_ref[p] = dot(picked, leaf_ref[p], NT).astype(BF16)


def keep_kernel(modes, meta_ref, modes_ref, leaf_ref, keep_ref):
    width = keep_ref.shape[2]
    y, zb = meta_ref[2], meta_ref[3]

    @pl.when(y == 0)
    def _():
        same = lax.broadcasted_iota(I32, (width, width), 0) == lax.broadcasted_iota(
            I32, (width, width), 1
        )
        same = jnp.where(same, 1.0, 0.0).astype(BF16)
        for p in range(2):
            keep_ref[p] = dot(same, leaf_ref[p], NT).astype(BF16)

    @pl.when(y == 1)
    def _():
        column = lax.broadcasted_iota(I32, (1, width), 1)
        source = source_of(column, modes_ref, meta_ref[1], modes, zb)
        picked = lax.broadcasted_iota(I32, (width, width), 0) == source
        picked = jnp.where(picked, 1.0, 0.0).astype(BF16)
        for p in range(2):
            keep_ref[p] = dot(leaf_ref[p], picked).astype(BF16)


def leaf_call(kernel, rows, meta, modes, leaves, which):
    width = leaves.shape[-1]
    return pl.pallas_call(
        functools.partial(kernel, modes.shape[1]),
        grid_spec=pltpu.PrefetchScalarGridSpec(
            num_scalar_prefetch=2,
            grid=(1,),
            in_specs=[
                pl.BlockSpec(
                    (None, None, 2, width, width),
                    lambda i, meta_ref, modes_ref: (0, meta_ref[which], 0, 0, 0),
                )
            ],
            out_specs=pl.BlockSpec((2, rows, width), lambda i, *_: (0, 0, 0)),
        ),
        out_shape=jax.ShapeDtypeStruct((2, rows, width), BF16),
        compiler_params=pltpu.CompilerParams(vmem_limit_bytes=LIMIT),
    )(meta, modes, leaves)


def whole(shape):
    return pl.BlockSpec(shape, lambda i, *_: (0,) * len(shape))


def call(kernel, meta, arrays, outs):
    return pl.pallas_call(
        kernel,
        grid_spec=pltpu.PrefetchScalarGridSpec(
            num_scalar_prefetch=1,
            grid=(1,),
            in_specs=[whole(a.shape) for a in arrays],
            out_specs=[whole(o.shape) for o in outs],
        ),
        out_shape=outs,
        compiler_params=pltpu.CompilerParams(vmem_limit_bytes=LIMIT),
    )(meta, *arrays)


def pair_kernel(meta_ref, left_ref, right_ref, out_ref):
    re, im = complex_dot(left_ref[0], left_ref[1], right_ref[0], right_ref[1])
    out_ref[0] = re.astype(BF16)
    out_ref[1] = im.astype(BF16)


def branch_kernel(meta_ref, own_ref, got_ref, own_sib_ref, got_sib_ref, first_ref, second_ref):
    y, zb, core = meta_ref[2], meta_ref[3], meta_ref[4]
    rows, width = own_ref.shape[1:]
    part = rows // 2
    high_here = y == zb

    def multiply(left_ref, near_ref, far_ref):
        re = im = None
        for side, ref in ((core, near_ref), (1 - core, far_ref)):
            at = pl.ds(pl.multiple_of(side * rows, rows), rows)
            r, m = complex_dot(left_ref[0, :, at], left_ref[1, :, at], ref[0], ref[1])
            re, im = (r, m) if re is None else (re + r, im + m)
        return re.astype(BF16), im.astype(BF16)

    def store(p, top, bottom):
        @pl.when(zb == 0)
        def _():
            first_ref[p] = top
            second_ref[p] = bottom

        @pl.when(zb == 1)
        def _():
            first_ref[p] = bottom
            second_ref[p] = top

    def finish(parts):
        @pl.when(y == 1)
        def _():
            for p, value in enumerate(parts):
                store(p, value[:part], value[part:])

        @pl.when(y == 0)
        def _():
            same = lax.broadcasted_iota(I32, (width, width), 0) == lax.broadcasted_iota(
                I32, (width, width), 1
            )
            same = jnp.where(same, 1.0, 0.0).astype(BF16)
            for p, value in enumerate(parts):
                turned = dot(same, value, NT).astype(BF16)
                both = jnp.concatenate([turned[:rows], turned[rows:]], 1)
                store(p, both[:part], both[part:])

    @pl.when(high_here)
    def _():
        finish(multiply(got_ref, own_ref, own_sib_ref))

    @pl.when(jnp.logical_not(high_here))
    def _():
        finish(multiply(own_ref, got_ref, got_sib_ref))


def stem_kernel(meta_ref, own_ref, sib_ref, *refs):
    pieces, (out_ref, o_ref, n1_ref, sem) = refs[:-4], refs[-4:]
    items = len(pieces) // 4
    zb, core, y = meta_ref[0], meta_ref[1], meta_ref[2]
    part, width = pieces[0].shape[1:]
    half = width // 2
    copies = []
    for m in range(items):
        step = meta_ref[3 + m]
        column = y if m % 2 == 0 else 1 - y
        for q in range(4):
            side = core if q < 2 else 1 - core
            h = zb if q % 2 == 0 else 1 - zb
            for s in range(2):
                row = jnp.where(column == 1, side, s) * half + h * part
                col = jnp.where(column == 1, s, side) * half
                copy = pltpu.make_async_copy(
                    pieces[4 * m + q].at[:, :, s * half : (s + 1) * half],
                    o_ref.at[
                        step,
                        :,
                        pl.ds(pl.multiple_of(row, part), part),
                        pl.ds(pl.multiple_of(col, half), half),
                    ],
                    sem.at[8 * m + 2 * q + s],
                )
                copy.start()
                copies.append(copy)
    for copy in copies:
        copy.wait()
    for f, ref in ((core, own_ref), (1 - core, sib_ref)):
        at = pl.ds(pl.multiple_of(f * half, half), half)
        t = complex_dot(ref[0], ref[1], o_ref[0, 0], o_ref[0, 1])
        for p in range(2):
            value = t[p].astype(BF16)
            for e in range(2):
                n1_ref[e, p, :, at] = value[:, e * half : (e + 1) * half]
    mine = pl.ds(pl.multiple_of(core * half, half), half)
    o12 = complex_dot(o_ref[1, 0], o_ref[1, 1], o_ref[2, 0, :, mine], o_ref[2, 1, :, mine])
    o12 = [v.astype(BF16) for v in o12]
    re = im = None
    for e in range(2):
        at = slice(e * half, (e + 1) * half)
        n4 = complex_dot(n1_ref[e, 0], n1_ref[e, 1], *o12)
        r, m = complex_dot(
            n4[0].astype(BF16), n4[1].astype(BF16), o_ref[3, 0, at, :], o_ref[3, 1, at, :]
        )
        re, im = (r, m) if re is None else (re + r, im + m)
    out_ref[0] = re
    out_ref[1] = im


def stem_call(meta, own, sib, items):
    shape = own.shape
    width = shape[2]
    pieces = [piece for item in items for piece in item]
    return pl.pallas_call(
        stem_kernel,
        grid_spec=pltpu.PrefetchScalarGridSpec(
            num_scalar_prefetch=1,
            grid=(1,),
            in_specs=[whole(shape)] * 2 + [pl.BlockSpec(memory_space=pl.ANY)] * len(pieces),
            out_specs=whole(shape),
            scratch_shapes=[
                pltpu.VMEM((len(items), 2, width, width), BF16),
                pltpu.VMEM((2, *shape), BF16),
                pltpu.SemaphoreType.DMA((2 * len(pieces),)),
            ],
        ),
        out_shape=jax.ShapeDtypeStruct(shape, F32),
        compiler_params=pltpu.CompilerParams(vmem_limit_bytes=LIMIT),
    )(meta, own, sib, *pieces)


def swap(value, axis, bit):
    n = lax.axis_size(axis)
    return lax.ppermute(value, axis, [(i, i ^ bit) for i in range(n)])


def other_core(value):
    return swap(value, "narrow", 1)


def tree(leaves, modes, k_keep, k_send, y, zb, core):
    width = leaves.shape[-1]
    rows = width // lax.axis_size("narrow")
    meta = jnp.stack([k_send, k_keep, y, zb, core]).astype(I32)
    send = leaf_call(send_kernel, rows, meta, modes, leaves, 0)
    keep = leaf_call(keep_kernel, width, meta, modes, leaves, 1)
    left = swap(send, "wide", 1)
    [pair] = call(pair_kernel, meta, [left, keep], [jax.ShapeDtypeStruct(left.shape, BF16)])
    got = swap(pair, "wide", 2)
    piece = jax.ShapeDtypeStruct((2, rows // 2, width), BF16)
    return call(
        branch_kernel, meta, [pair, got, other_core(pair), other_core(got)], [piece, piece]
    )


def item_of(first, second):
    return [first, second, other_core(first), other_core(second)]


def each_own_two(own_stem, sib_stem, leaves, owners, modes, y, zb, group, core):
    def steps_of(g):
        index = jnp.arange(owners.shape[0], dtype=I32)
        mine = owners == g
        low = jnp.min(jnp.where(mine, index, owners.shape[0] - 1))
        high = jnp.max(jnp.where(mine, index, 0))
        return jnp.where(y == 0, low, high), jnp.where(y == 0, high, low)

    keep, send = steps_of(group)
    far_keep, far_send = steps_of(1 - group)
    first, second = tree(leaves, modes, keep, send, y, zb, core)
    far = swap(first, "wide", 4)
    near = [item_of(first, second), item_of(swap(first, "wide", 1), swap(second, "wide", 1))]
    far_second = swap(far, "wide", 2)
    away = [item_of(far, far_second), item_of(swap(far, "wide", 1), swap(far_second, "wide", 1))]
    meta = jnp.stack([zb, core, y, keep, send, far_keep, far_send]).astype(I32)
    return stem_call(meta, own_stem, sib_stem, near + away)


def any_owners(own_stem, sib_stem, leaves, owners, modes, y, zb, group, core):
    items, order = [], []
    two = lax.axis_size("wide") == 8
    for j in range(leaves.shape[1] // 2):
        keep, send = 2 * j + y, 2 * j + 1 - y
        first, second = tree(leaves, modes, keep, send, y, zb, core)
        owned = owners[keep] == group
        if two:
            first = jnp.where(owned, first, swap(first, "wide", 4))
            second = swap(first, "wide", 2)
            cross = [swap(first, "wide", 1), swap(second, "wide", 1)]
        else:
            sums = [
                lax.psum(
                    jnp.where(owned & (zb == 0) & (y == side), v, jnp.zeros_like(v)), "wide"
                )
                for side in range(2)
                for v in (first, second)
            ]
            first, second = (jnp.where(y == 0, a, b) for a, b in zip(sums[:2], sums[2:]))
            cross = [jnp.where(y == 0, b, a) for a, b in zip(sums[:2], sums[2:])]
        items += [item_of(first, second), item_of(*cross)]
        order += [keep, send]
    meta = jnp.stack([zb if two else jnp.zeros_like(zb), core, y, *order]).astype(I32)
    return stem_call(meta, own_stem, sib_stem, items)


MODE = "cond"


def local(stem_tensor, leaves, root_devices, mode_orders):
    w = lax.axis_index("wide")
    core = lax.axis_index("narrow")
    y, zb, group = w & 1, w >> 1 & 1, w >> 2
    owners = root_devices // 4
    own_stem = stem_tensor.astype(BF16)
    given = (own_stem, other_core(own_stem), leaves, owners, mode_orders, y, zb, group, core)
    if lax.axis_size("wide") != 8 or MODE == "four":
        return any_owners(*given)
    if MODE == "two":
        return each_own_two(*given)
    return lax.cond(jnp.sum(owners) == 2, each_own_two, any_owners, *given)


def solution(mesh):
    placed = (
        P(None, ("cuts", "wide", "narrow"), None),
        P(("cuts", "wide"), None, None, None, None),
        P(),
        P(),
    )
    return jax.shard_map(
        local,
        mesh=mesh,
        in_specs=placed,
        out_specs=P(None, ("cuts", "wide", "narrow"), None),
        check_vma=False,
    )
```

time: 125 us -> 112 us (0.90)
  starting transfers between devices: 48.7 us -> 15.7 us
  waiting for transfers between devices: 34.5 us -> 63.3 us
  between operations: 5.03 us -> 0.68 us
  local copies, waits for them, and re-layouts: 6.62 us -> 3.44 us
  Pallas kernels: 26.6 us -> 24.4 us
  loops' own time: 0 us -> 1.49 us
    ppermute x33 -> x25, starting transfers between devices: 48.7 us -> 15.7 us  [swap(): return lax.ppermute(value, axis, [(i, i ^ bit) for i in range(n)])]
    ppermute x33 -> x25, waiting for transfers between devices: 34.5 us -> 63.3 us  [swap(): return lax.ppermute(value, axis, [(i, i ^ bit) for i in range(n)])]
    pallas_call x10 -> x4, Pallas kernels: 22.7 us -> 8.54 us  [call(): pl.pallas_call(kernel, grid_spec=pltpu.PrefetchScalarGridSpec(num_scalar_...]
    pallas_call x0 -> x1, Pallas kernels: none -> 9.24 us  [stem_call(): pl.pallas_call(stem_kernel, grid_spec=pltpu.PrefetchScalarGridSpec(num_sc...]
    unnamed x14 -> x6, local copies, waits for them, and re-layouts: 5.08 us -> 1.32 us
    pallas_call x4, Pallas kernels: 3.86 us -> 6.57 us  [leaf_call(): pl.pallas_call(functools.partial(kernel, modes.shape[1]), grid_spec=pltpu...]
    another operation x0 -> x1, loops' own time: none -> 1.49 us  [local(): return lax.cond(jnp.sum(owners) == 2, each_own_two, any_owners, *given)]
    cond x0 -> x6, local copies, waits for them, and re-layouts: none -> 1.28 us
  transfers between devices with their start and end apart: 33 -> 25, of which waited for: 9 -> 13; matrix products, arithmetic and copies ran while one was open for 4% -> 1% of each run, Pallas kernels for 17% -> 12%
where the time goes in v2:
time: 112 us; the launch traced here: 111 us
  waiting for transfers between devices  63.3 us (57%)
  Pallas kernels  24.4 us (22%)
  starting transfers between devices  15.7 us (14%)
  local copies, waits for them, and re-layouts  3.44 us (3%)
  other arithmetic  2.45 us (2%)
  loops' own time  1.49 us (1%)
    ppermute x25, waiting for transfers between devices, swap(): return lax.ppermute(value, axis, [(i, i ^ bit) for i in range(n)])  63.3 us
    ppermute x25, starting transfers between devices, swap(): return lax.ppermute(value, axis, [(i, i ^ bit) for i in range(n)])  15.7 us
    pallas_call x1, Pallas kernels, stem_call(): pl.pallas_call(stem_kernel, grid_spec=pltpu.PrefetchScalarGridSpec(num_sc...  9.24 us
    pallas_call x4, Pallas kernels, call(): pl.pallas_call(kernel, grid_spec=pltpu.PrefetchScalarGridSpec(num_scalar_...  8.54 us
    pallas_call x4, Pallas kernels, leaf_call(): pl.pallas_call(functools.partial(kernel, modes.shape[1]), grid_spec=pltpu...  6.57 us
  transfers between devices with their start and end apart: 25, of which 13 were waited for; matrix products, arithmetic and copies ran while one was open for 1% of the time, Pallas kernels for 12%

profile of v2, /device:TPU:0, one launch (start us, length us, event | category | flops | bytes accessed | tf_op | source)
XLA Modules:
  0.0 111.4 jit_solution(15391410791268772316)
XLA Ops:
  0.0 1.8 %convert_element_type.7 = bf16[2,512,512]{2,1,0:T(8,128)(2,1)S(1)} convert(f32[2,512,512]{2,1,0:T(8,128)} %param.6) | non-fusion elementwise | flops 524288 | bytes 3145728 | tf_op jit(solution)/shard_map/convert_element_type | solution.py:324
  4.6 105.5 %conditional.1 = (f32[2,512,512]{2,1,0:T(8,128)S(1)}) conditional(s32[]{:T(128)} %convert_element_type.6, (s32[]{:T(128)}, s32[]{:T(128)}, s32[]{:T(128)}, s32[4]{0:T(128)S(1)}, s32[]{:T(128)}, /*index=5*/s32[4,9]{1,0:T(4,128)S(1)}, bf16[1,4,2,512,512]{4,3,2,1,0:T(8,128)(2,1)}, bf16[2,512,512]{2,1,0:T(8,128)(2,1)S(1)}, ...), branch_computations={%region_1.2_spmd, %region_2.7_spmd} | conditional | flops 262155 | bytes 60294448 | solution.py:330
  5.9 1.8 %branch_0_fun.9 = bf16[2,256,512]{2,1,0:T(8,128)(2,1)S(1)} custom-call(s32[5]{0:T(128)S(1)} %stack.45.meta_ref, s32[4,9]{1,0:T(4,128)S(1)} %get-tuple-element.51.modes_ref, bf16[1,4,2,512,512]{4,3,2,1,0:T(8,128)(2,1)} %get-tuple-element.52.leaf_ref), custom_call_target="tpu_custom_call" | custom-call | tf_op jit(solution)/shard_map/cond/branch_0_fun/pallas_call | solution.py:75
  7.8 3.5 %collective-permute-start.18 = (bf16[2,256,512]{2,1,0:T(8,128)(2,1)S(1)}, bf16[2,256,512]{2,1,0:T(8,128)(2,1)S(1)}, u32[]{:S(2)}, u32[]{:S(2)}) collective-permute-start(bf16[2,256,512]{2,1,0:T(8,128)(2,1)S(1)} %branch_0_fun.9), channel_id=1, source_target_pairs={{0,2},{2,0},{4,6},{6,4},{8,10},{10,8},{12,14},{14,12},{1,3},{3,1},... | collective-permute-start | bytes 1572872 | tf_op jit(solution)/shard_map/cond/branch_0_fun/ppermute | solution.py:244
  11.3 2.1 %branch_0_fun.13 = bf16[2,256,512]{2,1,0:T(8,128)(2,1)S(1)} custom-call(s32[5]{0:T(128)S(1)} %stack.46.meta_ref, s32[4,9]{1,0:T(4,128)S(1)} %get-tuple-element.51.modes_ref, bf16[1,4,2,512,512]{4,3,2,1,0:T(8,128)(2,1)} %get-tuple-element.52.leaf_ref), custom_call_target="tpu_custom_call" | custom-call | tf_op jit(solution)/shard_map/cond/branch_0_fun/pallas_call | solution.py:75
  14.1 1.3 %branch_0_fun.10.right_ref = bf16[2,512,512]{2,1,0:T(8,128)(2,1)S(1)} custom-call(s32[5]{0:T(128)S(1)} %stack.45.meta_ref, s32[4,9]{1,0:T(4,128)S(1)} %get-tuple-element.51.modes_ref, bf16[1,4,2,512,512]{4,3,2,1,0:T(8,128)(2,1)S(1)} %copy-done), custom_call_target="tpu_custom_call" | custom-call | tf_op jit(solution)/shard_map/cond/branch_0_fun/pallas_call | solution.py:75
  15.4 8.6 %collective-permute-done.18.left_ref = bf16[2,256,512]{2,1,0:T(8,128)(2,1)S(1)} collective-permute-done((bf16[2,256,512]{2,1,0:T(8,128)(2,1)S(1)}, bf16[2,256,512]{2,1,0:T(8,128)(2,1)S(1)}, u32[]{:S(2)}, u32[]{:S(2)}) %collective-permute-start.18) | collective-permute-done | bytes 524320 | tf_op jit(solution)/shard_map/cond/branch_0_fun/ppermute | solution.py:244
  25.2 1.6 %collective-permute-start.19 = (bf16[2,256,512]{2,1,0:T(8,128)(2,1)S(1)}, bf16[2,256,512]{2,1,0:T(8,128)(2,1)S(1)}, u32[]{:S(2)}, u32[]{:S(2)}) collective-permute-start(bf16[2,256,512]{2,1,0:T(8,128)(2,1)S(1)} %branch_0_fun.11.own_ref), channel_id=1, source_target_pairs={{0,4},{2,6},{4,0},{6,2},{8,12},{10,14},{12,8},{14,10},{1,5},{3,7},... | collective-permute-start | bytes 1572872 | tf_op jit(solution)/shard_map/cond/branch_0_fun/ppermute | solution.py:244
  26.9 1.3 %branch_0_fun.14.right_ref = bf16[2,512,512]{2,1,0:T(8,128)(2,1)S(1)} custom-call(s32[5]{0:T(128)S(1)} %stack.46.meta_ref, s32[4,9]{1,0:T(4,128)S(1)} %get-tuple-element.51.modes_ref, bf16[1,4,2,512,512]{4,3,2,1,0:T(8,128)(2,1)S(1)} %copy-done), custom_call_target="tpu_custom_call" | custom-call | tf_op jit(solution)/shard_map/cond/branch_0_fun/pallas_call | solution.py:75
  28.2 6.5 %collective-permute-done.30.left_ref = bf16[2,256,512]{2,1,0:T(8,128)(2,1)S(1)} collective-permute-done((bf16[2,256,512]{2,1,0:T(8,128)(2,1)S(1)}, bf16[2,256,512]{2,1,0:T(8,128)(2,1)S(1)}, u32[]{:S(2)}, u32[]{:S(2)}) %collective-permute-start.30) | collective-permute-done | bytes 524320 | tf_op jit(solution)/shard_map/cond/branch_0_fun/ppermute | solution.py:244
  36.0 1.6 %collective-permute-start.31 = (bf16[2,256,512]{2,1,0:T(8,128)(2,1)S(1)}, bf16[2,256,512]{2,1,0:T(8,128)(2,1)S(1)}, u32[]{:S(2)}, u32[]{:S(2)}) collective-permute-start(bf16[2,256,512]{2,1,0:T(8,128)(2,1)S(1)} %branch_0_fun.15.own_ref), channel_id=1, source_target_pairs={{0,4},{2,6},{4,0},{6,2},{8,12},{10,14},{12,8},{14,10},{1,5},{3,7},... | collective-permute-start | bytes 1572872 | tf_op jit(solution)/shard_map/cond/branch_0_fun/ppermute | solution.py:244
  38.7 10.7 %collective-permute-done.31.got_ref = bf16[2,256,512]{2,1,0:T(8,128)(2,1)S(1)} collective-permute-done((bf16[2,256,512]{2,1,0:T(8,128)(2,1)S(1)}, bf16[2,256,512]{2,1,0:T(8,128)(2,1)S(1)}, u32[]{:S(2)}, u32[]{:S(2)}) %collective-permute-start.31) | collective-permute-done | bytes 524320 | tf_op jit(solution)/shard_map/cond/branch_0_fun/ppermute | solution.py:244
  49.5 2.9 %branch_0_fun.12 = (bf16[2,128,512]{2,1,0:T(8,128)(2,1)S(1)}, bf16[2,128,512]{2,1,0:T(8,128)(2,1)}) custom-call(s32[5]{0:T(128)S(1)} %stack.45.meta_ref, bf16[2,256,512]{2,1,0:T(8,128)(2,1)S(1)} %branch_0_fun.11.own_ref, bf16[2,256,512]{2,1,0:T(8,128)(2,1)S(1)} %collective-permute-done.19.got_ref, ...), custom_call_target="tpu_custom_call" | custom-call | tf_op jit(solution)/shard_map/cond/branch_0_fun/pallas_call | solution.py:98
  52.4 2.6 %collective-permute-start.22 = (bf16[2,128,512]{2,1,0:T(8,128)(2,1)S(1)}, bf16[2,128,512]{2,1,0:T(8,128)(2,1)S(1)}, u32[]{:S(2)}, u32[]{:S(2)}) collective-permute-start(bf16[2,128,512]{2,1,0:T(8,128)(2,1)S(1)} %get-tuple-element.53), channel_id=1, source_target_pairs={{0,8},{2,10},{4,12},{6,14},{8,0},{10,2},{12,4},{14,6},{1,9},{3,11}... | collective-permute-start | bytes 786440 | tf_op jit(solution)/shard_map/cond/branch_0_fun/ppermute | solution.py:244
  55.0 3.1 %branch_0_fun.16 = (bf16[2,128,512]{2,1,0:T(8,128)(2,1)S(1)}, bf16[2,128,512]{2,1,0:T(8,128)(2,1)}) custom-call(s32[5]{0:T(128)S(1)} %stack.46.meta_ref, bf16[2,256,512]{2,1,0:T(8,128)(2,1)S(1)} %branch_0_fun.15.own_ref, bf16[2,256,512]{2,1,0:T(8,128)(2,1)S(1)} %collective-permute-done.31.got_ref, ...), custom_call_target="tpu_custom_call" | custom-call | tf_op jit(solution)/shard_map/cond/branch_0_fun/pallas_call | solution.py:98
  60.2 13.4 %collective-permute-done.22 = bf16[2,128,512]{2,1,0:T(8,128)(2,1)S(1)} collective-permute-done((bf16[2,128,512]{2,1,0:T(8,128)(2,1)S(1)}, bf16[2,128,512]{2,1,0:T(8,128)(2,1)S(1)}, u32[]{:S(2)}, u32[]{:S(2)}) %collective-permute-start.22) | collective-permute-done | bytes 262176 | tf_op jit(solution)/shard_map/cond/branch_0_fun/ppermute | solution.py:244
  74.6 4.4 %collective-permute-done.34 = bf16[2,128,512]{2,1,0:T(8,128)(2,1)S(1)} collective-permute-done((bf16[2,128,512]{2,1,0:T(8,128)(2,1)S(1)}, bf16[2,128,512]{2,1,0:T(8,128)(2,1)S(1)}, u32[]{:S(2)}, u32[]{:S(2)}) %collective-permute-start.34) | collective-permute-done | bytes 262176 | tf_op jit(solution)/shard_map/cond/branch_0_fun/ppermute | solution.py:244
  81.8 2.7 %collective-permute-done.23.refs_1_ = bf16[2,128,512]{2,1,0:T(8,128)(2,1)S(1)} collective-permute-done((bf16[2,128,512]{2,1,0:T(8,128)(2,1)S(1)}, bf16[2,128,512]{2,1,0:T(8,128)(2,1)S(1)}, u32[]{:S(2)}, u32[]{:S(2)}) %collective-permute-start.23) | collective-permute-done | bytes 262176 | tf_op jit(solution)/shard_map/cond/branch_0_fun/ppermute | solution.py:244
  85.1 5.0 %collective-permute-done.35.refs_9_ = bf16[2,128,512]{2,1,0:T(8,128)(2,1)S(1)} collective-permute-done((bf16[2,128,512]{2,1,0:T(8,128)(2,1)S(1)}, bf16[2,128,512]{2,1,0:T(8,128)(2,1)S(1)}, u32[]{:S(2)}, u32[]{:S(2)}) %collective-permute-start.35) | collective-permute-done | bytes 262176 | tf_op jit(solution)/shard_map/cond/branch_0_fun/ppermute | solution.py:244
  91.2 2.6 %collective-permute-done.27.refs_5_ = bf16[2,128,512]{2,1,0:T(8,128)(2,1)S(1)} collective-permute-done((bf16[2,128,512]{2,1,0:T(8,128)(2,1)S(1)}, bf16[2,128,512]{2,1,0:T(8,128)(2,1)S(1)}, u32[]{:S(2)}, u32[]{:S(2)}) %collective-permute-start.27) | collective-permute-done | bytes 262176 | tf_op jit(solution)/shard_map/cond/branch_0_fun/ppermute | solution.py:244
  93.8 5.1 %collective-permute-done.39.refs_13_ = bf16[2,128,512]{2,1,0:T(8,128)(2,1)S(1)} collective-permute-done((bf16[2,128,512]{2,1,0:T(8,128)(2,1)S(1)}, bf16[2,128,512]{2,1,0:T(8,128)(2,1)S(1)}, u32[]{:S(2)}, u32[]{:S(2)}) %collective-permute-start.39) | collective-permute-done | bytes 262176 | tf_op jit(solution)/shard_map/cond/branch_0_fun/ppermute | solution.py:244
  99.0 1.6 %collective-permute-done.41.refs_15_ = bf16[2,128,512]{2,1,0:T(8,128)(2,1)} collective-permute-done((bf16[2,128,512]{2,1,0:T(8,128)(2,1)S(1)}, bf16[2,128,512]{2,1,0:T(8,128)(2,1)}, u32[]{:S(2)}, u32[]{:S(2)}) %collective-permute-start.41) | collective-permute-done | bytes 262176 | tf_op jit(solution)/shard_map/cond/branch_0_fun/ppermute | solution.py:244
  100.6 9.2 %branch_0_fun.17 = f32[2,512,512]{2,1,0:T(8,128)S(1)} custom-call(s32[7]{0:T(128)S(1)} %stack.44.meta_ref, bf16[2,512,512]{2,1,0:T(8,128)(2,1)} %copy-done.2, bf16[2,512,512]{2,1,0:T(8,128)(2,1)} %copy-done.4, bf16[2,128,512]{2,1,0:T(8,128)(2,1)S(1)} %broadcast_select_fusion.1.refs_0_, bf16[2,128,512]{2,1,0:T(8,128)(2,1)S(1)} %collective-permute-done.23.refs_1_, ...), custom_call_target="tpu_custom_call" | custom-call | tf_op jit(solution)/shard_map/cond/branch_0_fun/pallas_call | solution.py:224
  110.1 1.3 %copy-done.6 = f32[2,512,512]{2,1,0:T(8,128)} copy-done((f32[2,512,512]{2,1,0:T(8,128)}, f32[2,512,512]{2,1,0:T(8,128)S(1)}, u32[]{:S(2)}) %copy-start.6) | copy-done | bytes 2097176
  (56 shorter events, 14.3 us)
Async XLA Ops:
  1.8 2.8 %collective-permute-start.42 = (bf16[2,512,512]{2,1,0:T(8,128)(2,1)S(1)}, bf16[2,512,512]{2,1,0:T(8,128)(2,1)S(1)}, u32[]{:S(2)}, u32[]{:S(2)}) collective-permute-start(bf16[2,512,512]{2,1,0:T(8,128)(2,1)S(1)} %convert_element_type.7), channel_id=1, source_target_pairs={{0,1},{1,0},{2,3},{3,2},{4,5},{5,4},{6,7},{7,6},{8,9},{9,8},{10,11... | collective-permute-start | bytes 3145736 | tf_op jit(solution)/shard_map/ppermute | solution.py:244
  7.8 16.2 %collective-permute-start.18 = (bf16[2,256,512]{2,1,0:T(8,128)(2,1)S(1)}, bf16[2,256,512]{2,1,0:T(8,128)(2,1)S(1)}, u32[]{:S(2)}, u32[]{:S(2)}) collective-permute-start(bf16[2,256,512]{2,1,0:T(8,128)(2,1)S(1)} %branch_0_fun.9), channel_id=1, source_target_pairs={{0,2},{2,0},{4,6},{6,4},{8,10},{10,8},{12,14},{14,12},{1,3},{3,1},... | collective-permute-start | bytes 1572872 | tf_op jit(solution)/shard_map/cond/branch_0_fun/ppermute | solution.py:244
  13.5 21.2 %collective-permute-start.30 = (bf16[2,256,512]{2,1,0:T(8,128)(2,1)S(1)}, bf16[2,256,512]{2,1,0:T(8,128)(2,1)S(1)}, u32[]{:S(2)}, u32[]{:S(2)}) collective-permute-start(bf16[2,256,512]{2,1,0:T(8,128)(2,1)S(1)} %branch_0_fun.13), channel_id=1, source_target_pairs={{0,2},{2,0},{4,6},{6,4},{8,10},{10,8},{12,14},{14,12},{1,3},{3,1},... | collective-permute-start | bytes 1572872 | tf_op jit(solution)/shard_map/cond/branch_0_fun/ppermute | solution.py:244
  25.2 13.0 %collective-permute-start.19 = (bf16[2,256,512]{2,1,0:T(8,128)(2,1)S(1)}, bf16[2,256,512]{2,1,0:T(8,128)(2,1)S(1)}, u32[]{:S(2)}, u32[]{:S(2)}) collective-permute-start(bf16[2,256,512]{2,1,0:T(8,128)(2,1)S(1)} %branch_0_fun.11.own_ref), channel_id=1, source_target_pairs={{0,4},{2,6},{4,0},{6,2},{8,12},{10,14},{12,8},{14,10},{1,5},{3,7},... | collective-permute-start | bytes 1572872 | tf_op jit(solution)/shard_map/cond/branch_0_fun/ppermute | solution.py:244
  36.0 13.5 %collective-permute-start.31 = (bf16[2,256,512]{2,1,0:T(8,128)(2,1)S(1)}, bf16[2,256,512]{2,1,0:T(8,128)(2,1)S(1)}, u32[]{:S(2)}, u32[]{:S(2)}) collective-permute-start(bf16[2,256,512]{2,1,0:T(8,128)(2,1)S(1)} %branch_0_fun.15.own_ref), channel_id=1, source_target_pairs={{0,4},{2,6},{4,0},{6,2},{8,12},{10,14},{12,8},{14,10},{1,5},{3,7},... | collective-permute-start | bytes 1572872 | tf_op jit(solution)/shard_map/cond/branch_0_fun/ppermute | solution.py:244
  37.6 11.9 %collective-permute-start.20 = (bf16[2,256,512]{2,1,0:T(8,128)(2,1)S(1)}, bf16[2,256,512]{2,1,0:T(8,128)(2,1)S(1)}, u32[]{:S(2)}, u32[]{:S(2)}) collective-permute-start(bf16[2,256,512]{2,1,0:T(8,128)(2,1)S(1)} %branch_0_fun.11.own_ref), channel_id=1, source_target_pairs={{0,1},{1,0},{2,3},{3,2},{4,5},{5,4},{6,7},{7,6},{8,9},{9,8},{10,11... | collective-permute-start | bytes 1572872 | tf_op jit(solution)/shard_map/cond/branch_0_fun/ppermute | solution.py:244
  38.2 11.2 %collective-permute-start.21 = (bf16[2,256,512]{2,1,0:T(8,128)(2,1)S(1)}, bf16[2,256,512]{2,1,0:T(8,128)(2,1)S(1)}, u32[]{:S(2)}, u32[]{:S(2)}) collective-permute-start(bf16[2,256,512]{2,1,0:T(8,128)(2,1)S(1)} %collective-permute-done.19.got_ref), channel_id=1, source_target_pairs={{0,1},{1,0},{2,3},{3,2},{4,5},{5,4},{6,7},{7,6},{8,9},{9,8},{10,11... | collective-permute-start | bytes 1572872 | tf_op jit(solution)/shard_map/cond/branch_0_fun/ppermute | solution.py:244
  38.2 16.8 %collective-permute-start.32 = (bf16[2,256,512]{2,1,0:T(8,128)(2,1)S(1)}, bf16[2,256,512]{2,1,0:T(8,128)(2,1)S(1)}, u32[]{:S(2)}, u32[]{:S(2)}) collective-permute-start(bf16[2,256,512]{2,1,0:T(8,128)(2,1)S(1)} %branch_0_fun.15.own_ref), channel_id=1, source_target_pairs={{0,1},{1,0},{2,3},{3,2},{4,5},{5,4},{6,7},{7,6},{8,9},{9,8},{10,11... | collective-permute-start | bytes 1572872 | tf_op jit(solution)/shard_map/cond/branch_0_fun/ppermute | solution.py:244
  49.5 5.6 %collective-permute-start.33 = (bf16[2,256,512]{2,1,0:T(8,128)(2,1)S(1)}, bf16[2,256,512]{2,1,0:T(8,128)(2,1)S(1)}, u32[]{:S(2)}, u32[]{:S(2)}) collective-permute-start(bf16[2,256,512]{2,1,0:T(8,128)(2,1)S(1)} %collective-permute-done.31.got_ref), channel_id=1, source_target_pairs={{0,1},{1,0},{2,3},{3,2},{4,5},{5,4},{6,7},{7,6},{8,9},{9,8},{10,11... | collective-permute-start | bytes 1572872 | tf_op jit(solution)/shard_map/cond/branch_0_fun/ppermute | solution.py:244
  52.4 21.2 %collective-permute-start.22 = (bf16[2,128,512]{2,1,0:T(8,128)(2,1)S(1)}, bf16[2,128,512]{2,1,0:T(8,128)(2,1)S(1)}, u32[]{:S(2)}, u32[]{:S(2)}) collective-permute-start(bf16[2,128,512]{2,1,0:T(8,128)(2,1)S(1)} %get-tuple-element.53), channel_id=1, source_target_pairs={{0,8},{2,10},{4,12},{6,14},{8,0},{10,2},{12,4},{14,6},{1,9},{3,11}... | collective-permute-start | bytes 786440 | tf_op jit(solution)/shard_map/cond/branch_0_fun/ppermute | solution.py:244
  58.1 20.8 %collective-permute-start.34 = (bf16[2,128,512]{2,1,0:T(8,128)(2,1)S(1)}, bf16[2,128,512]{2,1,0:T(8,128)(2,1)S(1)}, u32[]{:S(2)}, u32[]{:S(2)}) collective-permute-start(bf16[2,128,512]{2,1,0:T(8,128)(2,1)S(1)} %get-tuple-element.54), channel_id=1, source_target_pairs={{0,8},{2,10},{4,12},{6,14},{8,0},{10,2},{12,4},{14,6},{1,9},{3,11}... | collective-permute-start | bytes 786440 | tf_op jit(solution)/shard_map/cond/branch_0_fun/ppermute | solution.py:244
  73.7 7.6 %collective-permute-start.26 = (bf16[2,128,512]{2,1,0:T(8,128)(2,1)S(1)}, bf16[2,128,512]{2,1,0:T(8,128)(2,1)S(1)}, u32[]{:S(2)}, u32[]{:S(2)}) collective-permute-start(bf16[2,128,512]{2,1,0:T(8,128)(2,1)S(1)} %broadcast_select_fusion.1.refs_0_), channel_id=1, source_target_pairs={{0,2},{2,0},{4,6},{6,4},{8,10},{10,8},{12,14},{14,12},{1,3},{3,1},... | collective-permute-start | bytes 786440 | tf_op jit(solution)/shard_map/cond/branch_0_fun/ppermute | solution.py:244
  74.3 7.0 %collective-permute-start.24 = (bf16[2,128,512]{2,1,0:T(8,128)(2,1)S(1)}, bf16[2,128,512]{2,1,0:T(8,128)(2,1)S(1)}, u32[]{:S(2)}, u32[]{:S(2)}) collective-permute-start(bf16[2,128,512]{2,1,0:T(8,128)(2,1)S(1)} %broadcast_select_fusion.1.refs_0_), channel_id=1, source_target_pairs={{0,1},{1,0},{2,3},{3,2},{4,5},{5,4},{6,7},{7,6},{8,9},{9,8},{10,11... | collective-permute-start | bytes 786440 | tf_op jit(solution)/shard_map/cond/branch_0_fun/ppermute | solution.py:244
  74.3 10.2 %collective-permute-start.23 = (bf16[2,128,512]{2,1,0:T(8,128)(2,1)S(1)}, bf16[2,128,512]{2,1,0:T(8,128)(2,1)S(1)}, u32[]{:S(2)}, u32[]{:S(2)}) collective-permute-start(bf16[2,128,512]{2,1,0:T(8,128)(2,1)S(1)} %broadcast_select_fusion.1.refs_0_), channel_id=1, source_target_pairs={{0,4},{2,6},{4,0},{6,2},{8,12},{10,14},{12,8},{14,10},{1,5},{3,7},... | collective-permute-start | bytes 786440 | tf_op jit(solution)/shard_map/cond/branch_0_fun/ppermute | solution.py:244
  79.0 11.1 %collective-permute-start.35 = (bf16[2,128,512]{2,1,0:T(8,128)(2,1)S(1)}, bf16[2,128,512]{2,1,0:T(8,128)(2,1)S(1)}, u32[]{:S(2)}, u32[]{:S(2)}) collective-permute-start(bf16[2,128,512]{2,1,0:T(8,128)(2,1)S(1)} %broadcast_select_fusion.refs_8_), channel_id=1, source_target_pairs={{0,4},{2,6},{4,0},{6,2},{8,12},{10,14},{12,8},{14,10},{1,5},{3,7},... | collective-permute-start | bytes 786440 | tf_op jit(solution)/shard_map/cond/branch_0_fun/ppermute | solution.py:244
  79.7 10.9 %collective-permute-start.38 = (bf16[2,128,512]{2,1,0:T(8,128)(2,1)S(1)}, bf16[2,128,512]{2,1,0:T(8,128)(2,1)S(1)}, u32[]{:S(2)}, u32[]{:S(2)}) collective-permute-start(bf16[2,128,512]{2,1,0:T(8,128)(2,1)S(1)} %broadcast_select_fusion.refs_8_), channel_id=1, source_target_pairs={{0,2},{2,0},{4,6},{6,4},{8,10},{10,8},{12,14},{14,12},{1,3},{3,1},... | collective-permute-start | bytes 786440 | tf_op jit(solution)/shard_map/cond/branch_0_fun/ppermute | solution.py:244
  81.3 9.4 %collective-permute-start.36 = (bf16[2,128,512]{2,1,0:T(8,128)(2,1)S(1)}, bf16[2,128,512]{2,1,0:T(8,128)(2,1)S(1)}, u32[]{:S(2)}, u32[]{:S(2)}) collective-permute-start(bf16[2,128,512]{2,1,0:T(8,128)(2,1)S(1)} %broadcast_select_fusion.refs_8_), channel_id=1, source_target_pairs={{0,1},{1,0},{2,3},{3,2},{4,5},{5,4},{6,7},{7,6},{8,9},{9,8},{10,11... | collective-permute-start | bytes 786440 | tf_op jit(solution)/shard_map/cond/branch_0_fun/ppermute | solution.py:244
  81.3 9.9 %collective-permute-start.28 = (bf16[2,128,512]{2,1,0:T(8,128)(2,1)S(1)}, bf16[2,128,512]{2,1,0:T(8,128)(2,1)S(1)}, u32[]{:S(2)}, u32[]{:S(2)}) collective-permute-start(bf16[2,128,512]{2,1,0:T(8,128)(2,1)S(1)} %collective-permute-done.26.refs_4_), channel_id=1, source_target_pairs={{0,1},{1,0},{2,3},{3,2},{4,5},{5,4},{6,7},{7,6},{8,9},{9,8},{10,11... | collective-permute-start | bytes 786440 | tf_op jit(solution)/shard_map/cond/branch_0_fun/ppermute | solution.py:244
  84.5 9.3 %collective-permute-start.27 = (bf16[2,128,512]{2,1,0:T(8,128)(2,1)S(1)}, bf16[2,128,512]{2,1,0:T(8,128)(2,1)S(1)}, u32[]{:S(2)}, u32[]{:S(2)}) collective-permute-start(bf16[2,128,512]{2,1,0:T(8,128)(2,1)S(1)} %collective-permute-done.23.refs_1_), channel_id=1, source_target_pairs={{0,2},{2,0},{4,6},{6,4},{8,10},{10,8},{12,14},{14,12},{1,3},{3,1},... | collective-permute-start | bytes 786440 | tf_op jit(solution)/shard_map/cond/branch_0_fun/ppermute | solution.py:244
  90.1 8.8 %collective-permute-start.39 = (bf16[2,128,512]{2,1,0:T(8,128)(2,1)S(1)}, bf16[2,128,512]{2,1,0:T(8,128)(2,1)S(1)}, u32[]{:S(2)}, u32[]{:S(2)}) collective-permute-start(bf16[2,128,512]{2,1,0:T(8,128)(2,1)S(1)} %collective-permute-done.35.refs_9_), channel_id=1, source_target_pairs={{0,2},{2,0},{4,6},{6,4},{8,10},{10,8},{12,14},{14,12},{1,3},{3,1},... | collective-permute-start | bytes 786440 | tf_op jit(solution)/shard_map/cond/branch_0_fun/ppermute | solution.py:244
  90.6 8.4 %collective-permute-start.25 = (bf16[2,128,512]{2,1,0:T(8,128)(2,1)S(1)}, bf16[2,128,512]{2,1,0:T(8,128)(2,1)S(1)}, u32[]{:S(2)}, u32[]{:S(2)}) collective-permute-start(bf16[2,128,512]{2,1,0:T(8,128)(2,1)S(1)} %collective-permute-done.23.refs_1_), channel_id=1, source_target_pairs={{0,1},{1,0},{2,3},{3,2},{4,5},{5,4},{6,7},{7,6},{8,9},{9,8},{10,11... | collective-permute-start | bytes 786440 | tf_op jit(solution)/shard_map/cond/branch_0_fun/ppermute | solution.py:244
  90.7 8.4 %collective-permute-start.37 = (bf16[2,128,512]{2,1,0:T(8,128)(2,1)S(1)}, bf16[2,128,512]{2,1,0:T(8,128)(2,1)S(1)}, u32[]{:S(2)}, u32[]{:S(2)}) collective-permute-start(bf16[2,128,512]{2,1,0:T(8,128)(2,1)S(1)} %collective-permute-done.35.refs_9_), channel_id=1, source_target_pairs={{0,1},{1,0},{2,3},{3,2},{4,5},{5,4},{6,7},{7,6},{8,9},{9,8},{10,11... | collective-permute-start | bytes 786440 | tf_op jit(solution)/shard_map/cond/branch_0_fun/ppermute | solution.py:244
  91.2 7.9 %collective-permute-start.40 = (bf16[2,128,512]{2,1,0:T(8,128)(2,1)S(1)}, bf16[2,128,512]{2,1,0:T(8,128)(2,1)}, u32[]{:S(2)}, u32[]{:S(2)}) collective-permute-start(bf16[2,128,512]{2,1,0:T(8,128)(2,1)S(1)} %collective-permute-done.38.refs_12_), channel_id=1, source_target_pairs={{0,1},{1,0},{2,3},{3,2},{4,5},{5,4},{6,7},{7,6},{8,9},{9,8},{10,11... | collective-permute-start | bytes 786440 | tf_op jit(solution)/shard_map/cond/branch_0_fun/ppermute | solution.py:244
  93.8 5.2 %collective-permute-start.29 = (bf16[2,128,512]{2,1,0:T(8,128)(2,1)S(1)}, bf16[2,128,512]{2,1,0:T(8,128)(2,1)}, u32[]{:S(2)}, u32[]{:S(2)}) collective-permute-start(bf16[2,128,512]{2,1,0:T(8,128)(2,1)S(1)} %collective-permute-done.27.refs_5_), channel_id=1, source_target_pairs={{0,1},{1,0},{2,3},{3,2},{4,5},{5,4},{6,7},{7,6},{8,9},{9,8},{10,11... | collective-permute-start | bytes 786440 | tf_op jit(solution)/shard_map/cond/branch_0_fun/ppermute | solution.py:244
  (7 other events, 14.9 us)

commit v3 on v2

v3 whole, which is shorter than its diff:
```python
import functools

import jax
import jax.numpy as jnp
from jax import lax
from jax.experimental import pallas as pl
from jax.experimental.pallas import tpu as pltpu
from jax.sharding import PartitionSpec as P

F32, BF16, I32 = jnp.float32, jnp.bfloat16, jnp.int32
NN = (((1,), (0,)), ((), ()))
NT = (((1,), (1,)), ((), ()))
LIMIT = 48 * 1024 * 1024
LEAF_LIMIT = 61 * 1024 * 1024
CHUNKS_TWO, CHUNKS_FOUR = 2, 1


def dot(left, right, dims=NN):
    return lax.dot_general(left, right, dims, preferred_element_type=F32)


def complex_dot(lr, li, rr, ri, dims=NN):
    return dot(lr, rr, dims) - dot(li, ri, dims), dot(lr, ri, dims) + dot(li, rr, dims)


def source_of(column, modes_ref, step, modes, permuted):
    total = jnp.zeros_like(column)
    for b in range(modes):
        weight = jnp.left_shift(jnp.int32(1), modes_ref[step, b])
        total = total + jnp.where((column >> b) & 1 == 1, weight, 0)
    return jnp.where(permuted == 1, total, column)


def place():
    w = lax.axis_index("wide")
    return w & 1, w >> 1 & 1, w >> 2, lax.axis_index("narrow")


def steps_of(plan, roots_ref, y, group):
    if plan is not None:
        low, high = (jnp.int32(k) for k in plan)
    else:
        low = high = None
        for k in range(roots_ref.shape[0]):
            mine = roots_ref[k] >> 2 == group
            high = jnp.where(mine, k, 0 if high is None else high)
        for k in reversed(range(roots_ref.shape[0])):
            mine = roots_ref[k] >> 2 == group
            low = jnp.where(mine, k, k if low is None else low)
    return jnp.where(y == 0, low, high), jnp.where(y == 0, high, low)


def send_kernel(plan, roots_ref, modes_ref, leaves_ref, *refs):
    sends, (leaf_ref, sem) = refs[:-2], refs[-2:]
    part, width = sends[0].shape[1:]
    rows = part * len(sends)
    y, zb, group, core = place()
    _, step = steps_of(plan, roots_ref, y, group)

    @pl.when(y == 0)
    def _():
        copies = []
        for i, send_ref in enumerate(sends):
            at = pl.ds(pl.multiple_of(core * rows + i * part, part), part)
            copies.append(
                pltpu.make_async_copy(leaves_ref.at[0, step, :, at], send_ref, sem.at[i])
            )
            copies[-1].start()
        for copy in copies:
            copy.wait()

    @pl.when(y == 1)
    def _():
        copy = pltpu.make_async_copy(leaves_ref.at[0, step], leaf_ref, sem.at[0])
        copy.start()
        column = lax.broadcasted_iota(I32, (rows, 1), 0) + core * rows
        source = source_of(column, modes_ref, step, modes_ref.shape[1], zb)
        picked = lax.broadcasted_iota(I32, (rows, width), 1) == source
        picked = jnp.where(picked, 1.0, 0.0).astype(BF16)
        copy.wait()
        for p in range(2):
            made = dot(picked, leaf_ref[p], NT).astype(BF16)
            for i, send_ref in enumerate(sends):
                send_ref[p] = made[i * part : (i + 1) * part]


def keep_kernel(plan, roots_ref, modes_ref, leaves_ref, keep_ref, leaf_ref, sem):
    width = keep_ref.shape[2]
    y, zb, group, core = place()
    step, _ = steps_of(plan, roots_ref, y, group)
    copy = pltpu.make_async_copy(leaves_ref.at[0, step], leaf_ref, sem.at[0])
    copy.start()
    copy.wait()

    @pl.when(y == 0)
    def _():
        same = lax.broadcasted_iota(I32, (width, width), 0) == lax.broadcasted_iota(
            I32, (width, width), 1
        )
        same = jnp.where(same, 1.0, 0.0).astype(BF16)
        for p in range(2):
            keep_ref[p] = dot(same, leaf_ref[p], NT).astype(BF16)

    @pl.when(y == 1)
    def _():
        column = lax.broadcasted_iota(I32, (1, width), 1)
        source = source_of(column, modes_ref, step, modes_ref.shape[1], zb)
        picked = lax.broadcasted_iota(I32, (width, width), 0) == source
        picked = jnp.where(picked, 1.0, 0.0).astype(BF16)
        for p in range(2):
            keep_ref[p] = dot(leaf_ref[p], picked).astype(BF16)


def leaf_call(kernel, parts, rows, plan, roots, modes, leaves):
    width = leaves.shape[-1]
    return pl.pallas_call(
        functools.partial(kernel, plan),
        grid_spec=pltpu.PrefetchScalarGridSpec(
            num_scalar_prefetch=2,
            grid=(1,),
            in_specs=[pl.BlockSpec(memory_space=pl.ANY)],
            out_specs=[whole((2, rows, width))] * parts,
            scratch_shapes=[pltpu.VMEM((2, width, width), BF16), pltpu.SemaphoreType.DMA((parts,))],
        ),
        out_shape=[jax.ShapeDtypeStruct((2, rows, width), BF16)] * parts,
        compiler_params=pltpu.CompilerParams(vmem_limit_bytes=LEAF_LIMIT),
    )(roots, modes, leaves)


def whole(shape):
    return pl.BlockSpec(shape, lambda i, *_: (0,) * len(shape))


def call(kernel, arrays, outs):
    return pl.pallas_call(
        kernel,
        grid=(1,),
        in_specs=[whole(a.shape) for a in arrays],
        out_specs=[whole(o.shape) for o in outs],
        out_shape=outs,
        compiler_params=pltpu.CompilerParams(vmem_limit_bytes=LIMIT),
    )(*arrays)


def pair_kernel(left_ref, right_ref, out_ref):
    re, im = complex_dot(left_ref[0], left_ref[1], right_ref[0], right_ref[1])
    out_ref[0] = re.astype(BF16)
    out_ref[1] = im.astype(BF16)


def branch_kernel(chunks, *refs):
    own, got, own_sib, got_sib = (refs[i * chunks : (i + 1) * chunks] for i in range(4))
    first_ref, second_ref = refs[4 * chunks : 4 * chunks + 2]
    both_ref = refs[4 * chunks + 2] if len(refs) > 4 * chunks + 2 else None
    y, zb, _, core = place()
    rows, width = own[0].shape[1] * chunks, own[0].shape[2]
    part = rows // 2
    high_here = y == zb

    def joined(group, p, at=slice(None)):
        values = [ref[p, :, at] for ref in group]
        return values[0] if len(values) == 1 else jnp.concatenate(values, 0)

    def multiply(left, near, far):
        re = im = None
        for side, right in ((core, near), (1 - core, far)):
            at = pl.ds(pl.multiple_of(side * rows, rows), rows)
            r, m = complex_dot(
                joined(left, 0, at), joined(left, 1, at), joined(right, 0), joined(right, 1)
            )
            re, im = (r, m) if re is None else (re + r, im + m)
        return re.astype(BF16), im.astype(BF16)

    def store(p, top, bottom):
        @pl.when(zb == 0)
        def _():
            first_ref[p] = top
            second_ref[p] = bottom
            if both_ref is not None:
                both_ref[0, p] = top
                both_ref[1, p] = bottom

        @pl.when(zb == 1)
        def _():
            first_ref[p] = bottom
            second_ref[p] = top
            if both_ref is not None:
                both_ref[0, p] = bottom
                both_ref[1, p] = top

    def finish(parts):
        @pl.when(y == 1)
        def _():
            for p, value in enumerate(parts):
                store(p, value[:part], value[part:])

        @pl.when(y == 0)
        def _():
            same = lax.broadcasted_iota(I32, (rows, rows), 0) == lax.broadcasted_iota(
                I32, (rows, rows), 1
            )
            same = jnp.where(same, 1.0, 0.0).astype(BF16)
            for p, value in enumerate(parts):
                turned = [dot(same, value[:, i : i + rows], NT) for i in range(0, width, rows)]
                both = jnp.concatenate(turned, 1).astype(BF16)
                store(p, both[:part], both[part:])

    @pl.when(high_here)
    def _():
        finish(multiply(got, own, own_sib))

    @pl.when(jnp.logical_not(high_here))
    def _():
        finish(multiply(own, got, got_sib))


def halves(ref, count):
    return [ref] if count == 1 else [ref.at[h] for h in range(count)]


def stem_kernel(plans, turn, layout, roots_ref, own_hbm, sib_hbm, *refs):
    pieces, (out_hbm, o_ref, n1_ref, own_ref, sib_ref, out_ref, sem) = refs[:-7], refs[-7:]
    pieces = [piece for ref, n in zip(pieces, layout) for piece in halves(ref, n)]
    items = len(pieces) // 4
    y, zb, group, core = place()
    zb = zb if turn else 0
    part, width = pieces[0].shape[1:]
    half = width // 2
    first = [
        pltpu.make_async_copy(own_hbm, own_ref, sem.at[items]),
        pltpu.make_async_copy(sib_hbm, sib_ref, sem.at[items + 1]),
    ]
    for copy in first:
        copy.start()
    for m in range(items):
        plan = plans[m // 2] if plans else None
        steps = steps_of(plan, roots_ref, y, group if m < 2 else 1 - group)
        step = steps[m % 2]
        column = y if m % 2 == 0 else 1 - y
        for q in range(4):
            side = core if q < 2 else 1 - core
            h = zb if q % 2 == 0 else 1 - zb
            for s in range(2):
                row = jnp.where(column == 1, side, s) * half + h * part
                col = jnp.where(column == 1, s, side) * half
                pltpu.make_async_copy(
                    pieces[4 * m + q].at[:, :, s * half : (s + 1) * half],
                    o_ref.at[
                        step,
                        :,
                        pl.ds(pl.multiple_of(row, part), part),
                        pl.ds(pl.multiple_of(col, half), half),
                    ],
                    sem.at[step],
                ).start()

    def arrived(step):
        pltpu.make_async_copy(o_ref.at[step], o_ref.at[step], sem.at[step]).wait()

    for copy in first:
        copy.wait()
    arrived(0)
    for f, ref in ((core, own_ref), (1 - core, sib_ref)):
        at = pl.ds(pl.multiple_of(f * half, half), half)
        t = complex_dot(ref[0], ref[1], o_ref[0, 0], o_ref[0, 1])
        for p in range(2):
            value = t[p].astype(BF16)
            for e in range(2):
                n1_ref[e, p, :, at] = value[:, e * half : (e + 1) * half]
    mine = pl.ds(pl.multiple_of(core * half, half), half)
    arrived(1)
    arrived(2)
    o12 = complex_dot(o_ref[1, 0], o_ref[1, 1], o_ref[2, 0, :, mine], o_ref[2, 1, :, mine])
    o12 = [v.astype(BF16) for v in o12]
    arrived(3)
    rows = own_ref.shape[1]
    copies = []
    for r in range(2):
        band = slice(r * rows // 2, (r + 1) * rows // 2)
        n4 = [complex_dot(n1_ref[e, 0, band], n1_ref[e, 1, band], *o12) for e in range(2)]
        n4 = [jnp.concatenate([n4[0][p], n4[1][p]], 1).astype(BF16) for p in range(2)]
        made = complex_dot(*n4, o_ref[3, 0], o_ref[3, 1])
        for p in range(2):
            out_ref[p, band] = made[p]
        copy = pltpu.make_async_copy(
            out_ref.at[:, band], out_hbm.at[:, band], sem.at[items + 2 + r]
        )
        copy.start()
        copies.append(copy)
    for copy in copies:
        copy.wait()


def stem_call(plans, turn, roots, own, sib, items):
    shape = own.shape
    width = shape[2]
    pieces = [piece for item in items for piece in item]
    layout = tuple(piece.ndim == 4 and piece.shape[0] or 1 for piece in pieces)
    anywhere = pl.BlockSpec(memory_space=pl.ANY)
    return pl.pallas_call(
        functools.partial(stem_kernel, plans, turn, layout),
        grid_spec=pltpu.PrefetchScalarGridSpec(
            num_scalar_prefetch=1,
            grid=(1,),
            in_specs=[anywhere] * (2 + len(pieces)),
            out_specs=anywhere,
            scratch_shapes=[
                pltpu.VMEM((len(items), 2, width, width), BF16),
                pltpu.VMEM((2, *shape), BF16),
                pltpu.VMEM(shape, BF16),
                pltpu.VMEM(shape, BF16),
                pltpu.VMEM(shape, F32),
                pltpu.SemaphoreType.DMA((len(items) + 4,)),
            ],
        ),
        out_shape=jax.ShapeDtypeStruct(shape, F32),
        compiler_params=pltpu.CompilerParams(vmem_limit_bytes=LIMIT),
    )(roots, own, sib, *pieces)


def swap(value, axis, bit):
    n = lax.axis_size(axis)
    return lax.ppermute(value, axis, [(i, i ^ bit) for i in range(n)])


def other_core(value):
    return swap(value, "narrow", 1)


def tree(leaves, roots, modes, plan, chunks, joint):
    width = leaves.shape[-1]
    rows = width // lax.axis_size("narrow")
    sends = leaf_call(send_kernel, chunks, rows // chunks, plan, roots, modes, leaves)
    [keep] = leaf_call(keep_kernel, 1, width, plan, roots, modes, leaves)
    lefts = [swap(send, "wide", 1) for send in sends]
    pairs = [
        call(pair_kernel, [left, keep], [jax.ShapeDtypeStruct(left.shape, BF16)])[0]
        for left in lefts
    ]
    gots = [swap(pair, "wide", 2) for pair in pairs]
    sibs = [other_core(v) for v in pairs + gots]
    piece = jax.ShapeDtypeStruct((2, rows // 2, width), BF16)
    outs = [piece, piece]
    if joint:
        outs.append(jax.ShapeDtypeStruct((2, *piece.shape), BF16))
    return call(functools.partial(branch_kernel, chunks), pairs + gots + sibs, outs)


def item_of(first, second):
    return [first, second, other_core(first), other_core(second)]


def each_own_two(stem, leaves, roots, modes):
    own = stem.astype(BF16)
    sib = other_core(own)
    first, _, both = tree(leaves, roots, modes, None, CHUNKS_TWO, True)
    far = swap(first, "wide", 4)
    cross = swap(both, "wide", 1)
    near = [[both, other_core(both)], [cross, other_core(cross)]]
    far_second = swap(far, "wide", 2)
    away = [item_of(far, far_second), item_of(swap(far, "wide", 1), swap(far_second, "wide", 1))]
    return stem_call(None, True, roots, own, sib, near + away)


def any_owners(stem, leaves, roots, modes):
    y, zb, group, _ = place()
    own = stem.astype(BF16)
    sib = other_core(own)
    two = lax.axis_size("wide") == 8
    items, plans = [], []
    for j in range(leaves.shape[1] // 2):
        plan = (2 * j, 2 * j + 1)
        first, second = tree(leaves, roots, modes, plan, CHUNKS_FOUR, False)
        owned = roots[2 * j + y] // 4 == group
        if two:
            here = jnp.where(owned, first, swap(first, "wide", 4))
            second = swap(here, "wide", 2)
            cross = [swap(here, "wide", 1), swap(second, "wide", 1)]
        else:
            sums = [
                lax.psum(
                    jnp.where(owned & (zb == 0) & (y == side), v, jnp.zeros_like(v)), "wide"
                )
                for side in range(2)
                for v in (first, second)
            ]
            here, second = (jnp.where(y == 0, a, b) for a, b in zip(sums[:2], sums[2:]))
            cross = [jnp.where(y == 0, b, a) for a, b in zip(sums[:2], sums[2:])]
        items += [item_of(here, second), item_of(*cross)]
        plans.append(plan)
    return stem_call(tuple(plans), two, roots, own, sib, items)


MODE = "cond"


def local(stem_tensor, leaves, root_devices, mode_orders):
    given = (stem_tensor, leaves, root_devices, mode_orders)
    if lax.axis_size("wide") != 8 or MODE == "four":
        return any_owners(*given)
    if MODE == "two":
        return each_own_two(*given)
    return lax.cond(jnp.sum(root_devices // 4) == 2, each_own_two, any_owners, *given)


def solution(mesh):
    placed = (
        P(None, ("cuts", "wide", "narrow"), None),
        P(("cuts", "wide"), None, None, None, None),
        P(),
        P(),
    )
    return jax.shard_map(
        local,
        mesh=mesh,
        in_specs=placed,
        out_specs=P(None, ("cuts", "wide", "narrow"), None),
        check_vma=False,
    )
```

time: 112 us -> 107 us (0.955)
  waiting for transfers between devices: 63.3 us -> 51.9 us
  loops' own time: 1.49 us -> 5.19 us
  Pallas kernels: 24.4 us -> 26.6 us
  starting transfers between devices: 15.7 us -> 17.3 us
    ppermute x25, waiting for transfers between devices: 63.3 us -> 51.9 us  [swap(): return lax.ppermute(value, axis, [(i, i ^ bit) for i in range(n)])]
    another operation x1, loops' own time: 1.49 us -> 5.19 us  [local(): lax.cond(jnp.sum(root_devices // 4) == 2, each_own_two, any_owners, *given)]
    pallas_call x9, Pallas kernels: 24.4 us -> 26.6 us  [the longest x4 12.2 us: leaf_call(): pl.pallas_call(functools.partial(kernel, plan), grid_spec=pltpu.PrefetchS...]
    ppermute x25, starting transfers between devices: 15.7 us -> 17.3 us  [swap(): return lax.ppermute(value, axis, [(i, i ^ bit) for i in range(n)])]
    convert_element_type x1, other arithmetic: 1.75 us -> 0.13 us  [any_owners(): own = stem.astype(BF16)]
    unnamed x6 -> x0, local copies, waits for them, and re-layouts: 1.32 us -> none
    cond x6 -> x12, local copies, waits for them, and re-layouts: 1.28 us -> 2.47 us
  transfers between devices with their start and end apart: 25 -> 25, of which waited for: 13 -> 12; matrix products, arithmetic and copies ran while one was open for 1% -> 1% of each run, Pallas kernels for 12% -> 14%
where the time goes in v3:
time: 107 us; the launch traced here: 106 us
  waiting for transfers between devices  51.9 us (49%)
  Pallas kernels  26.6 us (25%)
  starting transfers between devices  17.3 us (16%)
  loops' own time  5.19 us (5%)
  local copies, waits for them, and re-layouts  3.05 us (3%)
  other arithmetic  1.49 us (1%)
    ppermute x25, waiting for transfers between devices, swap(): return lax.ppermute(value, axis, [(i, i ^ bit) for i in range(n)])  51.9 us
    ppermute x25, starting transfers between devices, swap(): return lax.ppermute(value, axis, [(i, i ^ bit) for i in range(n)])  17.3 us
    pallas_call x4, Pallas kernels, leaf_call(): pl.pallas_call(functools.partial(kernel, plan), grid_spec=pltpu.PrefetchS...  12.2 us
    pallas_call x1, Pallas kernels, stem_call(): pl.pallas_call(functools.partial(stem_kernel, plans, turn, layout), grid_...  8.81 us
    pallas_call x4, Pallas kernels, call(): pl.pallas_call(kernel, grid=(1,), in_specs=[whole(a.shape) for a in array...  5.6 us
    another operation x1, loops' own time, local(): lax.cond(jnp.sum(root_devices // 4) == 2, each_own_two, any_owners, *given)  5.19 us
    cond x12, local copies, waits for them, and re-layouts  2.47 us
  transfers between devices with their start and end apart: 25, of which 12 were waited for; matrix products, arithmetic and copies ran while one was open for 1% of the time, Pallas kernels for 14%

profile of v3, /device:TPU:0, one launch (start us, length us, event | category | flops | bytes accessed | tf_op | source)
XLA Modules:
  0.0 106.3 jit_solution(5032559549722139479)
XLA Ops:
  0.0 1.3 %fusion = s32[]{:T(128)} fusion(s32[4]{0:T(128)} %param.8), kind=kLoop, calls=%fused_computation.6 | loop fusion | flops 63 | bytes 20 | tf_op jit(solution)/shard_map/reduce_sum | solution.py:403
  2.0 104.2 %conditional.1 = (f32[2,512,512]{2,1,0:T(8,128)}) conditional(s32[]{:T(128)} %convert_element_type.9, (f32[2,512,512]{2,1,0:T(8,128)}, s32[4]{0:T(128)}, s32[4,9]{1,0:T(4,128)}, bf16[1,4,2,512,512]{4,3,2,1,0:T(8,128)(2,1)}) %tuple.11, (f32[2,512,512]{2,1,0:T(8,128)}, s32[4]{0:T(128)}, s32[4,9]{1,0:T(4,128)}, ...), branch_computations={%region_1.2_spmd, %region_2.3_spmd} | conditional | flops 786476 | bytes 63441124 | solution.py:403
  2.0 2.7 %branch_0_fun.13 = bf16[2,256,512]{2,1,0:T(8,128)(2,1)} custom-call(s32[4]{0:T(128)} %get-tuple-element.24.roots_ref, s32[4,9]{1,0:T(4,128)} %get-tuple-element.26.modes_ref, bf16[1,4,2,512,512]{4,3,2,1,0:T(8,128)(2,1)} %get-tuple-element.27.leaves_ref), custom_call_target="tpu_custom_call" | custom-call | tf_op jit(solution)/shard_map/cond/branch_0_fun/pallas_call | solution.py:116
  4.7 3.7 %collective-permute-start.33 = (bf16[2,256,512]{2,1,0:T(8,128)(2,1)}, bf16[2,256,512]{2,1,0:T(8,128)(2,1)S(1)}, u32[]{:S(2)}, u32[]{:S(2)}) collective-permute-start(bf16[2,256,512]{2,1,0:T(8,128)(2,1)} %branch_0_fun.13), channel_id=1, source_target_pairs={{0,2},{2,0},{4,6},{6,4},{8,10},{10,8},{12,14},{14,12},{1,3},{3,1},... | collective-permute-start | bytes 1572872 | tf_op jit(solution)/shard_map/cond/branch_0_fun/ppermute | solution.py:323
  8.4 2.4 %branch_0_fun.9 = bf16[2,256,512]{2,1,0:T(8,128)(2,1)} custom-call(s32[4]{0:T(128)S(1)} %copy-done.9, s32[4,9]{1,0:T(4,128)S(1)} %copy-done.7, bf16[1,4,2,512,512]{4,3,2,1,0:T(8,128)(2,1)} %get-tuple-element.27.leaves_ref), custom_call_target="tpu_custom_call" | custom-call | tf_op jit(solution)/shard_map/cond/branch_0_fun/pallas_call | solution.py:116
  11.6 3.5 %branch_0_fun.14.right_ref = bf16[2,512,512]{2,1,0:T(8,128)(2,1)} custom-call(s32[4]{0:T(128)S(1)} %copy-done.9, s32[4,9]{1,0:T(4,128)S(1)} %copy-done.7, bf16[1,4,2,512,512]{4,3,2,1,0:T(8,128)(2,1)} %get-tuple-element.27.leaves_ref), custom_call_target="tpu_custom_call" | custom-call | tf_op jit(solution)/shard_map/cond/branch_0_fun/pallas_call | solution.py:116
  15.1 6.2 %collective-permute-done.33.left_ref = bf16[2,256,512]{2,1,0:T(8,128)(2,1)S(1)} collective-permute-done((bf16[2,256,512]{2,1,0:T(8,128)(2,1)}, bf16[2,256,512]{2,1,0:T(8,128)(2,1)S(1)}, u32[]{:S(2)}, u32[]{:S(2)}) %collective-permute-start.33) | collective-permute-done | bytes 524320 | tf_op jit(solution)/shard_map/cond/branch_0_fun/ppermute | solution.py:323
  21.3 1.2 %copy-done.1 = bf16[2,512,512]{2,1,0:T(8,128)(2,1)S(1)} copy-done((bf16[2,512,512]{2,1,0:T(8,128)(2,1)S(1)}, bf16[2,512,512]{2,1,0:T(8,128)(2,1)}, u32[]{:S(2)}) %copy-start.1) | copy-done | bytes 1048600 | tf_op jit(solution)/shard_map/cond
  23.3 1.6 %collective-permute-start.34 = (bf16[2,256,512]{2,1,0:T(8,128)(2,1)S(1)}, bf16[2,256,512]{2,1,0:T(8,128)(2,1)S(1)}, u32[]{:S(2)}, u32[]{:S(2)}) collective-permute-start(bf16[2,256,512]{2,1,0:T(8,128)(2,1)S(1)} %branch_0_fun.15.refs_0_), channel_id=1, source_target_pairs={{0,4},{2,6},{4,0},{6,2},{8,12},{10,14},{12,8},{14,10},{1,5},{3,7},... | collective-permute-start | bytes 1572872 | tf_op jit(solution)/shard_map/cond/branch_0_fun/ppermute | solution.py:323
  24.9 3.5 %branch_0_fun.10.right_ref = bf16[2,512,512]{2,1,0:T(8,128)(2,1)} custom-call(s32[4]{0:T(128)S(1)} %copy-done.9, s32[4,9]{1,0:T(4,128)S(1)} %copy-done.7, bf16[1,4,2,512,512]{4,3,2,1,0:T(8,128)(2,1)} %get-tuple-element.27.leaves_ref), custom_call_target="tpu_custom_call" | custom-call | tf_op jit(solution)/shard_map/cond/branch_0_fun/pallas_call | solution.py:116
  28.4 3.3 %collective-permute-done.21.left_ref = bf16[2,256,512]{2,1,0:T(8,128)(2,1)S(1)} collective-permute-done((bf16[2,256,512]{2,1,0:T(8,128)(2,1)}, bf16[2,256,512]{2,1,0:T(8,128)(2,1)S(1)}, u32[]{:S(2)}, u32[]{:S(2)}) %collective-permute-start.21) | collective-permute-done | bytes 524320 | tf_op jit(solution)/shard_map/cond/branch_0_fun/ppermute | solution.py:323
  33.7 1.6 %collective-permute-start.22 = (bf16[2,256,512]{2,1,0:T(8,128)(2,1)S(1)}, bf16[2,256,512]{2,1,0:T(8,128)(2,1)S(1)}, u32[]{:S(2)}, u32[]{:S(2)}) collective-permute-start(bf16[2,256,512]{2,1,0:T(8,128)(2,1)S(1)} %branch_0_fun.11.refs_0_), channel_id=1, source_target_pairs={{0,4},{2,6},{4,0},{6,2},{8,12},{10,14},{12,8},{14,10},{1,5},{3,7},... | collective-permute-start | bytes 1572872 | tf_op jit(solution)/shard_map/cond/branch_0_fun/ppermute | solution.py:323
  36.1 10.7 %collective-permute-done.22.refs_1_ = bf16[2,256,512]{2,1,0:T(8,128)(2,1)S(1)} collective-permute-done((bf16[2,256,512]{2,1,0:T(8,128)(2,1)S(1)}, bf16[2,256,512]{2,1,0:T(8,128)(2,1)S(1)}, u32[]{:S(2)}, u32[]{:S(2)}) %collective-permute-start.22) | collective-permute-done | bytes 524320 | tf_op jit(solution)/shard_map/cond/branch_0_fun/ppermute | solution.py:323
  47.6 2.0 %branch_0_fun.16 = (bf16[2,128,512]{2,1,0:T(8,128)(2,1)S(1)}, bf16[2,128,512]{2,1,0:T(8,128)(2,1)}) custom-call(bf16[2,256,512]{2,1,0:T(8,128)(2,1)S(1)} %branch_0_fun.15.refs_0_, bf16[2,256,512]{2,1,0:T(8,128)(2,1)S(1)} %collective-permute-done.34.refs_1_, bf16[2,256,512]{2,1,0:T(8,128)(2,1)S(1)} %collective-permute-done.35.refs_2_, ...), custom_call_target="tpu_custom_call" | custom-call | tf_op jit(solution)/shard_map/cond/branch_0_fun/pallas_call | solution.py:135
  49.6 2.6 %collective-permute-start.37 = (bf16[2,128,512]{2,1,0:T(8,128)(2,1)S(1)}, bf16[2,128,512]{2,1,0:T(8,128)(2,1)S(1)}, u32[]{:S(2)}, u32[]{:S(2)}) collective-permute-start(bf16[2,128,512]{2,1,0:T(8,128)(2,1)S(1)} %get-tuple-element.29), channel_id=1, source_target_pairs={{0,8},{2,10},{4,12},{6,14},{8,0},{10,2},{12,4},{14,6},{1,9},{3,11}... | collective-permute-start | bytes 786440 | tf_op jit(solution)/shard_map/cond/branch_0_fun/ppermute | solution.py:323
  52.2 2.2 %branch_0_fun.12 = (bf16[2,128,512]{2,1,0:T(8,128)(2,1)S(1)}, bf16[2,128,512]{2,1,0:T(8,128)(2,1)}) custom-call(bf16[2,256,512]{2,1,0:T(8,128)(2,1)S(1)} %branch_0_fun.11.refs_0_, bf16[2,256,512]{2,1,0:T(8,128)(2,1)S(1)} %collective-permute-done.22.refs_1_, bf16[2,256,512]{2,1,0:T(8,128)(2,1)S(1)} %collective-permute-done.23.refs_2_, ...), custom_call_target="tpu_custom_call" | custom-call | tf_op jit(solution)/shard_map/cond/branch_0_fun/pallas_call | solution.py:135
  60.1 10.8 %collective-permute-done.37 = bf16[2,128,512]{2,1,0:T(8,128)(2,1)S(1)} collective-permute-done((bf16[2,128,512]{2,1,0:T(8,128)(2,1)S(1)}, bf16[2,128,512]{2,1,0:T(8,128)(2,1)S(1)}, u32[]{:S(2)}, u32[]{:S(2)}) %collective-permute-start.37) | collective-permute-done | bytes 262176 | tf_op jit(solution)/shard_map/cond/branch_0_fun/ppermute | solution.py:323
  71.9 3.7 %collective-permute-done.25 = bf16[2,128,512]{2,1,0:T(8,128)(2,1)S(1)} collective-permute-done((bf16[2,128,512]{2,1,0:T(8,128)(2,1)S(1)}, bf16[2,128,512]{2,1,0:T(8,128)(2,1)S(1)}, u32[]{:S(2)}, u32[]{:S(2)}) %collective-permute-start.25) | collective-permute-done | bytes 262176 | tf_op jit(solution)/shard_map/cond/branch_0_fun/ppermute | solution.py:323
  78.0 3.3 %collective-permute-done.38.refs_9_ = bf16[2,128,512]{2,1,0:T(8,128)(2,1)S(1)} collective-permute-done((bf16[2,128,512]{2,1,0:T(8,128)(2,1)S(1)}, bf16[2,128,512]{2,1,0:T(8,128)(2,1)S(1)}, u32[]{:S(2)}, u32[]{:S(2)}) %collective-permute-start.38) | collective-permute-done | bytes 262176 | tf_op jit(solution)/shard_map/cond/branch_0_fun/ppermute | solution.py:323
  82.2 4.6 %collective-permute-done.26.refs_1_ = bf16[2,128,512]{2,1,0:T(8,128)(2,1)S(1)} collective-permute-done((bf16[2,128,512]{2,1,0:T(8,128)(2,1)S(1)}, bf16[2,128,512]{2,1,0:T(8,128)(2,1)S(1)}, u32[]{:S(2)}, u32[]{:S(2)}) %collective-permute-start.26) | collective-permute-done | bytes 262176 | tf_op jit(solution)/shard_map/cond/branch_0_fun/ppermute | solution.py:323
  88.3 2.0 %collective-permute-done.42.refs_13_ = bf16[2,128,512]{2,1,0:T(8,128)(2,1)S(1)} collective-permute-done((bf16[2,128,512]{2,1,0:T(8,128)(2,1)S(1)}, bf16[2,128,512]{2,1,0:T(8,128)(2,1)S(1)}, u32[]{:S(2)}, u32[]{:S(2)}) %collective-permute-start.42) | collective-permute-done | bytes 262176 | tf_op jit(solution)/shard_map/cond/branch_0_fun/ppermute | solution.py:323
  90.3 5.2 %collective-permute-done.30.refs_5_ = bf16[2,128,512]{2,1,0:T(8,128)(2,1)S(1)} collective-permute-done((bf16[2,128,512]{2,1,0:T(8,128)(2,1)S(1)}, bf16[2,128,512]{2,1,0:T(8,128)(2,1)S(1)}, u32[]{:S(2)}, u32[]{:S(2)}) %collective-permute-start.30) | collective-permute-done | bytes 262176 | tf_op jit(solution)/shard_map/cond/branch_0_fun/ppermute | solution.py:323
  95.6 1.5 %collective-permute-done.32.refs_7_ = bf16[2,128,512]{2,1,0:T(8,128)(2,1)S(1)} collective-permute-done((bf16[2,128,512]{2,1,0:T(8,128)(2,1)S(1)}, bf16[2,128,512]{2,1,0:T(8,128)(2,1)S(1)}, u32[]{:S(2)}, u32[]{:S(2)}) %collective-permute-start.32) | collective-permute-done | bytes 262176 | tf_op jit(solution)/shard_map/cond/branch_0_fun/ppermute | solution.py:323
  97.1 8.8 %branch_0_fun.17 = f32[2,512,512]{2,1,0:T(8,128)} custom-call(s32[4]{0:T(128)S(1)} %copy-done.9, bf16[2,512,512]{2,1,0:T(8,128)(2,1)S(1)} %convert_element_type.6.own_hbm, bf16[2,512,512]{2,1,0:T(8,128)(2,1)} %copy-done.5, bf16[2,128,512]{2,1,0:T(8,128)(2,1)S(1)} %broadcast_select_fusion.1.refs_0_, bf16[2,128,512]{2,1,0:T(8,128)(2,1)S(1)} %collective-permute-done.26.refs_1_, ...), custom_call_target="tpu_custom_call" | custom-call | tf_op jit(solution)/shard_map/cond/branch_0_fun/pallas_call | solution.py:300
  (53 shorter events, 11.6 us)
Async XLA Ops:
  4.7 16.7 %collective-permute-start.33 = (bf16[2,256,512]{2,1,0:T(8,128)(2,1)}, bf16[2,256,512]{2,1,0:T(8,128)(2,1)S(1)}, u32[]{:S(2)}, u32[]{:S(2)}) collective-permute-start(bf16[2,256,512]{2,1,0:T(8,128)(2,1)} %branch_0_fun.13), channel_id=1, source_target_pairs={{0,2},{2,0},{4,6},{6,4},{8,10},{10,8},{12,14},{14,12},{1,3},{3,1},... | collective-permute-start | bytes 1572872 | tf_op jit(solution)/shard_map/cond/branch_0_fun/ppermute | solution.py:323
  10.8 20.9 %collective-permute-start.21 = (bf16[2,256,512]{2,1,0:T(8,128)(2,1)}, bf16[2,256,512]{2,1,0:T(8,128)(2,1)S(1)}, u32[]{:S(2)}, u32[]{:S(2)}) collective-permute-start(bf16[2,256,512]{2,1,0:T(8,128)(2,1)} %branch_0_fun.9), channel_id=1, source_target_pairs={{0,2},{2,0},{4,6},{6,4},{8,10},{10,8},{12,14},{14,12},{1,3},{3,1},... | collective-permute-start | bytes 1572872 | tf_op jit(solution)/shard_map/cond/branch_0_fun/ppermute | solution.py:323
  23.3 12.3 %collective-permute-start.34 = (bf16[2,256,512]{2,1,0:T(8,128)(2,1)S(1)}, bf16[2,256,512]{2,1,0:T(8,128)(2,1)S(1)}, u32[]{:S(2)}, u32[]{:S(2)}) collective-permute-start(bf16[2,256,512]{2,1,0:T(8,128)(2,1)S(1)} %branch_0_fun.15.refs_0_), channel_id=1, source_target_pairs={{0,4},{2,6},{4,0},{6,2},{8,12},{10,14},{12,8},{14,10},{1,5},{3,7},... | collective-permute-start | bytes 1572872 | tf_op jit(solution)/shard_map/cond/branch_0_fun/ppermute | solution.py:323
  33.7 13.2 %collective-permute-start.22 = (bf16[2,256,512]{2,1,0:T(8,128)(2,1)S(1)}, bf16[2,256,512]{2,1,0:T(8,128)(2,1)S(1)}, u32[]{:S(2)}, u32[]{:S(2)}) collective-permute-start(bf16[2,256,512]{2,1,0:T(8,128)(2,1)S(1)} %branch_0_fun.11.refs_0_), channel_id=1, source_target_pairs={{0,4},{2,6},{4,0},{6,2},{8,12},{10,14},{12,8},{14,10},{1,5},{3,7},... | collective-permute-start | bytes 1572872 | tf_op jit(solution)/shard_map/cond/branch_0_fun/ppermute | solution.py:323
  35.3 12.2 %collective-permute-start.35 = (bf16[2,256,512]{2,1,0:T(8,128)(2,1)S(1)}, bf16[2,256,512]{2,1,0:T(8,128)(2,1)S(1)}, u32[]{:S(2)}, u32[]{:S(2)}) collective-permute-start(bf16[2,256,512]{2,1,0:T(8,128)(2,1)S(1)} %branch_0_fun.15.refs_0_), channel_id=1, source_target_pairs={{0,1},{1,0},{2,3},{3,2},{4,5},{5,4},{6,7},{7,6},{8,9},{9,8},{10,11... | collective-permute-start | bytes 1572872 | tf_op jit(solution)/shard_map/cond/branch_0_fun/ppermute | solution.py:323
  35.6 12.0 %collective-permute-start.36 = (bf16[2,256,512]{2,1,0:T(8,128)(2,1)S(1)}, bf16[2,256,512]{2,1,0:T(8,128)(2,1)S(1)}, u32[]{:S(2)}, u32[]{:S(2)}) collective-permute-start(bf16[2,256,512]{2,1,0:T(8,128)(2,1)S(1)} %collective-permute-done.34.refs_1_), channel_id=1, source_target_pairs={{0,1},{1,0},{2,3},{3,2},{4,5},{5,4},{6,7},{7,6},{8,9},{9,8},{10,11... | collective-permute-start | bytes 1572872 | tf_op jit(solution)/shard_map/cond/branch_0_fun/ppermute | solution.py:323
  35.8 16.3 %collective-permute-start.23 = (bf16[2,256,512]{2,1,0:T(8,128)(2,1)S(1)}, bf16[2,256,512]{2,1,0:T(8,128)(2,1)S(1)}, u32[]{:S(2)}, u32[]{:S(2)}) collective-permute-start(bf16[2,256,512]{2,1,0:T(8,128)(2,1)S(1)} %branch_0_fun.11.refs_0_), channel_id=1, source_target_pairs={{0,1},{1,0},{2,3},{3,2},{4,5},{5,4},{6,7},{7,6},{8,9},{9,8},{10,11... | collective-permute-start | bytes 1572872 | tf_op jit(solution)/shard_map/cond/branch_0_fun/ppermute | solution.py:323
  46.8 5.3 %collective-permute-start.24 = (bf16[2,256,512]{2,1,0:T(8,128)(2,1)S(1)}, bf16[2,256,512]{2,1,0:T(8,128)(2,1)S(1)}, u32[]{:S(2)}, u32[]{:S(2)}) collective-permute-start(bf16[2,256,512]{2,1,0:T(8,128)(2,1)S(1)} %collective-permute-done.22.refs_1_), channel_id=1, source_target_pairs={{0,1},{1,0},{2,3},{3,2},{4,5},{5,4},{6,7},{7,6},{8,9},{9,8},{10,11... | collective-permute-start | bytes 1572872 | tf_op jit(solution)/shard_map/cond/branch_0_fun/ppermute | solution.py:323
  47.0 29.4 %collective-permute-start.20 = (bf16[2,512,512]{2,1,0:T(8,128)(2,1)S(1)}, bf16[2,512,512]{2,1,0:T(8,128)(2,1)S(1)}, u32[]{:S(2)}, u32[]{:S(2)}) collective-permute-start(bf16[2,512,512]{2,1,0:T(8,128)(2,1)S(1)} %convert_element_type.6.own_hbm), channel_id=1, source_target_pairs={{0,1},{1,0},{2,3},{3,2},{4,5},{5,4},{6,7},{7,6},{8,9},{9,8},{10,11... | collective-permute-start | bytes 3145736 | tf_op jit(solution)/shard_map/cond/branch_0_fun/ppermute | solution.py:323
  49.6 21.3 %collective-permute-start.37 = (bf16[2,128,512]{2,1,0:T(8,128)(2,1)S(1)}, bf16[2,128,512]{2,1,0:T(8,128)(2,1)S(1)}, u32[]{:S(2)}, u32[]{:S(2)}) collective-permute-start(bf16[2,128,512]{2,1,0:T(8,128)(2,1)S(1)} %get-tuple-element.29), channel_id=1, source_target_pairs={{0,8},{2,10},{4,12},{6,14},{8,0},{10,2},{12,4},{14,6},{1,9},{3,11}... | collective-permute-start | bytes 786440 | tf_op jit(solution)/shard_map/cond/branch_0_fun/ppermute | solution.py:323
  54.4 21.3 %collective-permute-start.25 = (bf16[2,128,512]{2,1,0:T(8,128)(2,1)S(1)}, bf16[2,128,512]{2,1,0:T(8,128)(2,1)S(1)}, u32[]{:S(2)}, u32[]{:S(2)}) collective-permute-start(bf16[2,128,512]{2,1,0:T(8,128)(2,1)S(1)} %get-tuple-element.28), channel_id=1, source_target_pairs={{0,8},{2,10},{4,12},{6,14},{8,0},{10,2},{12,4},{14,6},{1,9},{3,11}... | collective-permute-start | bytes 786440 | tf_op jit(solution)/shard_map/cond/branch_0_fun/ppermute | solution.py:323
  70.9 6.5 %collective-permute-start.41 = (bf16[2,128,512]{2,1,0:T(8,128)(2,1)S(1)}, bf16[2,128,512]{2,1,0:T(8,128)(2,1)S(1)}, u32[]{:S(2)}, u32[]{:S(2)}) collective-permute-start(bf16[2,128,512]{2,1,0:T(8,128)(2,1)S(1)} %broadcast_select_fusion.refs_8_), channel_id=1, source_target_pairs={{0,2},{2,0},{4,6},{6,4},{8,10},{10,8},{12,14},{14,12},{1,3},{3,1},... | collective-permute-start | bytes 786440 | tf_op jit(solution)/shard_map/cond/branch_0_fun/ppermute | solution.py:323
  71.9 5.6 %collective-permute-start.39 = (bf16[2,128,512]{2,1,0:T(8,128)(2,1)S(1)}, bf16[2,128,512]{2,1,0:T(8,128)(2,1)S(1)}, u32[]{:S(2)}, u32[]{:S(2)}) collective-permute-start(bf16[2,128,512]{2,1,0:T(8,128)(2,1)S(1)} %broadcast_select_fusion.refs_8_), channel_id=1, source_target_pairs={{0,1},{1,0},{2,3},{3,2},{4,5},{5,4},{6,7},{7,6},{8,9},{9,8},{10,11... | collective-permute-start | bytes 786440 | tf_op jit(solution)/shard_map/cond/branch_0_fun/ppermute | solution.py:323
  71.9 9.3 %collective-permute-start.38 = (bf16[2,128,512]{2,1,0:T(8,128)(2,1)S(1)}, bf16[2,128,512]{2,1,0:T(8,128)(2,1)S(1)}, u32[]{:S(2)}, u32[]{:S(2)}) collective-permute-start(bf16[2,128,512]{2,1,0:T(8,128)(2,1)S(1)} %broadcast_select_fusion.refs_8_), channel_id=1, source_target_pairs={{0,4},{2,6},{4,0},{6,2},{8,12},{10,14},{12,8},{14,10},{1,5},{3,7},... | collective-permute-start | bytes 786440 | tf_op jit(solution)/shard_map/cond/branch_0_fun/ppermute | solution.py:323
  75.7 11.1 %collective-permute-start.26 = (bf16[2,128,512]{2,1,0:T(8,128)(2,1)S(1)}, bf16[2,128,512]{2,1,0:T(8,128)(2,1)S(1)}, u32[]{:S(2)}, u32[]{:S(2)}) collective-permute-start(bf16[2,128,512]{2,1,0:T(8,128)(2,1)S(1)} %broadcast_select_fusion.1.refs_0_), channel_id=1, source_target_pairs={{0,4},{2,6},{4,0},{6,2},{8,12},{10,14},{12,8},{14,10},{1,5},{3,7},... | collective-permute-start | bytes 786440 | tf_op jit(solution)/shard_map/cond/branch_0_fun/ppermute | solution.py:323
  76.4 11.4 %collective-permute-start.29 = (bf16[2,128,512]{2,1,0:T(8,128)(2,1)S(1)}, bf16[2,128,512]{2,1,0:T(8,128)(2,1)S(1)}, u32[]{:S(2)}, u32[]{:S(2)}) collective-permute-start(bf16[2,128,512]{2,1,0:T(8,128)(2,1)S(1)} %broadcast_select_fusion.1.refs_0_), channel_id=1, source_target_pairs={{0,2},{2,0},{4,6},{6,4},{8,10},{10,8},{12,14},{14,12},{1,3},{3,1},... | collective-permute-start | bytes 786440 | tf_op jit(solution)/shard_map/cond/branch_0_fun/ppermute | solution.py:323
  77.4 10.3 %collective-permute-start.27 = (bf16[2,128,512]{2,1,0:T(8,128)(2,1)S(1)}, bf16[2,128,512]{2,1,0:T(8,128)(2,1)S(1)}, u32[]{:S(2)}, u32[]{:S(2)}) collective-permute-start(bf16[2,128,512]{2,1,0:T(8,128)(2,1)S(1)} %broadcast_select_fusion.1.refs_0_), channel_id=1, source_target_pairs={{0,1},{1,0},{2,3},{3,2},{4,5},{5,4},{6,7},{7,6},{8,9},{9,8},{10,11... | collective-permute-start | bytes 786440 | tf_op jit(solution)/shard_map/cond/branch_0_fun/ppermute | solution.py:323
  77.5 10.8 %collective-permute-start.43 = (bf16[2,128,512]{2,1,0:T(8,128)(2,1)S(1)}, bf16[2,128,512]{2,1,0:T(8,128)(2,1)S(1)}, u32[]{:S(2)}, u32[]{:S(2)}) collective-permute-start(bf16[2,128,512]{2,1,0:T(8,128)(2,1)S(1)} %collective-permute-done.41.refs_12_), channel_id=1, source_target_pairs={{0,1},{1,0},{2,3},{3,2},{4,5},{5,4},{6,7},{7,6},{8,9},{9,8},{10,11... | collective-permute-start | bytes 786440 | tf_op jit(solution)/shard_map/cond/branch_0_fun/ppermute | solution.py:323
  81.2 9.1 %collective-permute-start.42 = (bf16[2,128,512]{2,1,0:T(8,128)(2,1)S(1)}, bf16[2,128,512]{2,1,0:T(8,128)(2,1)S(1)}, u32[]{:S(2)}, u32[]{:S(2)}) collective-permute-start(bf16[2,128,512]{2,1,0:T(8,128)(2,1)S(1)} %collective-permute-done.38.refs_9_), channel_id=1, source_target_pairs={{0,2},{2,0},{4,6},{6,4},{8,10},{10,8},{12,14},{14,12},{1,3},{3,1},... | collective-permute-start | bytes 786440 | tf_op jit(solution)/shard_map/cond/branch_0_fun/ppermute | solution.py:323
  86.8 8.7 %collective-permute-start.30 = (bf16[2,128,512]{2,1,0:T(8,128)(2,1)S(1)}, bf16[2,128,512]{2,1,0:T(8,128)(2,1)S(1)}, u32[]{:S(2)}, u32[]{:S(2)}) collective-permute-start(bf16[2,128,512]{2,1,0:T(8,128)(2,1)S(1)} %collective-permute-done.26.refs_1_), channel_id=1, source_target_pairs={{0,2},{2,0},{4,6},{6,4},{8,10},{10,8},{12,14},{14,12},{1,3},{3,1},... | collective-permute-start | bytes 786440 | tf_op jit(solution)/shard_map/cond/branch_0_fun/ppermute | solution.py:323
  87.7 7.8 %collective-permute-start.40 = (bf16[2,128,512]{2,1,0:T(8,128)(2,1)S(1)}, bf16[2,128,512]{2,1,0:T(8,128)(2,1)S(1)}, u32[]{:S(2)}, u32[]{:S(2)}) collective-permute-start(bf16[2,128,512]{2,1,0:T(8,128)(2,1)S(1)} %collective-permute-done.38.refs_9_), channel_id=1, source_target_pairs={{0,1},{1,0},{2,3},{3,2},{4,5},{5,4},{6,7},{7,6},{8,9},{9,8},{10,11... | collective-permute-start | bytes 786440 | tf_op jit(solution)/shard_map/cond/branch_0_fun/ppermute | solution.py:323
  87.7 7.8 %collective-permute-start.28 = (bf16[2,128,512]{2,1,0:T(8,128)(2,1)S(1)}, bf16[2,128,512]{2,1,0:T(8,128)(2,1)S(1)}, u32[]{:S(2)}, u32[]{:S(2)}) collective-permute-start(bf16[2,128,512]{2,1,0:T(8,128)(2,1)S(1)} %collective-permute-done.26.refs_1_), channel_id=1, source_target_pairs={{0,1},{1,0},{2,3},{3,2},{4,5},{5,4},{6,7},{7,6},{8,9},{9,8},{10,11... | collective-permute-start | bytes 786440 | tf_op jit(solution)/shard_map/cond/branch_0_fun/ppermute | solution.py:323
  88.2 7.3 %collective-permute-start.31 = (bf16[2,128,512]{2,1,0:T(8,128)(2,1)S(1)}, bf16[2,128,512]{2,1,0:T(8,128)(2,1)S(1)}, u32[]{:S(2)}, u32[]{:S(2)}) collective-permute-start(bf16[2,128,512]{2,1,0:T(8,128)(2,1)S(1)} %collective-permute-done.29.refs_4_), channel_id=1, source_target_pairs={{0,1},{1,0},{2,3},{3,2},{4,5},{5,4},{6,7},{7,6},{8,9},{9,8},{10,11... | collective-permute-start | bytes 786440 | tf_op jit(solution)/shard_map/cond/branch_0_fun/ppermute | solution.py:323
  90.3 5.2 %collective-permute-start.44 = (bf16[2,128,512]{2,1,0:T(8,128)(2,1)S(1)}, bf16[2,128,512]{2,1,0:T(8,128)(2,1)S(1)}, u32[]{:S(2)}, u32[]{:S(2)}) collective-permute-start(bf16[2,128,512]{2,1,0:T(8,128)(2,1)S(1)} %collective-permute-done.42.refs_13_), channel_id=1, source_target_pairs={{0,1},{1,0},{2,3},{3,2},{4,5},{5,4},{6,7},{7,6},{8,9},{9,8},{10,11... | collective-permute-start | bytes 786440 | tf_op jit(solution)/shard_map/cond/branch_0_fun/ppermute | solution.py:323
  (7 other events, 51.4 us)

commit v4 on v3

--- a/solution.py
+++ b/solution.py
@@ -11,16 +11,22 @@
 NN = (((1,), (0,)), ((), ()))
 NT = (((1,), (1,)), ((), ()))
 LIMIT = 48 * 1024 * 1024
-LEAF_LIMIT = 61 * 1024 * 1024
+SEND_LIMIT = 61 * 1024 * 1024
+KEEP_LIMIT = 48 * 1024 * 1024
 CHUNKS_TWO, CHUNKS_FOUR = 2, 1
+CUTS_TWO, CUTS_FOUR = 1, 1
 
 
 def dot(left, right, dims=NN):
     return lax.dot_general(left, right, dims, preferred_element_type=F32)
 
 
-def complex_dot(lr, li, rr, ri, dims=NN):
-    return dot(lr, rr, dims) - dot(li, ri, dims), dot(lr, ri, dims) + dot(li, rr, dims)
+def complex_dot(lr, li, rr, ri):
+    left = jnp.concatenate([lr, li], 1)
+    return (
+        dot(left, jnp.concatenate([rr, -ri], 0)),
+        dot(left, jnp.concatenate([ri, rr], 0)),
+    )
 
 
 def source_of(column, modes_ref, step, modes, permuted):
@@ -111,7 +117,7 @@
             keep_ref[p] = dot(leaf_ref[p], picked).astype(BF16)
 
 
-def leaf_call(kernel, parts, rows, plan, roots, modes, leaves):
+def leaf_call(kernel, limit, parts, rows, plan, roots, modes, leaves):
     width = leaves.shape[-1]
     return pl.pallas_call(
         functools.partial(kernel, plan),
@@ -123,7 +129,7 @@
             scratch_shapes=[pltpu.VMEM((2, width, width), BF16), pltpu.SemaphoreType.DMA((parts,))],
         ),
         out_shape=[jax.ShapeDtypeStruct((2, rows, width), BF16)] * parts,
-        compiler_params=pltpu.CompilerParams(vmem_limit_bytes=LEAF_LIMIT),
+        compiler_params=pltpu.CompilerParams(vmem_limit_bytes=limit),
     )(roots, modes, leaves)
 
 
@@ -148,10 +154,9 @@
     out_ref[1] = im.astype(BF16)
 
 
-def branch_kernel(chunks, *refs):
+def branch_kernel(chunks, cuts, *refs):
     own, got, own_sib, got_sib = (refs[i * chunks : (i + 1) * chunks] for i in range(4))
-    first_ref, second_ref = refs[4 * chunks : 4 * chunks + 2]
-    both_ref = refs[4 * chunks + 2] if len(refs) > 4 * chunks + 2 else None
+    firsts, other_ref = refs[4 * chunks : 4 * chunks + cuts], refs[4 * chunks + cuts]
     y, zb, _, core = place()
     rows, width = own[0].shape[1] * chunks, own[0].shape[2]
     part = rows // 2
@@ -172,21 +177,17 @@
         return re.astype(BF16), im.astype(BF16)
 
     def store(p, top, bottom):
-        @pl.when(zb == 0)
-        def _():
-            first_ref[p] = top
-            second_ref[p] = bottom
-            if both_ref is not None:
-                both_ref[0, p] = top
-                both_ref[1, p] = bottom
-
-        @pl.when(zb == 1)
-        def _():
-            first_ref[p] = bottom
-            second_ref[p] = top
-            if both_ref is not None:
-                both_ref[0, p] = bottom
-                both_ref[1, p] = top
+        for here, first, second in ((0, top, bottom), (1, bottom, top)):
+
+            @pl.when(zb == here)
+            def _():
+                for i, ref in enumerate(firsts):
+                    ref[p] = first[i * part // cuts : (i + 1) * part // cuts]
+                if len(other_ref.shape) == 4:
+                    other_ref[0, p] = first
+                    other_ref[1, p] = second
+                else:
+                    other_ref[p] = second
 
     def finish(parts):
         @pl.when(y == 1)
@@ -214,18 +215,14 @@
         finish(multiply(own, got, got_sib))
 
 
-def halves(ref, count):
-    return [ref] if count == 1 else [ref.at[h] for h in range(count)]
-
-
 def stem_kernel(plans, turn, layout, roots_ref, own_hbm, sib_hbm, *refs):
     pieces, (out_hbm, o_ref, n1_ref, own_ref, sib_ref, out_ref, sem) = refs[:-7], refs[-7:]
-    pieces = [piece for ref, n in zip(pieces, layout) for piece in halves(ref, n)]
-    items = len(pieces) // 4
+    items = 4
     y, zb, group, core = place()
     zb = zb if turn else 0
-    part, width = pieces[0].shape[1:]
+    width = own_hbm.shape[2]
     half = width // 2
+    part = half // 2
     first = [
         pltpu.make_async_copy(own_hbm, own_ref, sem.at[items]),
         pltpu.make_async_copy(sib_hbm, sib_ref, sem.at[items + 1]),
@@ -237,22 +234,27 @@
         steps = steps_of(plan, roots_ref, y, group if m < 2 else 1 - group)
         step = steps[m % 2]
         column = y if m % 2 == 0 else 1 - y
-        for q in range(4):
-            side = core if q < 2 else 1 - core
-            h = zb if q % 2 == 0 else 1 - zb
-            for s in range(2):
-                row = jnp.where(column == 1, side, s) * half + h * part
-                col = jnp.where(column == 1, s, side) * half
-                pltpu.make_async_copy(
-                    pieces[4 * m + q].at[:, :, s * half : (s + 1) * half],
-                    o_ref.at[
-                        step,
-                        :,
-                        pl.ds(pl.multiple_of(row, part), part),
-                        pl.ds(pl.multiple_of(col, half), half),
-                    ],
-                    sem.at[step],
-                ).start()
+        for ref, (item, far, halves) in zip(pieces, layout):
+            if item != m:
+                continue
+            side = 1 - core if far else core
+            for h, offset in halves:
+                source = ref if len(halves) == 1 else ref.at[h]
+                count = source.shape[1]
+                for s in range(2):
+                    row = jnp.where(column == 1, side, s) * half + offset
+                    row = row + (1 - zb if h else zb) * part
+                    col = jnp.where(column == 1, s, side) * half
+                    pltpu.make_async_copy(
+                        source.at[:, :, s * half : (s + 1) * half],
+                        o_ref.at[
+                            step,
+                            :,
+                            pl.ds(pl.multiple_of(row, count), count),
+                            pl.ds(pl.multiple_of(col, half), half),
+                        ],
+                        sem.at[step],
+                    ).start()
 
     def arrived(step):
         pltpu.make_async_copy(o_ref.at[step], o_ref.at[step], sem.at[step]).wait()
@@ -294,11 +296,14 @@
 def stem_call(plans, turn, roots, own, sib, items):
     shape = own.shape
     width = shape[2]
-    pieces = [piece for item in items for piece in item]
-    layout = tuple(piece.ndim == 4 and piece.shape[0] or 1 for piece in pieces)
+    pieces, layout = [], []
+    for m, item in enumerate(items):
+        for array, far, halves in item:
+            pieces.append(array)
+            layout.append((m, far, halves))
     anywhere = pl.BlockSpec(memory_space=pl.ANY)
     return pl.pallas_call(
-        functools.partial(stem_kernel, plans, turn, layout),
+        functools.partial(stem_kernel, plans, turn, tuple(layout)),
         grid_spec=pltpu.PrefetchScalarGridSpec(
             num_scalar_prefetch=1,
             grid=(1,),
@@ -327,11 +332,39 @@
     return swap(value, "narrow", 1)
 
 
-def tree(leaves, roots, modes, plan, chunks, joint):
+def select_kernel(plan, roots_ref, made_ref, other_ref, out_ref):
+    y, _, group, _ = place()
+    step, _ = steps_of(plan, roots_ref, y, group)
+    owned = roots_ref[step] >> 2 == group
+
+    @pl.when(owned)
+    def _():
+        out_ref[...] = made_ref[...]
+
+    @pl.when(jnp.logical_not(owned))
+    def _():
+        out_ref[...] = other_ref[...]
+
+
+def select_call(plan, roots, made, other):
+    return pl.pallas_call(
+        functools.partial(select_kernel, plan),
+        grid_spec=pltpu.PrefetchScalarGridSpec(
+            num_scalar_prefetch=1,
+            grid=(1,),
+            in_specs=[whole(made.shape)] * 2,
+            out_specs=whole(made.shape),
+        ),
+        out_shape=jax.ShapeDtypeStruct(made.shape, made.dtype),
+        compiler_params=pltpu.CompilerParams(vmem_limit_bytes=LIMIT),
+    )(roots, made, other)
+
+
+def tree(leaves, roots, modes, plan, chunks, joint, cuts):
     width = leaves.shape[-1]
     rows = width // lax.axis_size("narrow")
-    sends = leaf_call(send_kernel, chunks, rows // chunks, plan, roots, modes, leaves)
-    [keep] = leaf_call(keep_kernel, 1, width, plan, roots, modes, leaves)
+    sends = leaf_call(send_kernel, SEND_LIMIT, chunks, rows // chunks, plan, roots, modes, leaves)
+    [keep] = leaf_call(keep_kernel, KEEP_LIMIT, 1, width, plan, roots, modes, leaves)
     lefts = [swap(send, "wide", 1) for send in sends]
     pairs = [
         call(pair_kernel, [left, keep], [jax.ShapeDtypeStruct(left.shape, BF16)])[0]
@@ -340,25 +373,40 @@
     gots = [swap(pair, "wide", 2) for pair in pairs]
     sibs = [other_core(v) for v in pairs + gots]
     piece = jax.ShapeDtypeStruct((2, rows // 2, width), BF16)
-    outs = [piece, piece]
-    if joint:
-        outs.append(jax.ShapeDtypeStruct((2, *piece.shape), BF16))
-    return call(functools.partial(branch_kernel, chunks), pairs + gots + sibs, outs)
-
-
-def item_of(first, second):
-    return [first, second, other_core(first), other_core(second)]
+    cut = jax.ShapeDtypeStruct((2, rows // 2 // cuts, width), BF16)
+    other = jax.ShapeDtypeStruct((2, *piece.shape), BF16) if joint else piece
+    made = call(
+        functools.partial(branch_kernel, chunks, cuts), pairs + gots + sibs, [cut] * cuts + [other]
+    )
+    return made[:-1], made[-1]
+
+
+def item_of(firsts, seconds):
+    item = []
+    for half, group in enumerate((firsts, seconds)):
+        for i, piece in enumerate(group):
+            place_of = ((half, i * piece.shape[1]),)
+            item += [(piece, False, place_of), (other_core(piece), True, place_of)]
+    return item
+
+
+def joint_item(both):
+    place_of = ((0, 0), (1, 0))
+    return [(both, False, place_of), (other_core(both), True, place_of)]
+
+
+def all_swapped(values, bit):
+    return [swap(value, "wide", bit) for value in values]
 
 
 def each_own_two(stem, leaves, roots, modes):
     own = stem.astype(BF16)
     sib = other_core(own)
-    first, _, both = tree(leaves, roots, modes, None, CHUNKS_TWO, True)
-    far = swap(first, "wide", 4)
-    cross = swap(both, "wide", 1)
-    near = [[both, other_core(both)], [cross, other_core(cross)]]
-    far_second = swap(far, "wide", 2)
-    away = [item_of(far, far_second), item_of(swap(far, "wide", 1), swap(far_second, "wide", 1))]
+    firsts, both = tree(leaves, roots, modes, None, CHUNKS_TWO, True, CUTS_TWO)
+    far = all_swapped(firsts, 4)
+    near = [joint_item(both), joint_item(swap(both, "wide", 1))]
+    far_second = all_swapped(far, 2)
+    away = [item_of(far, far_second), item_of(all_swapped(far, 1), all_swapped(far_second, 1))]
     return stem_call(None, True, roots, own, sib, near + away)
 
 
@@ -370,23 +418,25 @@
     items, plans = [], []
     for j in range(leaves.shape[1] // 2):
         plan = (2 * j, 2 * j + 1)
-        first, second = tree(leaves, roots, modes, plan, CHUNKS_FOUR, False)
+        firsts, second = tree(
+            leaves, roots, modes, plan, CHUNKS_FOUR, False, CUTS_FOUR if two else 1
+        )
         owned = roots[2 * j + y] // 4 == group
         if two:
-            here = jnp.where(owned, first, swap(first, "wide", 4))
-            second = swap(here, "wide", 2)
-            cross = [swap(here, "wide", 1), swap(second, "wide", 1)]
+            here = [select_call(plan, roots, v, swap(v, "wide", 4)) for v in firsts]
+            seconds = all_swapped(here, 2)
+            cross = [all_swapped(here, 1), all_swapped(seconds, 1)]
         else:
             sums = [
                 lax.psum(
                     jnp.where(owned & (zb == 0) & (y == side), v, jnp.zeros_like(v)), "wide"
                 )
                 for side in range(2)
-                for v in (first, second)
+                for v in (firsts[0], second)
             ]
-            here, second = (jnp.where(y == 0, a, b) for a, b in zip(sums[:2], sums[2:]))
-            cross = [jnp.where(y == 0, b, a) for a, b in zip(sums[:2], sums[2:])]
-        items += [item_of(here, second), item_of(*cross)]
+            here, seconds = ([jnp.where(y == 0, a, b)] for a, b in zip(sums[:2], sums[2:]))
+            cross = [[jnp.where(y == 0, b, a)] for a, b in zip(sums[:2], sums[2:])]
+        items += [item_of(here, seconds), item_of(*cross)]
         plans.append(plan)
     return stem_call(tuple(plans), two, roots, own, sib, items)
 

time: 107 us -> 106 us (level)
  waiting for transfers between devices: 51.9 us -> 61.3 us
  loops' own time: 5.19 us -> 0.39 us
  Pallas kernels: 26.6 us -> 23.7 us
  local copies, waits for them, and re-layouts: 3.05 us -> 1.34 us
    ppermute x25, waiting for transfers between devices: 51.9 us -> 61.3 us  [swap(): return lax.ppermute(value, axis, [(i, i ^ bit) for i in range(n)])]
    another operation x1, loops' own time: 5.19 us -> 0.39 us  [local(): lax.cond(jnp.sum(root_devices // 4) == 2, each_own_two, any_owners, *given)]
    pallas_call x4, Pallas kernels: 12.2 us -> 9.35 us  [leaf_call(): pl.pallas_call(functools.partial(kernel, plan), grid_spec=pltpu.PrefetchS...]
    cond x12 -> x10, local copies, waits for them, and re-layouts: 2.47 us -> 0.03 us
    unnamed x0 -> x2, local copies, waits for them, and re-layouts: none -> 1.31 us
    pallas_call x1 -> x3, Pallas kernels: 8.81 us -> 8.95 us  [the longest x1 7.62 us: stem_call(): pl.pallas_call(functools.partial(stem_kernel, plans, turn, tuple(layout))...]
  transfers between devices with their start and end apart: 25 -> 25, of which waited for: 12 -> 12; matrix products, arithmetic and copies ran while one was open for 1% -> 0% of each run, Pallas kernels for 14% -> 13%
where the time goes in v4:
time: 106 us
  waiting for transfers between devices  61.3 us (58%)
  Pallas kernels  23.7 us (22%)
  starting transfers between devices  16.8 us (16%)
  other arithmetic  1.43 us (1%)
  local copies, waits for them, and re-layouts  1.34 us (1%)
    ppermute x25, waiting for transfers between devices, swap(): return lax.ppermute(value, axis, [(i, i ^ bit) for i in range(n)])  61.3 us
    ppermute x25, starting transfers between devices, swap(): return lax.ppermute(value, axis, [(i, i ^ bit) for i in range(n)])  16.8 us
    pallas_call x4, Pallas kernels, leaf_call(): pl.pallas_call(functools.partial(kernel, plan), grid_spec=pltpu.PrefetchS...  9.35 us
    pallas_call x1, Pallas kernels, stem_call(): pl.pallas_call(functools.partial(stem_kernel, plans, turn, tuple(layout))...  7.62 us
    pallas_call x4, Pallas kernels, call(): pl.pallas_call(kernel, grid=(1,), in_specs=[whole(a.shape) for a in array...  5.4 us
  transfers between devices with their start and end apart: 25, of which 12 were waited for; matrix products, arithmetic and copies ran while one was open for 0% of the time, Pallas kernels for 13%

profile of v4, /device:TPU:0, one launch (start us, length us, event | category | flops | bytes accessed | tf_op | source)
XLA Modules:
  0.0 105.6 jit_solution(7065138423936102711)
XLA Ops:
  0.0 1.3 %fusion = s32[]{:T(128)} fusion(s32[4]{0:T(128)} %param.8), kind=kLoop, calls=%fused_computation.4 | loop fusion | flops 63 | bytes 20 | tf_op jit(solution)/shard_map/reduce_sum | solution.py:453
  2.0 102.3 %conditional.1 = (f32[2,512,512]{2,1,0:T(8,128)S(1)}) conditional(s32[]{:T(128)} %convert_element_type.9, (f32[2,512,512]{2,1,0:T(8,128)}, s32[4]{0:T(128)}, s32[4,9]{1,0:T(4,128)}, bf16[1,4,2,512,512]{4,3,2,1,0:T(8,128)(2,1)}) %tuple.11, (f32[2,512,512]{2,1,0:T(8,128)}, s32[4]{0:T(128)}, s32[4,9]{1,0:T(4,128)}, ...), branch_computations={%region_1.2_spmd, %region_2.3_spmd} | conditional | flops 524288 | bytes 70256384 | solution.py:453
  2.0 2.7 %branch_0_fun.16 = bf16[2,256,512]{2,1,0:T(8,128)(2,1)} custom-call(s32[4]{0:T(128)} %get-tuple-element.24.roots_ref, s32[4,9]{1,0:T(4,128)} %get-tuple-element.26.modes_ref, bf16[1,4,2,512,512]{4,3,2,1,0:T(8,128)(2,1)} %get-tuple-element.27.leaves_ref), custom_call_target="tpu_custom_call" | custom-call | tf_op jit(solution)/shard_map/cond/branch_0_fun/pallas_call | solution.py:122
  4.7 3.7 %collective-permute-start.13 = (bf16[2,256,512]{2,1,0:T(8,128)(2,1)}, bf16[2,256,512]{2,1,0:T(8,128)(2,1)S(1)}, u32[]{:S(2)}, u32[]{:S(2)}) collective-permute-start(bf16[2,256,512]{2,1,0:T(8,128)(2,1)} %branch_0_fun.16), channel_id=1, source_target_pairs={{0,2},{2,0},{4,6},{6,4},{8,10},{10,8},{12,14},{14,12},{1,3},{3,1},... | collective-permute-start | bytes 1572872 | tf_op jit(solution)/shard_map/cond/branch_0_fun/ppermute | solution.py:328
  8.4 2.4 %branch_0_fun.11 = bf16[2,256,512]{2,1,0:T(8,128)(2,1)} custom-call(s32[4]{0:T(128)S(1)} %copy-done.8, s32[4,9]{1,0:T(4,128)S(1)} %copy-done.6, bf16[1,4,2,512,512]{4,3,2,1,0:T(8,128)(2,1)} %get-tuple-element.27.leaves_ref), custom_call_target="tpu_custom_call" | custom-call | tf_op jit(solution)/shard_map/cond/branch_0_fun/pallas_call | solution.py:122
  11.6 2.8 %branch_0_fun.17.right_ref = bf16[2,512,512]{2,1,0:T(8,128)(2,1)S(1)} custom-call(s32[4]{0:T(128)S(1)} %copy-done.8, s32[4,9]{1,0:T(4,128)S(1)} %copy-done.6, bf16[1,4,2,512,512]{4,3,2,1,0:T(8,128)(2,1)} %get-tuple-element.27.leaves_ref), custom_call_target="tpu_custom_call" | custom-call | tf_op jit(solution)/shard_map/cond/branch_0_fun/pallas_call | solution.py:122
  14.4 6.9 %collective-permute-done.13.left_ref = bf16[2,256,512]{2,1,0:T(8,128)(2,1)S(1)} collective-permute-done((bf16[2,256,512]{2,1,0:T(8,128)(2,1)}, bf16[2,256,512]{2,1,0:T(8,128)(2,1)S(1)}, u32[]{:S(2)}, u32[]{:S(2)}) %collective-permute-start.13) | collective-permute-done | bytes 524320 | tf_op jit(solution)/shard_map/cond/branch_0_fun/ppermute | solution.py:328
  22.1 1.6 %collective-permute-start.14 = (bf16[2,256,512]{2,1,0:T(8,128)(2,1)S(1)}, bf16[2,256,512]{2,1,0:T(8,128)(2,1)S(1)}, u32[]{:S(2)}, u32[]{:S(2)}) collective-permute-start(bf16[2,256,512]{2,1,0:T(8,128)(2,1)S(1)} %branch_0_fun.18.refs_0_), channel_id=1, source_target_pairs={{0,4},{2,6},{4,0},{6,2},{8,12},{10,14},{12,8},{14,10},{1,5},{3,7},... | collective-permute-start | bytes 1572872 | tf_op jit(solution)/shard_map/cond/branch_0_fun/ppermute | solution.py:328
  23.7 1.4 %branch_0_fun.12.right_ref = bf16[2,512,512]{2,1,0:T(8,128)(2,1)S(1)} custom-call(s32[4]{0:T(128)S(1)} %copy-done.8, s32[4,9]{1,0:T(4,128)S(1)} %copy-done.6, bf16[1,4,2,512,512]{4,3,2,1,0:T(8,128)(2,1)S(1)} %copy-done), custom_call_target="tpu_custom_call" | custom-call | tf_op jit(solution)/shard_map/cond/branch_0_fun/pallas_call | solution.py:122
  25.1 6.6 %collective-permute-done.1.left_ref = bf16[2,256,512]{2,1,0:T(8,128)(2,1)S(1)} collective-permute-done((bf16[2,256,512]{2,1,0:T(8,128)(2,1)}, bf16[2,256,512]{2,1,0:T(8,128)(2,1)S(1)}, u32[]{:S(2)}, u32[]{:S(2)}) %collective-permute-start.1) | collective-permute-done | bytes 524320 | tf_op jit(solution)/shard_map/cond/branch_0_fun/ppermute | solution.py:328
  32.5 1.6 %collective-permute-start.2 = (bf16[2,256,512]{2,1,0:T(8,128)(2,1)S(1)}, bf16[2,256,512]{2,1,0:T(8,128)(2,1)S(1)}, u32[]{:S(2)}, u32[]{:S(2)}) collective-permute-start(bf16[2,256,512]{2,1,0:T(8,128)(2,1)S(1)} %branch_0_fun.13.refs_0_), channel_id=1, source_target_pairs={{0,4},{2,6},{4,0},{6,2},{8,12},{10,14},{12,8},{14,10},{1,5},{3,7},... | collective-permute-start | bytes 1572872 | tf_op jit(solution)/shard_map/cond/branch_0_fun/ppermute | solution.py:328
  35.3 10.3 %collective-permute-done.2.refs_1_ = bf16[2,256,512]{2,1,0:T(8,128)(2,1)S(1)} collective-permute-done((bf16[2,256,512]{2,1,0:T(8,128)(2,1)S(1)}, bf16[2,256,512]{2,1,0:T(8,128)(2,1)S(1)}, u32[]{:S(2)}, u32[]{:S(2)}) %collective-permute-start.2) | collective-permute-done | bytes 524320 | tf_op jit(solution)/shard_map/cond/branch_0_fun/ppermute | solution.py:328
  45.6 2.0 %branch_0_fun.19 = (bf16[2,128,512]{2,1,0:T(8,128)(2,1)S(1)}, bf16[2,128,512]{2,1,0:T(8,128)(2,1)}) custom-call(bf16[2,256,512]{2,1,0:T(8,128)(2,1)S(1)} %branch_0_fun.18.refs_0_, bf16[2,256,512]{2,1,0:T(8,128)(2,1)S(1)} %collective-permute-done.14.refs_1_, bf16[2,256,512]{2,1,0:T(8,128)(2,1)S(1)} %collective-permute-done.15.refs_2_, ...), custom_call_target="tpu_custom_call" | custom-call | tf_op jit(solution)/shard_map/cond/branch_0_fun/pallas_call | solution.py:141
  47.6 2.6 %collective-permute-start.17 = (bf16[2,128,512]{2,1,0:T(8,128)(2,1)S(1)}, bf16[2,128,512]{2,1,0:T(8,128)(2,1)S(1)}, u32[]{:S(2)}, u32[]{:S(2)}) collective-permute-start(bf16[2,128,512]{2,1,0:T(8,128)(2,1)S(1)} %get-tuple-element.29.made_ref), channel_id=1, source_target_pairs={{0,8},{2,10},{4,12},{6,14},{8,0},{10,2},{12,4},{14,6},{1,9},{3,11}... | collective-permute-start | bytes 786440 | tf_op jit(solution)/shard_map/cond/branch_0_fun/ppermute | solution.py:328
  50.2 2.0 %branch_0_fun.14 = (bf16[2,128,512]{2,1,0:T(8,128)(2,1)S(1)}, bf16[2,128,512]{2,1,0:T(8,128)(2,1)}) custom-call(bf16[2,256,512]{2,1,0:T(8,128)(2,1)S(1)} %branch_0_fun.13.refs_0_, bf16[2,256,512]{2,1,0:T(8,128)(2,1)S(1)} %collective-permute-done.2.refs_1_, bf16[2,256,512]{2,1,0:T(8,128)(2,1)S(1)} %collective-permute-done.3.refs_2_, ...), custom_call_target="tpu_custom_call" | custom-call | tf_op jit(solution)/shard_map/cond/branch_0_fun/pallas_call | solution.py:141
  52.6 16.3 %collective-permute-done.17.other_ref = bf16[2,128,512]{2,1,0:T(8,128)(2,1)S(1)} collective-permute-done((bf16[2,128,512]{2,1,0:T(8,128)(2,1)S(1)}, bf16[2,128,512]{2,1,0:T(8,128)(2,1)S(1)}, u32[]{:S(2)}, u32[]{:S(2)}) %collective-permute-start.17) | collective-permute-done | bytes 262176 | tf_op jit(solution)/shard_map/cond/branch_0_fun/ppermute | solution.py:328
  70.8 3.4 %collective-permute-done.5.other_ref = bf16[2,128,512]{2,1,0:T(8,128)(2,1)S(1)} collective-permute-done((bf16[2,128,512]{2,1,0:T(8,128)(2,1)S(1)}, bf16[2,128,512]{2,1,0:T(8,128)(2,1)S(1)}, u32[]{:S(2)}, u32[]{:S(2)}) %collective-permute-start.5) | collective-permute-done | bytes 262176 | tf_op jit(solution)/shard_map/cond/branch_0_fun/ppermute | solution.py:328
  77.0 2.8 %collective-permute-done.19.refs_10_ = bf16[2,128,512]{2,1,0:T(8,128)(2,1)S(1)} collective-permute-done((bf16[2,128,512]{2,1,0:T(8,128)(2,1)S(1)}, bf16[2,128,512]{2,1,0:T(8,128)(2,1)S(1)}, u32[]{:S(2)}, u32[]{:S(2)}) %collective-permute-start.19) | collective-permute-done | bytes 262176 | tf_op jit(solution)/shard_map/cond/branch_0_fun/ppermute | solution.py:328
  80.7 4.6 %collective-permute-done.7.refs_2_ = bf16[2,128,512]{2,1,0:T(8,128)(2,1)S(1)} collective-permute-done((bf16[2,128,512]{2,1,0:T(8,128)(2,1)S(1)}, bf16[2,128,512]{2,1,0:T(8,128)(2,1)S(1)}, u32[]{:S(2)}, u32[]{:S(2)}) %collective-permute-start.7) | collective-permute-done | bytes 262176 | tf_op jit(solution)/shard_map/cond/branch_0_fun/ppermute | solution.py:328
  86.8 3.0 %collective-permute-done.23.refs_14_ = bf16[2,128,512]{2,1,0:T(8,128)(2,1)S(1)} collective-permute-done((bf16[2,128,512]{2,1,0:T(8,128)(2,1)S(1)}, bf16[2,128,512]{2,1,0:T(8,128)(2,1)S(1)}, u32[]{:S(2)}, u32[]{:S(2)}) %collective-permute-start.23) | collective-permute-done | bytes 262176 | tf_op jit(solution)/shard_map/cond/branch_0_fun/ppermute | solution.py:328
  89.9 5.0 %collective-permute-done.11.refs_6_ = bf16[2,128,512]{2,1,0:T(8,128)(2,1)S(1)} collective-permute-done((bf16[2,128,512]{2,1,0:T(8,128)(2,1)S(1)}, bf16[2,128,512]{2,1,0:T(8,128)(2,1)S(1)}, u32[]{:S(2)}, u32[]{:S(2)}) %collective-permute-start.11) | collective-permute-done | bytes 262176 | tf_op jit(solution)/shard_map/cond/branch_0_fun/ppermute | solution.py:328
  94.9 1.5 %collective-permute-done.12.refs_7_ = bf16[2,128,512]{2,1,0:T(8,128)(2,1)S(1)} collective-permute-done((bf16[2,128,512]{2,1,0:T(8,128)(2,1)S(1)}, bf16[2,128,512]{2,1,0:T(8,128)(2,1)S(1)}, u32[]{:S(2)}, u32[]{:S(2)}) %collective-permute-start.12) | collective-permute-done | bytes 262176 | tf_op jit(solution)/shard_map/cond/branch_0_fun/ppermute | solution.py:328
  96.4 7.6 %branch_0_fun.21 = f32[2,512,512]{2,1,0:T(8,128)S(1)} custom-call(s32[4]{0:T(128)S(1)} %copy-done.8, bf16[2,512,512]{2,1,0:T(8,128)(2,1)S(1)} %convert_element_type.6.own_hbm, bf16[2,512,512]{2,1,0:T(8,128)(2,1)} %copy-done.4, bf16[2,128,512]{2,1,0:T(8,128)(2,1)S(1)} %branch_0_fun.15.refs_0_, bf16[2,128,512]{2,1,0:T(8,128)(2,1)S(1)} %collective-permute-done.6.refs_1_, ...), custom_call_target="tpu_custom_call" | custom-call | tf_op jit(solution)/shard_map/cond/branch_0_fun/pallas_call | solution.py:305
  104.3 1.3 %copy-done.3 = f32[2,512,512]{2,1,0:T(8,128)} copy-done((f32[2,512,512]{2,1,0:T(8,128)}, f32[2,512,512]{2,1,0:T(8,128)S(1)}, u32[]{:S(2)}) %copy-start.3) | copy-done | bytes 2097176
  (52 shorter events, 10.9 us)
Async XLA Ops:
  4.7 16.7 %collective-permute-start.13 = (bf16[2,256,512]{2,1,0:T(8,128)(2,1)}, bf16[2,256,512]{2,1,0:T(8,128)(2,1)S(1)}, u32[]{:S(2)}, u32[]{:S(2)}) collective-permute-start(bf16[2,256,512]{2,1,0:T(8,128)(2,1)} %branch_0_fun.16), channel_id=1, source_target_pairs={{0,2},{2,0},{4,6},{6,4},{8,10},{10,8},{12,14},{14,12},{1,3},{3,1},... | collective-permute-start | bytes 1572872 | tf_op jit(solution)/shard_map/cond/branch_0_fun/ppermute | solution.py:328
  10.8 20.9 %collective-permute-start.1 = (bf16[2,256,512]{2,1,0:T(8,128)(2,1)}, bf16[2,256,512]{2,1,0:T(8,128)(2,1)S(1)}, u32[]{:S(2)}, u32[]{:S(2)}) collective-permute-start(bf16[2,256,512]{2,1,0:T(8,128)(2,1)} %branch_0_fun.11), channel_id=1, source_target_pairs={{0,2},{2,0},{4,6},{6,4},{8,10},{10,8},{12,14},{14,12},{1,3},{3,1},... | collective-permute-start | bytes 1572872 | tf_op jit(solution)/shard_map/cond/branch_0_fun/ppermute | solution.py:328
  22.1 12.3 %collective-permute-start.14 = (bf16[2,256,512]{2,1,0:T(8,128)(2,1)S(1)}, bf16[2,256,512]{2,1,0:T(8,128)(2,1)S(1)}, u32[]{:S(2)}, u32[]{:S(2)}) collective-permute-start(bf16[2,256,512]{2,1,0:T(8,128)(2,1)S(1)} %branch_0_fun.18.refs_0_), channel_id=1, source_target_pairs={{0,4},{2,6},{4,0},{6,2},{8,12},{10,14},{12,8},{14,10},{1,5},{3,7},... | collective-permute-start | bytes 1572872 | tf_op jit(solution)/shard_map/cond/branch_0_fun/ppermute | solution.py:328
  32.5 13.2 %collective-permute-start.2 = (bf16[2,256,512]{2,1,0:T(8,128)(2,1)S(1)}, bf16[2,256,512]{2,1,0:T(8,128)(2,1)S(1)}, u32[]{:S(2)}, u32[]{:S(2)}) collective-permute-start(bf16[2,256,512]{2,1,0:T(8,128)(2,1)S(1)} %branch_0_fun.13.refs_0_), channel_id=1, source_target_pairs={{0,4},{2,6},{4,0},{6,2},{8,12},{10,14},{12,8},{14,10},{1,5},{3,7},... | collective-permute-start | bytes 1572872 | tf_op jit(solution)/shard_map/cond/branch_0_fun/ppermute | solution.py:328
  34.1 11.5 %collective-permute-start.15 = (bf16[2,256,512]{2,1,0:T(8,128)(2,1)S(1)}, bf16[2,256,512]{2,1,0:T(8,128)(2,1)S(1)}, u32[]{:S(2)}, u32[]{:S(2)}) collective-permute-start(bf16[2,256,512]{2,1,0:T(8,128)(2,1)S(1)} %branch_0_fun.18.refs_0_), channel_id=1, source_target_pairs={{0,1},{1,0},{2,3},{3,2},{4,5},{5,4},{6,7},{7,6},{8,9},{9,8},{10,11... | collective-permute-start | bytes 1572872 | tf_op jit(solution)/shard_map/cond/branch_0_fun/ppermute | solution.py:328
  34.4 11.2 %collective-permute-start.16 = (bf16[2,256,512]{2,1,0:T(8,128)(2,1)S(1)}, bf16[2,256,512]{2,1,0:T(8,128)(2,1)S(1)}, u32[]{:S(2)}, u32[]{:S(2)}) collective-permute-start(bf16[2,256,512]{2,1,0:T(8,128)(2,1)S(1)} %collective-permute-done.14.refs_1_), channel_id=1, source_target_pairs={{0,1},{1,0},{2,3},{3,2},{4,5},{5,4},{6,7},{7,6},{8,9},{9,8},{10,11... | collective-permute-start | bytes 1572872 | tf_op jit(solution)/shard_map/cond/branch_0_fun/ppermute | solution.py:328
  34.8 40.9 %collective-permute-start = (bf16[2,512,512]{2,1,0:T(8,128)(2,1)S(1)}, bf16[2,512,512]{2,1,0:T(8,128)(2,1)S(1)}, u32[]{:S(2)}, u32[]{:S(2)}) collective-permute-start(bf16[2,512,512]{2,1,0:T(8,128)(2,1)S(1)} %convert_element_type.6.own_hbm), channel_id=1, source_target_pairs={{0,1},{1,0},{2,3},{3,2},{4,5},{5,4},{6,7},{7,6},{8,9},{9,8},{10,11... | collective-permute-start | bytes 3145736 | tf_op jit(solution)/shard_map/cond/branch_0_fun/ppermute | solution.py:328
  35.1 15.1 %collective-permute-start.3 = (bf16[2,256,512]{2,1,0:T(8,128)(2,1)S(1)}, bf16[2,256,512]{2,1,0:T(8,128)(2,1)S(1)}, u32[]{:S(2)}, u32[]{:S(2)}) collective-permute-start(bf16[2,256,512]{2,1,0:T(8,128)(2,1)S(1)} %branch_0_fun.13.refs_0_), channel_id=1, source_target_pairs={{0,1},{1,0},{2,3},{3,2},{4,5},{5,4},{6,7},{7,6},{8,9},{9,8},{10,11... | collective-permute-start | bytes 1572872 | tf_op jit(solution)/shard_map/cond/branch_0_fun/ppermute | solution.py:328
  45.6 4.6 %collective-permute-start.4 = (bf16[2,256,512]{2,1,0:T(8,128)(2,1)S(1)}, bf16[2,256,512]{2,1,0:T(8,128)(2,1)S(1)}, u32[]{:S(2)}, u32[]{:S(2)}) collective-permute-start(bf16[2,256,512]{2,1,0:T(8,128)(2,1)S(1)} %collective-permute-done.2.refs_1_), channel_id=1, source_target_pairs={{0,1},{1,0},{2,3},{3,2},{4,5},{5,4},{6,7},{7,6},{8,9},{9,8},{10,11... | collective-permute-start | bytes 1572872 | tf_op jit(solution)/shard_map/cond/branch_0_fun/ppermute | solution.py:328
  47.6 21.2 %collective-permute-start.17 = (bf16[2,128,512]{2,1,0:T(8,128)(2,1)S(1)}, bf16[2,128,512]{2,1,0:T(8,128)(2,1)S(1)}, u32[]{:S(2)}, u32[]{:S(2)}) collective-permute-start(bf16[2,128,512]{2,1,0:T(8,128)(2,1)S(1)} %get-tuple-element.29.made_ref), channel_id=1, source_target_pairs={{0,8},{2,10},{4,12},{6,14},{8,0},{10,2},{12,4},{14,6},{1,9},{3,11}... | collective-permute-start | bytes 786440 | tf_op jit(solution)/shard_map/cond/branch_0_fun/ppermute | solution.py:328
  52.2 22.0 %collective-permute-start.5 = (bf16[2,128,512]{2,1,0:T(8,128)(2,1)S(1)}, bf16[2,128,512]{2,1,0:T(8,128)(2,1)S(1)}, u32[]{:S(2)}, u32[]{:S(2)}) collective-permute-start(bf16[2,128,512]{2,1,0:T(8,128)(2,1)S(1)} %get-tuple-element.28.made_ref), channel_id=1, source_target_pairs={{0,8},{2,10},{4,12},{6,14},{8,0},{10,2},{12,4},{14,6},{1,9},{3,11}... | collective-permute-start | bytes 786440 | tf_op jit(solution)/shard_map/cond/branch_0_fun/ppermute | solution.py:328
  69.5 7.6 %collective-permute-start.21 = (bf16[2,128,512]{2,1,0:T(8,128)(2,1)S(1)}, bf16[2,128,512]{2,1,0:T(8,128)(2,1)S(1)}, u32[]{:S(2)}, u32[]{:S(2)}) collective-permute-start(bf16[2,128,512]{2,1,0:T(8,128)(2,1)S(1)} %branch_0_fun.20.refs_8_), channel_id=1, source_target_pairs={{0,2},{2,0},{4,6},{6,4},{8,10},{10,8},{12,14},{14,12},{1,3},{3,1},... | collective-permute-start | bytes 786440 | tf_op jit(solution)/shard_map/cond/branch_0_fun/ppermute | solution.py:328
  70.4 9.4 %collective-permute-start.19 = (bf16[2,128,512]{2,1,0:T(8,128)(2,1)S(1)}, bf16[2,128,512]{2,1,0:T(8,128)(2,1)S(1)}, u32[]{:S(2)}, u32[]{:S(2)}) collective-permute-start(bf16[2,128,512]{2,1,0:T(8,128)(2,1)S(1)} %branch_0_fun.20.refs_8_), channel_id=1, source_target_pairs={{0,4},{2,6},{4,0},{6,2},{8,12},{10,14},{12,8},{14,10},{1,5},{3,7},... | collective-permute-start | bytes 786440 | tf_op jit(solution)/shard_map/cond/branch_0_fun/ppermute | solution.py:328
  70.8 9.1 %collective-permute-start.18 = (bf16[2,128,512]{2,1,0:T(8,128)(2,1)S(1)}, bf16[2,128,512]{2,1,0:T(8,128)(2,1)S(1)}, u32[]{:S(2)}, u32[]{:S(2)}) collective-permute-start(bf16[2,128,512]{2,1,0:T(8,128)(2,1)S(1)} %branch_0_fun.20.refs_8_), channel_id=1, source_target_pairs={{0,1},{1,0},{2,3},{3,2},{4,5},{5,4},{6,7},{7,6},{8,9},{9,8},{10,11... | collective-permute-start | bytes 786440 | tf_op jit(solution)/shard_map/cond/branch_0_fun/ppermute | solution.py:328
  75.0 10.4 %collective-permute-start.7 = (bf16[2,128,512]{2,1,0:T(8,128)(2,1)S(1)}, bf16[2,128,512]{2,1,0:T(8,128)(2,1)S(1)}, u32[]{:S(2)}, u32[]{:S(2)}) collective-permute-start(bf16[2,128,512]{2,1,0:T(8,128)(2,1)S(1)} %branch_0_fun.15.refs_0_), channel_id=1, source_target_pairs={{0,4},{2,6},{4,0},{6,2},{8,12},{10,14},{12,8},{14,10},{1,5},{3,7},... | collective-permute-start | bytes 786440 | tf_op jit(solution)/shard_map/cond/branch_0_fun/ppermute | solution.py:328
  75.7 10.6 %collective-permute-start.9 = (bf16[2,128,512]{2,1,0:T(8,128)(2,1)S(1)}, bf16[2,128,512]{2,1,0:T(8,128)(2,1)S(1)}, u32[]{:S(2)}, u32[]{:S(2)}) collective-permute-start(bf16[2,128,512]{2,1,0:T(8,128)(2,1)S(1)} %branch_0_fun.15.refs_0_), channel_id=1, source_target_pairs={{0,2},{2,0},{4,6},{6,4},{8,10},{10,8},{12,14},{14,12},{1,3},{3,1},... | collective-permute-start | bytes 786440 | tf_op jit(solution)/shard_map/cond/branch_0_fun/ppermute | solution.py:328
  77.0 9.2 %collective-permute-start.6 = (bf16[2,128,512]{2,1,0:T(8,128)(2,1)S(1)}, bf16[2,128,512]{2,1,0:T(8,128)(2,1)S(1)}, u32[]{:S(2)}, u32[]{:S(2)}) collective-permute-start(bf16[2,128,512]{2,1,0:T(8,128)(2,1)S(1)} %branch_0_fun.15.refs_0_), channel_id=1, source_target_pairs={{0,1},{1,0},{2,3},{3,2},{4,5},{5,4},{6,7},{7,6},{8,9},{9,8},{10,11... | collective-permute-start | bytes 786440 | tf_op jit(solution)/shard_map/cond/branch_0_fun/ppermute | solution.py:328
  79.8 7.0 %collective-permute-start.22 = (bf16[2,128,512]{2,1,0:T(8,128)(2,1)S(1)}, bf16[2,128,512]{2,1,0:T(8,128)(2,1)S(1)}, u32[]{:S(2)}, u32[]{:S(2)}) collective-permute-start(bf16[2,128,512]{2,1,0:T(8,128)(2,1)S(1)} %collective-permute-done.21.refs_12_), channel_id=1, source_target_pairs={{0,1},{1,0},{2,3},{3,2},{4,5},{5,4},{6,7},{7,6},{8,9},{9,8},{10,11... | collective-permute-start | bytes 786440 | tf_op jit(solution)/shard_map/cond/branch_0_fun/ppermute | solution.py:328
  79.8 10.1 %collective-permute-start.23 = (bf16[2,128,512]{2,1,0:T(8,128)(2,1)S(1)}, bf16[2,128,512]{2,1,0:T(8,128)(2,1)S(1)}, u32[]{:S(2)}, u32[]{:S(2)}) collective-permute-start(bf16[2,128,512]{2,1,0:T(8,128)(2,1)S(1)} %collective-permute-done.19.refs_10_), channel_id=1, source_target_pairs={{0,2},{2,0},{4,6},{6,4},{8,10},{10,8},{12,14},{14,12},{1,3},{3,1},... | collective-permute-start | bytes 786440 | tf_op jit(solution)/shard_map/cond/branch_0_fun/ppermute | solution.py:328
  85.3 9.5 %collective-permute-start.11 = (bf16[2,128,512]{2,1,0:T(8,128)(2,1)S(1)}, bf16[2,128,512]{2,1,0:T(8,128)(2,1)S(1)}, u32[]{:S(2)}, u32[]{:S(2)}) collective-permute-start(bf16[2,128,512]{2,1,0:T(8,128)(2,1)S(1)} %collective-permute-done.7.refs_2_), channel_id=1, source_target_pairs={{0,2},{2,0},{4,6},{6,4},{8,10},{10,8},{12,14},{14,12},{1,3},{3,1},... | collective-permute-start | bytes 786440 | tf_op jit(solution)/shard_map/cond/branch_0_fun/ppermute | solution.py:328
  86.2 8.6 %collective-permute-start.20 = (bf16[2,128,512]{2,1,0:T(8,128)(2,1)S(1)}, bf16[2,128,512]{2,1,0:T(8,128)(2,1)S(1)}, u32[]{:S(2)}, u32[]{:S(2)}) collective-permute-start(bf16[2,128,512]{2,1,0:T(8,128)(2,1)S(1)} %collective-permute-done.19.refs_10_), channel_id=1, source_target_pairs={{0,1},{1,0},{2,3},{3,2},{4,5},{5,4},{6,7},{7,6},{8,9},{9,8},{10,11... | collective-permute-start | bytes 786440 | tf_op jit(solution)/shard_map/cond/branch_0_fun/ppermute | solution.py:328
  86.3 8.6 %collective-permute-start.8 = (bf16[2,128,512]{2,1,0:T(8,128)(2,1)S(1)}, bf16[2,128,512]{2,1,0:T(8,128)(2,1)S(1)}, u32[]{:S(2)}, u32[]{:S(2)}) collective-permute-start(bf16[2,128,512]{2,1,0:T(8,128)(2,1)S(1)} %collective-permute-done.7.refs_2_), channel_id=1, source_target_pairs={{0,1},{1,0},{2,3},{3,2},{4,5},{5,4},{6,7},{7,6},{8,9},{9,8},{10,11... | collective-permute-start | bytes 786440 | tf_op jit(solution)/shard_map/cond/branch_0_fun/ppermute | solution.py:328
  86.8 8.1 %collective-permute-start.10 = (bf16[2,128,512]{2,1,0:T(8,128)(2,1)S(1)}, bf16[2,128,512]{2,1,0:T(8,128)(2,1)S(1)}, u32[]{:S(2)}, u32[]{:S(2)}) collective-permute-start(bf16[2,128,512]{2,1,0:T(8,128)(2,1)S(1)} %collective-permute-done.9.refs_4_), channel_id=1, source_target_pairs={{0,1},{1,0},{2,3},{3,2},{4,5},{5,4},{6,7},{7,6},{8,9},{9,8},{10,11... | collective-permute-start | bytes 786440 | tf_op jit(solution)/shard_map/cond/branch_0_fun/ppermute | solution.py:328
  89.9 5.0 %collective-permute-start.24 = (bf16[2,128,512]{2,1,0:T(8,128)(2,1)S(1)}, bf16[2,128,512]{2,1,0:T(8,128)(2,1)S(1)}, u32[]{:S(2)}, u32[]{:S(2)}) collective-permute-start(bf16[2,128,512]{2,1,0:T(8,128)(2,1)S(1)} %collective-permute-done.23.refs_14_), channel_id=1, source_target_pairs={{0,1},{1,0},{2,3},{3,2},{4,5},{5,4},{6,7},{7,6},{8,9},{9,8},{10,11... | collective-permute-start | bytes 786440 | tf_op jit(solution)/shard_map/cond/branch_0_fun/ppermute | solution.py:328
  (7 other events, 58.1 us)
